TPU v7x, 32 devices: a whole 2x2x4 slice. The times are simulated.
32 devices in a mesh: row: 8 (over y, x, core), col: 4 (over z).
Axes of the slice: x: 2, y: 2, z: 4, core: 2. Of those that a mesh axis runs over, the one named last changes fastest.
Arguments:
- grad_out: bfloat16 [1024, 16384], P('col', 'row'), may hold values from -6 to 6
- gate_act: bfloat16 [1024, 26624], P('row', 'col'), may hold values from -8 to 8
- up_act: bfloat16 [1024, 26624], P('row', 'col'), may hold values from -6 to 6
- down_weight: bfloat16 [26624, 16384], P('col', 'row'), may hold values from -0.046875 to 0.046875
Outputs:
- grad_gate: bfloat16 [1024, 26624], P('row', 'col')
- grad_up: bfloat16 [1024, 26624], P('row', 'col')
- grad_down: bfloat16 [26624, 16384], P('col', 'row')
All inputs are finite; a program needn't handle non-finite values.
Results may differ from a plain program's by a relative error of at most 0.0049.
Values may be sent and summed in bfloat16 or wider, within the bound.
No kernel may reach another device: no remote copies, remote signals or barrier semaphores. Data moves between devices by JAX's collectives and lax.ppermute only.
A program may use at most 448 MiB of HBM per device.

v0:
```python
import jax
import jax.numpy as jnp
from jax import lax
from jax.sharding import PartitionSpec as P


def swiglu_grads(grad_hidden, gate_act, up_act):
    gate_val = gate_act.astype(jnp.float32)
    up_val = up_act.astype(jnp.float32)
    sigmoid_g = jax.nn.sigmoid(gate_val)
    act_val = gate_val * sigmoid_g
    hidden = (act_val * up_val).astype(jnp.bfloat16)
    grad_gate = (grad_hidden * up_val * sigmoid_g * (1.0 + gate_val * (1.0 - sigmoid_g))).astype(
        jnp.bfloat16
    )
    grad_up = (grad_hidden * act_val).astype(jnp.bfloat16)
    return (hidden, grad_gate, grad_up)


def local(grad_out, gate_act, up_act, down_weight):
    dy_cols = lax.all_gather(grad_out, "col", axis=0, tiled=True)
    dy_rows = dy_cols
    grad_hidden = lax.psum_scatter(
        lax.dot_general(
            dy_rows, down_weight, (((1,), (1,)), ((), ())), preferred_element_type=jnp.float32
        ),
        "row",
        scatter_dimension=0,
        tiled=True,
    )
    hidden, grad_gate, grad_up = swiglu_grads(grad_hidden, gate_act, up_act)
    dy_rows = dy_cols
    grad_down = lax.dot_general(
        lax.all_gather(hidden, "row", axis=0, tiled=True),
        dy_rows,
        (((0,), (0,)), ((), ())),
        preferred_element_type=jnp.float32,
    ).astype(jnp.bfloat16)
    return (grad_gate, grad_up, grad_down)


def solution(mesh):
    return jax.shard_map(
        local,
        mesh=mesh,
        in_specs=(P("col", "row"), P("row", "col"), P("row", "col"), P("col", "row")),
        out_specs=(P("row", "col"), P("row", "col"), P("col", "row")),
        check_vma=False,
    )
```

profile of v0, /device:TPU:16, one launch (start us, length us, event | category | flops | bytes accessed | tf_op | source)
XLA Modules:
  0.0 419.5 jit_solution(5554438436687720951)
XLA Ops:
  7.2 0.0 all-gather.3.cloned.1.call-start
  7.2 0.7 all-gather.3.cloned.1.call-update
  7.9 0.0 reduce-scatter.2.cloned.1.call-start
  7.9 82.0 %all-gather.3.cloned.1.call-done = bf16[1024,2048]{1,0:T(8,128)(2,1)} async-done(((bf16[256,2048]{1,0:T(8,128)(2,1)}), bf16[1024,2048]{1,0:T(8,128)(2,1)}) %all-gather.3.cloned.1.call-update) | async-done | bytes 4194320 | tf_op jit(solution)/shard_map/all_gather | solution.py:21
  90.0 38.1 %fusion.8 = f32[1024,6656]{1,0:T(8,128)} fusion(bf16[1024,2048]{1,0:T(8,128)(2,1)} %all-gather.3.cloned.1.call-done, bf16[6656,2048]{1,0:T(8,128)(2,1)} %param.7), kind=kOutput, calls=%fused_computation.15 | convolution fusion | flops 27917287424 | bytes 58720256 | tf_op jit(solution)/shard_map/dot_general | solution.py:24
  128.1 0.0 copy-start
  128.1 0.0 copy-start.1
  128.1 0.0 reduce-scatter.2.cloned.1.call-update
  128.1 0.2 all-gather.5.cloned.1.call-start
  128.3 167.8 %reduce-scatter.2.cloned.1.call-done = f32[128,6656]{1,0:T(8,128)} async-done(((f32[1024,6656]{1,0:T(8,128)}), f32[128,6656]{1,0:T(8,128)}) %reduce-scatter.2.cloned.1.call-update) | async-done | bytes 3407888 | tf_op jit(solution)/shard_map/reduce_scatter | solution.py:23
  296.1 0.0 copy-done
  296.1 0.0 copy-done.1
  296.1 4.8 %multiply_convert_fusion = (bf16[128,6656]{1,0:T(8,128)(2,1)}, bf16[128,6656]{1,0:T(8,128)(2,1)}, bf16[128,6656]{1,0:T(8,128)(2,1)}) fusion(f32[128,6656]{1,0:T(8,128)} %reduce-scatter.2.cloned.1.call-done, bf16[128,6656]{1,0:T(8,128)(2,1)S(1)} %copy-done, bf16[128,6656]{1,0:T(8,128)(2,1)S(1)} %copy-done.1), kind=kLoop, calls=%fused_computation.14 | loop fusion | flops 14483456 | bytes 11927552 | tf_op jit(solution)/shard_map/convert_element_type | solution.py:16
  300.9 0.0 all-gather.5.cloned.1.call-update
  300.9 76.7 %all-gather.5.cloned.1.call-done = bf16[1024,6656]{1,0:T(8,128)(2,1)} async-done(((bf16[128,6656]{1,0:T(8,128)(2,1)}), bf16[1024,6656]{1,0:T(8,128)(2,1)}) %all-gather.5.cloned.1.call-update) | async-done | bytes 13631504 | tf_op jit(solution)/shard_map/all_gather | solution.py:34
  377.6 35.3 %convolution_convert_fusion = bf16[6656,2048]{1,0:T(8,128)(2,1)} fusion(bf16[1024,6656]{1,0:T(8,128)(2,1)} %all-gather.5.cloned.1.call-done, bf16[1024,2048]{1,0:T(8,128)(2,1)} %all-gather.3.cloned.1.call-done), kind=kOutput, calls=%fused_computation | convolution fusion | flops 27930918912 | bytes 45088768 | tf_op jit(solution)/shard_map/dot_general | solution.py:33
Async XLA Ops:
  7.2 82.8 %all-gather.3.cloned.1.call-start = ((), (), s32[]{:S(2)}) async-start(), calls=%async_computation.1 | async-start | bytes 5242880 | tf_op jit(solution)/shard_map/all_gather | solution.py:21
  7.9 288.2 %reduce-scatter.2.cloned.1.call-start = ((), (), s32[]{:S(2)}) async-start(), calls=%async_computation.2 | async-start | bytes 30670848 | tf_op jit(solution)/shard_map/reduce_scatter | solution.py:23
  128.1 168.1 %copy-start = (bf16[128,6656]{1,0:T(8,128)(2,1)S(1)}, bf16[128,6656]{1,0:T(8,128)(2,1)}, u32[]{:S(2)}) copy-start(bf16[128,6656]{1,0:T(8,128)(2,1)} %param.5) | copy-start | bytes 5111812
  128.1 168.1 %copy-start.1 = (bf16[128,6656]{1,0:T(8,128)(2,1)S(1)}, bf16[128,6656]{1,0:T(8,128)(2,1)}, u32[]{:S(2)}) copy-start(bf16[128,6656]{1,0:T(8,128)(2,1)} %param.6) | copy-start | bytes 5111812
  128.1 249.5 %all-gather.5.cloned.1.call-start = ((), (), s32[]{:S(2)}) async-start(), calls=%async_computation.3 | async-start | bytes 15335424 | tf_op jit(solution)/shard_map/all_gather | solution.py:34
Sparse Core Ops, SparseCore 0:
  9.6 80.3 all-gather.2
  128.2 167.8 reduce-scatter.1
  301.0 76.5 all-gather.4
where the time goes:
time: 421 us; the launch traced here: 419 us
  waiting for transfers between devices  327 us (78%)
  matrix products  73.4 us (17%)
  between operations  13.7 us (3%)
  other arithmetic  4.77 us (1%)
    reduce_scatter x1, waiting for transfers between devices, local(): lax.psum_scatter(lax.dot_general(dy_rows, down_weight, (((1,), (1,)), (()...  168 us
    all_gather x1, waiting for transfers between devices, local(): dy_cols = lax.all_gather(grad_out, 'col', axis=0, tiled=True)  82 us
    all_gather x1, waiting for transfers between devices, local(): lax.all_gather(hidden, 'row', axis=0, tiled=True)  76.7 us
    dot_general x1, matrix products, local(): lax.dot_general(dy_rows, down_weight, (((1,), (1,)), ((), ())), preferred...  38.1 us
    dot_general x1, matrix products, local(): lax.dot_general(lax.all_gather(hidden, 'row', axis=0, tiled=True), dy_row...  35.3 us
  transfers between devices with their start and end apart: 3, of which 3 were waited for; matrix products, arithmetic and copies ran while one was open for 0% of the time, Pallas kernels for 0%

commit v1 on v0

v1 whole, which is shorter than its diff:
```python
import jax
import jax.numpy as jnp
from jax import lax
from jax.sharding import PartitionSpec as P

CHUNKS = 4


def local(grad_out, gate_act, up_act, down_weight):
    f32, bf16 = jnp.float32, jnp.bfloat16
    gate = gate_act.astype(f32)
    hidden = (gate * jax.nn.sigmoid(gate) * up_act.astype(f32)).astype(bf16)
    dy = lax.all_gather(grad_out, "col", axis=0, tiled=True)
    hidden = lax.all_gather(hidden, "row", axis=0, tiled=True)
    dy, hidden = lax.optimization_barrier((dy, hidden))
    width = down_weight.shape[0] // CHUNKS
    gate_parts, up_parts = [], []
    for k in range(CHUNKS):
        cut = slice(k * width, (k + 1) * width)
        part = lax.dot_general(
            dy, down_weight[cut], (((1,), (1,)), ((), ())), preferred_element_type=f32
        ).astype(bf16)
        grad_hidden = lax.psum_scatter(part, "row", scatter_dimension=0, tiled=True).astype(f32)
        g, u = gate_act[:, cut].astype(f32), up_act[:, cut].astype(f32)
        sig = jax.nn.sigmoid(g)
        gate_parts.append((grad_hidden * u * sig * (1.0 + g * (1.0 - sig))).astype(bf16))
        up_parts.append((grad_hidden * (g * sig)).astype(bf16))
    grad_down = lax.dot_general(
        hidden, dy, (((0,), (0,)), ((), ())), preferred_element_type=f32
    ).astype(bf16)
    return jnp.concatenate(gate_parts, 1), jnp.concatenate(up_parts, 1), grad_down


def solution(mesh):
    return jax.shard_map(
        local,
        mesh=mesh,
        in_specs=(P("col", "row"), P("row", "col"), P("row", "col"), P("col", "row")),
        out_specs=(P("row", "col"), P("row", "col"), P("col", "row")),
        check_vma=False,
    )
```

time: 421 us -> 396 us (0.941)
  waiting for transfers between devices: 327 us -> 284 us
  matrix products: 73.4 us -> 87.1 us
  other arithmetic: 4.77 us -> 9.25 us
    reduce_scatter x1 -> x4, waiting for transfers between devices: 168 us -> 126 us  [local(): lax.psum_scatter(part, 'row', scatter_dimension=0, tiled=True).astype(f32)]
    dot_general x2 -> x5, matrix products: 73.4 us -> 87.1 us  [the longest x4 51.3 us: local(): lax.dot_general(dy, down_weight[cut], (((1,), (1,)), ((), ())), preferred...]
  transfers between devices with their start and end apart: 3 -> 6, of which waited for: 3 -> 5; matrix products, arithmetic and copies ran while one was open for 0% -> 20% of each run, Pallas kernels for 0% -> 0%
where the time goes in v1:
time: 396 us; the launch traced here: 395 us
  waiting for transfers between devices  284 us (72%)
  matrix products  87.1 us (22%)
  between operations  14.1 us (4%)
  other arithmetic  9.25 us (2%)
    reduce_scatter x4, waiting for transfers between devices, local(): lax.psum_scatter(part, 'row', scatter_dimension=0, tiled=True).astype(f32)  126 us
    all_gather x1, waiting for transfers between devices, local(): hidden = lax.all_gather(hidden, 'row', axis=0, tiled=True)  79 us
    all_gather x1, waiting for transfers between devices, local(): dy = lax.all_gather(grad_out, 'col', axis=0, tiled=True)  77.8 us
    dot_general x4, matrix products, local(): lax.dot_general(dy, down_weight[cut], (((1,), (1,)), ((), ())), preferred...  51.3 us
    dot_general x1, matrix products, local(): lax.dot_general(hidden, dy, (((0,), (0,)), ((), ())), preferred_element_t...  35.8 us
  transfers between devices with their start and end apart: 6, of which 5 were waited for; matrix products, arithmetic and copies ran while one was open for 20% of the time, Pallas kernels for 0%

profile of v1, /device:TPU:16, one launch (start us, length us, event | category | flops | bytes accessed | tf_op | source)
XLA Modules:
  0.0 394.7 jit_solution(11080802536092457093)
XLA Ops:
  7.2 0.0 all-gather.3.cloned.1.call-start
  7.2 0.7 all-gather.3.cloned.1.call-update
  7.9 0.0 all-gather.5.cloned.1.call-start
  7.9 4.2 %fusion.24 = bf16[128,6656]{1,0:T(8,128)(2,1)} fusion(bf16[128,6656]{1,0:T(8,128)(2,1)} %param.6, bf16[128,6656]{1,0:T(8,128)(2,1)} %param.5), kind=kLoop, calls=%fused_computation.19 | loop fusion | flops 6815744 | bytes 5111808 | tf_op jit(solution)/shard_map/convert_element_type | solution.py:12
  12.1 0.0 all-gather.5.cloned.1.call-update
  12.1 0.0 reduce-scatter.11.cloned.1.call-start
  12.2 77.8 %all-gather.3.cloned.1.call-done = bf16[1024,2048]{1,0:T(8,128)(2,1)} async-done(((bf16[256,2048]{1,0:T(8,128)(2,1)}), bf16[1024,2048]{1,0:T(8,128)(2,1)}) %all-gather.3.cloned.1.call-update) | async-done | bytes 4194320 | tf_op jit(solution)/shard_map/all_gather | solution.py:13
  90.0 79.0 %all-gather.5.cloned.1.call-done = bf16[1024,6656]{1,0:T(8,128)(2,1)} async-done(((bf16[128,6656]{1,0:T(8,128)(2,1)}), bf16[1024,6656]{1,0:T(8,128)(2,1)}) %all-gather.5.cloned.1.call-update) | async-done | bytes 13631504 | tf_op jit(solution)/shard_map/all_gather | solution.py:14
  169.0 12.8 %fusion.17 = bf16[1024,1664]{1,0:T(8,128)(2,1)} fusion(bf16[1024,2048]{1,0:T(8,128)(2,1)} %all-gather.3.cloned.1.call-done, bf16[6656,2048]{1,0:T(8,128)(2,1)} %param.7), kind=kOutput, calls=%fused_computation.14 | convolution fusion | flops 6981025792 | bytes 14417920 | tf_op jit(solution)/shard_map/dot_general | solution.py:20
  181.8 0.0 reduce-scatter.11.cloned.1.call-update
  181.8 0.0 reduce-scatter.9.cloned.1.call-start
  181.8 12.8 %fusion.14 = bf16[1024,1664]{1,0:T(8,128)(2,1)} fusion(bf16[1024,2048]{1,0:T(8,128)(2,1)} %all-gather.3.cloned.1.call-done, bf16[6656,2048]{1,0:T(8,128)(2,1)} %param.7), kind=kOutput, calls=%fused_computation.13 | convolution fusion | flops 6981025792 | bytes 14417920 | tf_op jit(solution)/shard_map/dot_general | solution.py:20
  194.6 0.0 reduce-scatter.9.cloned.1.call-update
  194.7 0.0 reduce-scatter.7.cloned.1.call-start
  194.7 12.9 %fusion.11 = bf16[1024,1664]{1,0:T(8,128)(2,1)} fusion(bf16[1024,2048]{1,0:T(8,128)(2,1)} %all-gather.3.cloned.1.call-done, bf16[6656,2048]{1,0:T(8,128)(2,1)} %param.7), kind=kOutput, calls=%fused_computation.12 | convolution fusion | flops 6981025792 | bytes 14417920 | tf_op jit(solution)/shard_map/dot_general | solution.py:20
  207.6 0.0 reduce-scatter.7.cloned.1.call-update
  207.6 0.2 reduce-scatter.5.cloned.1.call-start
  207.9 12.9 %fusion.8 = bf16[1024,1664]{1,0:T(8,128)(2,1)} fusion(bf16[1024,2048]{1,0:T(8,128)(2,1)} %all-gather.3.cloned.1.call-done, bf16[6656,2048]{1,0:T(8,128)(2,1)} %param.7), kind=kOutput, calls=%fused_computation.11 | convolution fusion | flops 6981025792 | bytes 14417920 | tf_op jit(solution)/shard_map/dot_general | solution.py:20
  220.7 0.0 reduce-scatter.5.cloned.1.call-update
  220.8 0.0 copy-start
  220.8 0.0 copy-start.1
  220.8 35.8 %convolution_convert_fusion = bf16[6656,2048]{1,0:T(8,128)(2,1)} fusion(bf16[1024,6656]{1,0:T(8,128)(2,1)} %all-gather.5.cloned.1.call-done, bf16[1024,2048]{1,0:T(8,128)(2,1)} %all-gather.3.cloned.1.call-done), kind=kOutput, calls=%fused_computation | convolution fusion | flops 27930918912 | bytes 45088768 | tf_op jit(solution)/shard_map/dot_general | solution.py:28
  256.6 0.0 reduce-scatter.11.cloned.1.call-done
  256.6 24.1 %reduce-scatter.9.cloned.1.call-done = bf16[128,1664]{1,0:T(8,128)(2,1)} async-done(((bf16[1024,1664]{1,0:T(8,128)(2,1)}), bf16[128,1664]{1,0:T(8,128)(2,1)}) %reduce-scatter.9.cloned.1.call-update) | async-done | bytes 426000 | tf_op jit(solution)/shard_map/reduce_scatter | solution.py:23
  280.7 50.8 %reduce-scatter.7.cloned.1.call-done = bf16[128,1664]{1,0:T(8,128)(2,1)} async-done(((bf16[1024,1664]{1,0:T(8,128)(2,1)}), bf16[128,1664]{1,0:T(8,128)(2,1)}) %reduce-scatter.7.cloned.1.call-update) | async-done | bytes 426000 | tf_op jit(solution)/shard_map/reduce_scatter | solution.py:23
  331.5 51.2 %reduce-scatter.5.cloned.1.call-done = bf16[128,1664]{1,0:T(8,128)(2,1)} async-done(((bf16[1024,1664]{1,0:T(8,128)(2,1)}), bf16[128,1664]{1,0:T(8,128)(2,1)}) %reduce-scatter.5.cloned.1.call-update) | async-done | bytes 426000 | tf_op jit(solution)/shard_map/reduce_scatter | solution.py:23
  382.7 0.0 copy-done
  382.7 0.0 copy-done.1
  382.7 3.2 fusion.27
  385.9 1.9 pad_maximum_fusion
Async XLA Ops:
  7.2 82.8 %all-gather.3.cloned.1.call-start = ((), (), s32[]{:S(2)}) async-start(), calls=%async_computation.4 | async-start | bytes 5242880 | tf_op jit(solution)/shard_map/all_gather | solution.py:13
  7.9 161.1 %all-gather.5.cloned.1.call-start = ((), (), s32[]{:S(2)}) async-start(), calls=%async_computation.5 | async-start | bytes 15335424 | tf_op jit(solution)/shard_map/all_gather | solution.py:14
  12.1 244.4 %reduce-scatter.11.cloned.1.call-start = ((), (), s32[]{:S(2)}) async-start(), calls=%async_computation.9 | async-start | bytes 3833856 | tf_op jit(solution)/shard_map/reduce_scatter | solution.py:23
  181.8 98.9 %reduce-scatter.9.cloned.1.call-start = ((), (), s32[]{:S(2)}) async-start(), calls=%async_computation.8 | async-start | bytes 3833856 | tf_op jit(solution)/shard_map/reduce_scatter | solution.py:23
  194.7 136.8 %reduce-scatter.7.cloned.1.call-start = ((), (), s32[]{:S(2)}) async-start(), calls=%async_computation.7 | async-start | bytes 3833856 | tf_op jit(solution)/shard_map/reduce_scatter | solution.py:23
  207.6 175.1 %reduce-scatter.5.cloned.1.call-start = ((), (), s32[]{:S(2)}) async-start(), calls=%async_computation.6 | async-start | bytes 3833856 | tf_op jit(solution)/shard_map/reduce_scatter | solution.py:23
  220.8 162.0 %copy-start = (bf16[128,6656]{1,0:T(8,128)(2,1)S(1)}, bf16[128,6656]{1,0:T(8,128)(2,1)}, u32[]{:S(2)}) copy-start(bf16[128,6656]{1,0:T(8,128)(2,1)} %param.6) | copy-start | bytes 5111812
  220.8 162.0 %copy-start.1 = (bf16[128,6656]{1,0:T(8,128)(2,1)S(1)}, bf16[128,6656]{1,0:T(8,128)(2,1)}, u32[]{:S(2)}) copy-start(bf16[128,6656]{1,0:T(8,128)(2,1)} %param.5) | copy-start | bytes 5111812
Sparse Core Ops, SparseCore 0:
  9.6 80.3 all-gather.2
  92.4 76.5 all-gather.4
  181.9 47.4 reduce-scatter.10
  233.2 47.4 reduce-scatter.8
  284.0 47.4 reduce-scatter.6
  335.2 47.4 reduce-scatter.4

commit v2 on v1

v2 whole, which is shorter than its diff:
```python
import functools

import jax
import jax.numpy as jnp
from jax import lax
from jax.experimental import pallas as pl
from jax.experimental.pallas import tpu as pltpu
from jax.sharding import PartitionSpec as P

F32, BF16 = jnp.float32, jnp.bfloat16
VMEM_LIMIT = 40 * 1024 * 1024
CHUNKS = 4
UNIT = 256


def params():
    return pltpu.CompilerParams(vmem_limit_bytes=VMEM_LIMIT)


def divisor(extent, most, step):
    best = extent
    for size in range(step, most + 1, step):
        if extent % size == 0:
            best = size
    return best


def hidden_kernel(gate_ref, up_ref, out_ref):
    gate = gate_ref[...].astype(F32)
    hidden = gate * jax.nn.sigmoid(gate) * up_ref[...].astype(F32)
    out_ref[...] = jnp.transpose(hidden).astype(BF16)


def hidden_transposed(gate, up, half):
    tokens, width = gate.shape
    rows = width // 2
    step = divisor(rows, 1664, 128)
    first = half * (rows // step)
    spec = pl.BlockSpec((tokens, step), lambda i: (0, first + i))
    return pl.pallas_call(
        hidden_kernel,
        grid=(rows // step,),
        in_specs=[spec, spec],
        out_specs=pl.BlockSpec((step, tokens), lambda i: (i, 0)),
        out_shape=jax.ShapeDtypeStruct((rows, tokens), BF16),
        compiler_params=params(),
        cost_estimate=pl.CostEstimate(
            flops=10 * rows * tokens, bytes_accessed=6 * rows * tokens, transcendentals=rows * tokens
        ),
        name="hidden",
    )(gate, up)


def reorder_kernel(order_ref, in_ref, out_ref):
    out_ref[...] = in_ref[...]


def reorder(x, order, rows):
    depth = x.shape[1]
    grid_spec = pltpu.PrefetchScalarGridSpec(
        num_scalar_prefetch=1,
        grid=(x.shape[0] // rows,),
        in_specs=[pl.BlockSpec((rows, depth), lambda i, at: (at[i], 0))],
        out_specs=pl.BlockSpec((rows, depth), lambda i, at: (i, 0)),
    )
    return pl.pallas_call(
        reorder_kernel,
        grid_spec=grid_spec,
        out_shape=jax.ShapeDtypeStruct(x.shape, x.dtype),
        compiler_params=params(),
        cost_estimate=pl.CostEstimate(flops=0, bytes_accessed=4 * x.size, transcendentals=0),
        name="reorder",
    )(order, x)


def product_kernel(dy_ref, weight_ref, keep_ref, send_ref):
    half = keep_ref.shape[0]
    part = lax.dot_general(
        dy_ref[...], weight_ref[...], (((1,), (1,)), ((), ())), preferred_element_type=F32
    )
    keep_ref[...] = part[:half]
    send_ref[...] = part[half:].astype(BF16)


def hidden_grad_terms(dy, weight, first, tiles):
    tokens, depth = dy.shape
    half, width = tokens // 2, tiles * UNIT
    return pl.pallas_call(
        product_kernel,
        grid=(tiles,),
        in_specs=[
            pl.BlockSpec((tokens, depth), lambda i: (0, 0)),
            pl.BlockSpec((UNIT, depth), lambda i: (first + i, 0)),
        ],
        out_specs=[
            pl.BlockSpec((half, UNIT), lambda i: (0, i)),
            pl.BlockSpec((half, UNIT), lambda i: (0, i)),
        ],
        out_shape=[
            jax.ShapeDtypeStruct((half, width), F32),
            jax.ShapeDtypeStruct((half, width), BF16),
        ],
        compiler_params=params(),
        cost_estimate=pl.CostEstimate(
            flops=2 * tokens * depth * width,
            bytes_accessed=2 * (tokens * depth + depth * width) + 6 * half * width,
            transcendentals=0,
        ),
        name="hidden_grad_terms",
    )(dy, weight)


def weight_grad_kernel(pieces, *refs):
    dy_ref, out_ref = refs[pieces], refs[-1]
    hidden = jnp.concatenate([ref[...] for ref in refs[:pieces]], axis=1)
    out_ref[...] = jnp.dot(hidden, dy_ref[...], preferred_element_type=F32).astype(BF16)


def weight_grad(pieces, dy, whole, half):
    rows, block = pieces[0].shape
    tokens, depth = dy.shape
    tall = divisor(rows, 832, 16)
    wide = divisor(depth, 1024, 128)
    first = half * (rows // tall)
    n = len(pieces)
    in_specs = [pl.BlockSpec((tall, block), lambda i, k: (i, 0))] * n + [
        pl.BlockSpec((tokens, wide), lambda i, k: (0, k))
    ]
    args = list(pieces) + [dy]
    kernel = functools.partial(weight_grad_kernel, n)
    aliases = {}
    if whole is not None:
        in_specs.append(pl.BlockSpec(memory_space=pl.ANY))
        args.append(whole)
        aliases = {n + 1: 0}
    return pl.pallas_call(
        kernel,
        grid=(rows // tall, depth // wide),
        in_specs=in_specs,
        out_specs=pl.BlockSpec((tall, wide), lambda i, k: (first + i, k)),
        out_shape=jax.ShapeDtypeStruct((2 * rows, depth), BF16),
        input_output_aliases=aliases,
        compiler_params=params(),
        cost_estimate=pl.CostEstimate(
            flops=2 * rows * tokens * depth,
            bytes_accessed=2 * (rows * tokens + tokens * depth + rows * depth),
            transcendentals=0,
        ),
        name="weight_grad",
    )(*args)


def local(row_count, grad_out, gate_act, up_act, down_weight):
    me = lax.axis_index("row")
    bits = []
    while 2 ** (len(bits) + 1) < row_count:
        bits.append(2 ** (len(bits) + 1))
    streams = (bits, bits[::-1])
    width = down_weight.shape[0]
    block = gate_act.shape[0]

    def swap(x, bit):
        return lax.ppermute(x, "row", [(r, r ^ bit) for r in range(row_count)])

    def flips(order):
        found = [0]
        for bit in order[::-1] + [1]:
            found = found + [f | bit for f in found]
        return found

    dy = lax.all_gather(grad_out, "col", axis=0, tiled=True)

    gathered = []
    for half in range(2):
        held = {0: hidden_transposed(gate_act, up_act, half)}
        for bit in streams[half] + [1]:
            held.update({f | bit: swap(x, bit) for f, x in list(held.items())})
        gathered.append(held)

    dys = [
        reorder(dy, jnp.bitwise_xor(jnp.array(flips(s), jnp.int32), me.astype(jnp.int32)), block)
        for s in streams
    ]

    units = width // UNIT
    edges = [units * k // CHUNKS for k in range(CHUNKS + 1)]
    gate_parts, up_parts = [], []
    for k in range(CHUNKS):
        first, tiles = edges[k], edges[k + 1] - edges[k]
        stream = k % 2
        keep, send = hidden_grad_terms(dys[stream], down_weight, first, tiles)
        terms = [keep, swap(send, 1)]
        for bit in streams[stream]:
            rows = terms[0].shape[0] // 2
            send = sum(t[rows:].astype(F32) for t in terms).astype(BF16)
            terms = [t[:rows] for t in terms] + [swap(send, bit)]
        grad_hidden = sum(t.astype(F32) for t in terms)
        cut = slice(first * UNIT, (first + tiles) * UNIT)
        g, u = gate_act[:, cut].astype(F32), up_act[:, cut].astype(F32)
        sig = jax.nn.sigmoid(g)
        gate_parts.append((grad_hidden * u * sig * (1.0 + g * (1.0 - sig))).astype(BF16))
        up_parts.append((grad_hidden * (g * sig)).astype(BF16))

    grad_down = None
    for half in range(2):
        pieces = [gathered[half][f] for f in flips(streams[0])]
        grad_down = weight_grad(pieces, dys[0], grad_down, half)
    return jnp.concatenate(gate_parts, 1), jnp.concatenate(up_parts, 1), grad_down


def solution(mesh):
    return jax.shard_map(
        functools.partial(local, mesh.shape["row"]),
        mesh=mesh,
        in_specs=(P("col", "row"), P("row", "col"), P("row", "col"), P("col", "row")),
        out_specs=(P("row", "col"), P("row", "col"), P("col", "row")),
        check_vma=False,
    )
```

time: 396 us -> 273 us (0.69)
  waiting for transfers between devices: 284 us -> 117 us
  matrix products: 87.1 us -> 0 us
  Pallas kernels: 0 us -> 83.1 us
  starting transfers between devices: 0.42 us -> 18.4 us
  local copies, waits for them, and re-layouts: 0.01 us -> 17.6 us
  other arithmetic: 9.25 us -> 18.3 us
    reduce_scatter x4 -> x0, waiting for transfers between devices: 126 us -> none  [local(): lax.psum_scatter(part, 'row', scatter_dimension=0, tiled=True).astype(f32)]
    dot_general x5 -> x0, matrix products: 87.1 us -> none  [the longest x4 51.3 us: local(): lax.dot_general(dy, down_weight[cut], (((1,), (1,)), ((), ())), preferred...]
    pallas_call x0 -> x10, Pallas kernels: none -> 83.1 us  [the longest x4 41.8 us: hidden_grad_terms(): pl.pallas_call(product_kernel, grid=(tiles,), in_specs=[pl.BlockSpec((tok...]
    all_gather x1 -> x0, waiting for transfers between devices: 79 us -> none  [local(): hidden = lax.all_gather(hidden, 'row', axis=0, tiled=True)]
    ppermute x0 -> x26, waiting for transfers between devices: none -> 61.6 us  [swap(): return lax.ppermute(x, 'row', [(r, r ^ bit) for r in range(row_count)])]
    all_gather x1, waiting for transfers between devices: 77.8 us -> 54.9 us  [local(): dy = lax.all_gather(grad_out, 'col', axis=0, tiled=True)]
    ppermute x0 -> x26, starting transfers between devices: none -> 18.4 us  [swap(): return lax.ppermute(x, 'row', [(r, r ^ bit) for r in range(row_count)])]
    unnamed x4 -> x42, local copies, waits for them, and re-layouts: 0.01 us -> 17.6 us
  transfers between devices with their start and end apart: 6 -> 27, of which waited for: 5 -> 7; matrix products, arithmetic and copies ran while one was open for 20% -> 6% of each run, Pallas kernels for 0% -> 31%
where the time goes in v2:
time: 273 us; the launch traced here: 269 us
  waiting for transfers between devices  117 us (43%)
  Pallas kernels  83.1 us (30%)
  starting transfers between devices  18.4 us (7%)
  other arithmetic  18.3 us (7%)
  local copies, waits for them, and re-layouts  17.6 us (6%)
  between operations  14.2 us (5%)
    ppermute x26, waiting for transfers between devices, swap(): return lax.ppermute(x, 'row', [(r, r ^ bit) for r in range(row_count)])  61.6 us
    all_gather x1, waiting for transfers between devices, local(): dy = lax.all_gather(grad_out, 'col', axis=0, tiled=True)  54.9 us
    pallas_call x4, Pallas kernels, hidden_grad_terms(): pl.pallas_call(product_kernel, grid=(tiles,), in_specs=[pl.BlockSpec((tok...  41.8 us
    pallas_call x2, Pallas kernels, weight_grad(): pl.pallas_call(kernel, grid=(rows // tall, depth // wide), in_specs=in_sp...  38 us
    ppermute x26, starting transfers between devices, swap(): return lax.ppermute(x, 'row', [(r, r ^ bit) for r in range(row_count)])  18.4 us
    unnamed x42, local copies, waits for them, and re-layouts  17.6 us
    convert_element_type x8, other arithmetic, local(): send = sum((t[rows:].astype(F32) for t in terms)).astype(BF16)  10 us
    convert_element_type x4, other arithmetic, local(): up_parts.append((grad_hidden * (g * sig)).astype(BF16))  6.43 us
  transfers between devices with their start and end apart: 27, of which 7 were waited for; matrix products, arithmetic and copies ran while one was open for 6% of the time, Pallas kernels for 31%

profile of v2, /device:TPU:16, one launch (start us, length us, event | category | flops | bytes accessed | tf_op | source)
XLA Modules:
  0.0 268.8 jit_solution(5694520945220880375)
XLA Ops:
  7.9 1.4 copy-done.2
  9.4 1.5 copy-done.4
  11.6 1.6 collective-permute-start.20
  14.4 1.5 collective-permute-start.12
  16.5 17.1 %collective-permute-done.20.refs_2_ = bf16[3328,128]{1,0:T(8,128)(2,1)} collective-permute-done((bf16[3328,128]{1,0:T(8,128)(2,1)S(1)}, bf16[3328,128]{1,0:T(8,128)(2,1)}, u32[]{:S(2)}, u32[]{:S(2)}) %collective-permute-start.20) | collective-permute-done | bytes 852000 | tf_op jit(solution)/shard_map/ppermute | solution.py:163
  33.6 1.5 collective-permute-start.21
  35.1 54.9 %all-gather.2.cloned.1.call-done.in_ref = bf16[1024,2048]{1,0:T(8,128)(2,1)} async-done(((bf16[256,2048]{1,0:T(8,128)(2,1)}), bf16[1024,2048]{1,0:T(8,128)(2,1)}) %all-gather.2.cloned.1.call-update) | async-done | bytes 4194320 | tf_op jit(solution)/shard_map/all_gather | solution.py:171
  90.0 2.2 copy-done
  92.2 0.9 reorder.2.dy_ref.refs_8_
  93.1 1.2 copy-done.1
  94.4 0.9 reorder.3.dy_ref
  95.3 11.3 %hidden_grad_terms.7 = (f32[512,1792]{1,0:T(8,128)S(1)}, bf16[512,1792]{1,0:T(8,128)(2,1)}) custom-call(bf16[1024,2048]{1,0:T(8,128)(2,1)S(1)} %reorder.3.dy_ref, bf16[6656,2048]{1,0:T(8,128)(2,1)} %weight_ref.7), custom_call_target="tpu_custom_call" | custom-call | flops 7516192768 | bytes 17039360 | tf_op jit(solution)/shard_map/hidden_grad_terms/pallas_call | solution.py:88
  106.6 1.5 collective-permute-start.14
  108.6 9.3 %hidden_grad_terms.6 = (f32[512,1536]{1,0:T(8,128)S(1)}, bf16[512,1536]{1,0:T(8,128)(2,1)S(1)}) custom-call(bf16[1024,2048]{1,0:T(8,128)(2,1)S(1)} %reorder.2.dy_ref.refs_8_, bf16[6656,2048]{1,0:T(8,128)(2,1)} %weight_ref.7), custom_call_target="tpu_custom_call" | custom-call | flops 6442450944 | bytes 15204352 | tf_op jit(solution)/shard_map/hidden_grad_terms/pallas_call | solution.py:88
  118.0 1.1 copy-done.14
  119.1 12.0 %hidden_grad_terms.5 = (f32[512,1792]{1,0:T(8,128)S(1)}, bf16[512,1792]{1,0:T(8,128)(2,1)}) custom-call(bf16[1024,2048]{1,0:T(8,128)(2,1)S(1)} %reorder.3.dy_ref, bf16[6656,2048]{1,0:T(8,128)(2,1)} %weight_ref.7), custom_call_target="tpu_custom_call" | custom-call | flops 7516192768 | bytes 17039360 | tf_op jit(solution)/shard_map/hidden_grad_terms/pallas_call | solution.py:88
  131.6 0.9 copy-done.15
  134.1 1.2 copy-done.16
  135.2 1.2 copy-done.18
  136.4 19.0 %weight_grad.2.refs_9_ = bf16[6656,2048]{1,0:T(8,128)(2,1)} custom-call(bf16[3328,128]{1,0:T(8,128)(2,1)S(1)} %hidden.3.refs_0_, bf16[3328,128]{1,0:T(8,128)(2,1)} %collective-permute-done.19.refs_1_, bf16[3328,128]{1,0:T(8,128)(2,1)} %collective-permute-done.20.refs_2_, bf16[3328,128]{1,0:T(8,128)(2,1)} %collective-permute-done.21.refs_3_, ...), custom_call_target="tpu_custom_call" | custom-call | flops 13958643712 | bytes 24641536 | tf_op jit(solution)/shard_map/weight_grad/pallas_call | solution.py:136
  155.4 9.3 %hidden_grad_terms.4 = (f32[512,1536]{1,0:T(8,128)S(1)}, bf16[512,1536]{1,0:T(8,128)(2,1)S(1)}) custom-call(bf16[1024,2048]{1,0:T(8,128)(2,1)S(1)} %reorder.2.dy_ref.refs_8_, bf16[6656,2048]{1,0:T(8,128)(2,1)} %weight_ref.7), custom_call_target="tpu_custom_call" | custom-call | flops 6442450944 | bytes 15204352 | tf_op jit(solution)/shard_map/hidden_grad_terms/pallas_call | solution.py:88
  164.7 1.7 copy-done.8
  166.7 0.9 copy-done.12
  169.0 1.3 copy-done.11
  170.4 1.2 copy-done.13
  171.5 18.9 %weight_grad.3 = bf16[6656,2048]{1,0:T(8,128)(2,1)} custom-call(bf16[3328,128]{1,0:T(8,128)(2,1)S(1)} %hidden.2.refs_0_, bf16[3328,128]{1,0:T(8,128)(2,1)} %collective-permute-done.12.refs_1_, bf16[3328,128]{1,0:T(8,128)(2,1)} %collective-permute-done.13.refs_2_, bf16[3328,128]{1,0:T(8,128)(2,1)} %collective-permute-done.14.refs_3_, ...), custom_call_target="tpu_custom_call", output_to_operand_aliasing={{}: (9, {})} | custom-call | flops 13958643712 | bytes 24641536 | tf_op jit(solution)/shard_map/weight_grad/pallas_call | solution.py:136
  190.5 1.5 add_convert_fusion.2
  192.6 1.3 add_convert_fusion.3
  193.9 1.5 collective-permute-start.1
  195.4 1.3 add_convert_fusion.1
  196.8 1.5 collective-permute-start.4
  198.3 1.3 add_convert_fusion
  200.3 12.1 %collective-permute-done.7 = bf16[256,1536]{1,0:T(8,128)(2,1)S(1)} collective-permute-done((bf16[256,1536]{1,0:T(8,128)(2,1)S(1)}, bf16[256,1536]{1,0:T(8,128)(2,1)S(1)}, u32[]{:S(2)}, u32[]{:S(2)}) %collective-permute-start.7) | collective-permute-done | bytes 786464 | tf_op jit(solution)/shard_map/ppermute | solution.py:163
  212.4 1.1 add_convert_fusion.6
  213.5 1.5 collective-permute-start.8
  215.1 13.4 %collective-permute-done.1 = bf16[256,1536]{1,0:T(8,128)(2,1)S(1)} collective-permute-done((bf16[256,1536]{1,0:T(8,128)(2,1)S(1)}, bf16[256,1536]{1,0:T(8,128)(2,1)S(1)}, u32[]{:S(2)}, u32[]{:S(2)}) %collective-permute-start.1) | collective-permute-done | bytes 786464 | tf_op jit(solution)/shard_map/ppermute | solution.py:163
  228.4 1.1 add_convert_fusion.7
  229.6 1.5 collective-permute-start.2
  231.1 1.2 add_convert_fusion.5
  232.9 6.9 %collective-permute-done.10 = bf16[256,1792]{1,0:T(8,128)(2,1)S(1)} collective-permute-done((bf16[256,1792]{1,0:T(8,128)(2,1)S(1)}, bf16[256,1792]{1,0:T(8,128)(2,1)S(1)}, u32[]{:S(2)}, u32[]{:S(2)}) %collective-permute-start.10) | collective-permute-done | bytes 917536 | tf_op jit(solution)/shard_map/ppermute | solution.py:163
  239.8 1.2 add_convert_fusion.4
  241.6 6.6 %collective-permute-done.8 = bf16[128,1536]{1,0:T(8,128)(2,1)S(1)} collective-permute-done((bf16[128,1536]{1,0:T(8,128)(2,1)S(1)}, bf16[128,1536]{1,0:T(8,128)(2,1)S(1)}, u32[]{:S(2)}, u32[]{:S(2)}) %collective-permute-start.8) | collective-permute-done | bytes 393248 | tf_op jit(solution)/shard_map/ppermute | solution.py:163
  248.2 1.6 fusion.31
  249.8 5.4 %collective-permute-done.2 = bf16[128,1536]{1,0:T(8,128)(2,1)S(1)} collective-permute-done((bf16[128,1536]{1,0:T(8,128)(2,1)S(1)}, bf16[128,1536]{1,0:T(8,128)(2,1)S(1)}, u32[]{:S(2)}, u32[]{:S(2)}) %collective-permute-start.2) | collective-permute-done | bytes 393248 | tf_op jit(solution)/shard_map/ppermute | solution.py:163
  255.2 1.5 fusion.23
  256.7 1.7 fusion.7
  258.4 1.7 fusion.15
  260.1 1.9 pad_maximum_fusion
  (74 shorter events, 10.2 us)
Async XLA Ops:
  7.2 82.8 %all-gather.2.cloned.1.call-start = ((), (), s32[]{:S(2)}) async-start(), calls=%async_computation | async-start | bytes 5242880 | tf_op jit(solution)/shard_map/all_gather | solution.py:171
  7.9 1.5 copy-start.2
  9.4 1.5 copy-start.4
  11.5 4.9 %copy-start.20 = (s32[8]{0:T(128)S(1)}, s32[8]{0:T(128)}, u32[]{:S(2)}) copy-start(s32[8]{0:T(128)} %constant.13.clone) | copy-start | bytes 100
  11.5 23.5 %copy-start.19 = (s32[8]{0:T(128)S(1)}, s32[8]{0:T(128)}, u32[]{:S(2)}) copy-start(s32[8]{0:T(128)} %constant.14.clone) | copy-start | bytes 100
  11.6 22.0 %collective-permute-start.20 = (bf16[3328,128]{1,0:T(8,128)(2,1)S(1)}, bf16[3328,128]{1,0:T(8,128)(2,1)}, u32[]{:S(2)}, u32[]{:S(2)}) collective-permute-start(bf16[3328,128]{1,0:T(8,128)(2,1)S(1)} %hidden.3.refs_0_), channel_id=1, source_target_pairs={{0,8},{4,12},{8,0},{12,4},{16,24},{20,28},{24,16},{28,20},{1,9},{5... | collective-permute-start | bytes 2555912 | tf_op jit(solution)/shard_map/ppermute | solution.py:163
  13.8 92.7 %collective-permute-start.13 = (bf16[3328,128]{1,0:T(8,128)(2,1)S(1)}, bf16[3328,128]{1,0:T(8,128)(2,1)}, u32[]{:S(2)}, u32[]{:S(2)}) collective-permute-start(bf16[3328,128]{1,0:T(8,128)(2,1)S(1)} %hidden.2.refs_0_), channel_id=1, source_target_pairs={{0,8},{4,12},{8,0},{12,4},{16,24},{20,28},{24,16},{28,20},{1,9},{5... | collective-permute-start | bytes 2555912 | tf_op jit(solution)/shard_map/ppermute | solution.py:163
  14.4 92.1 %collective-permute-start.12 = (bf16[3328,128]{1,0:T(8,128)(2,1)S(1)}, bf16[3328,128]{1,0:T(8,128)(2,1)}, u32[]{:S(2)}, u32[]{:S(2)}) collective-permute-start(bf16[3328,128]{1,0:T(8,128)(2,1)S(1)} %hidden.2.refs_0_), channel_id=1, source_target_pairs={{0,16},{4,20},{8,24},{12,28},{16,0},{20,4},{24,8},{28,12},{1,17},{... | collective-permute-start | bytes 2555912 | tf_op jit(solution)/shard_map/ppermute | solution.py:163
  16.0 115.1 %collective-permute-start.22 = (bf16[3328,128]{1,0:T(8,128)(2,1)S(1)}, bf16[3328,128]{1,0:T(8,128)(2,1)}, u32[]{:S(2)}, u32[]{:S(2)}) collective-permute-start(bf16[3328,128]{1,0:T(8,128)(2,1)S(1)} %hidden.3.refs_0_), channel_id=1, source_target_pairs={{0,4},{4,0},{8,12},{12,8},{16,20},{20,16},{24,28},{28,24},{1,5},{5... | collective-permute-start | bytes 2555912 | tf_op jit(solution)/shard_map/ppermute | solution.py:163
  16.0 92.2 %collective-permute-start.19 = (bf16[3328,128]{1,0:T(8,128)(2,1)S(1)}, bf16[3328,128]{1,0:T(8,128)(2,1)}, u32[]{:S(2)}, u32[]{:S(2)}) collective-permute-start(bf16[3328,128]{1,0:T(8,128)(2,1)S(1)} %hidden.3.refs_0_), channel_id=1, source_target_pairs={{0,16},{4,20},{8,24},{12,28},{16,0},{20,4},{24,8},{28,12},{1,17},{... | collective-permute-start | bytes 2555912 | tf_op jit(solution)/shard_map/ppermute | solution.py:163
  33.6 74.7 %collective-permute-start.21 = (bf16[3328,128]{1,0:T(8,128)(2,1)}, bf16[3328,128]{1,0:T(8,128)(2,1)}, u32[]{:S(2)}, u32[]{:S(2)}) collective-permute-start(bf16[3328,128]{1,0:T(8,128)(2,1)} %collective-permute-done.20.refs_2_), channel_id=1, source_target_pairs={{0,16},{4,20},{8,24},{12,28},{16,0},{20,4},{24,8},{28,12},{1,17},{... | collective-permute-start | bytes 2555912 | tf_op jit(solution)/shard_map/ppermute | solution.py:163
  90.0 2.2 copy-start
  92.2 2.2 copy-start.1
  106.6 25.0 %collective-permute-start.24 = (bf16[3328,128]{1,0:T(8,128)(2,1)}, bf16[3328,128]{1,0:T(8,128)(2,1)S(1)}, u32[]{:S(2)}, u32[]{:S(2)}) collective-permute-start(bf16[3328,128]{1,0:T(8,128)(2,1)} %collective-permute-done.20.refs_2_), channel_id=1, source_target_pairs={{0,4},{4,0},{8,12},{12,8},{16,20},{20,16},{24,28},{28,24},{1,5},{5... | collective-permute-start | bytes 2555912 | tf_op jit(solution)/shard_map/ppermute | solution.py:163
  106.6 24.6 %collective-permute-start.14 = (bf16[3328,128]{1,0:T(8,128)(2,1)}, bf16[3328,128]{1,0:T(8,128)(2,1)}, u32[]{:S(2)}, u32[]{:S(2)}) collective-permute-start(bf16[3328,128]{1,0:T(8,128)(2,1)} %collective-permute-done.12.refs_1_), channel_id=1, source_target_pairs={{0,8},{4,12},{8,0},{12,4},{16,24},{20,28},{24,16},{28,20},{1,9},{5... | collective-permute-start | bytes 2555912 | tf_op jit(solution)/shard_map/ppermute | solution.py:163
  108.1 24.5 %collective-permute-start.23 = (bf16[3328,128]{1,0:T(8,128)(2,1)}, bf16[3328,128]{1,0:T(8,128)(2,1)S(1)}, u32[]{:S(2)}, u32[]{:S(2)}) collective-permute-start(bf16[3328,128]{1,0:T(8,128)(2,1)} %collective-permute-done.19.refs_1_), channel_id=1, source_target_pairs={{0,4},{4,0},{8,12},{12,8},{16,20},{20,16},{24,28},{28,24},{1,5},{5... | collective-permute-start | bytes 2555912 | tf_op jit(solution)/shard_map/ppermute | solution.py:163
  108.3 25.6 %collective-permute-start.25 = (bf16[3328,128]{1,0:T(8,128)(2,1)}, bf16[3328,128]{1,0:T(8,128)(2,1)}, u32[]{:S(2)}, u32[]{:S(2)}) collective-permute-start(bf16[3328,128]{1,0:T(8,128)(2,1)} %collective-permute-done.21.refs_3_), channel_id=1, source_target_pairs={{0,4},{4,0},{8,12},{12,8},{16,20},{20,16},{24,28},{28,24},{1,5},{5... | collective-permute-start | bytes 2555912 | tf_op jit(solution)/shard_map/ppermute | solution.py:163
  117.9 1.1 copy-start.14
  119.1 12.0 %copy-start.6 = (f32[512,1536]{1,0:T(8,128)}, f32[512,1536]{1,0:T(8,128)S(1)}, u32[]{:S(2)}) copy-start(f32[512,1536]{1,0:T(8,128)S(1)} %get-tuple-element.15) | copy-start | bytes 9437188
  131.1 35.3 %collective-permute-start.15 = (bf16[3328,128]{1,0:T(8,128)(2,1)S(1)}, bf16[3328,128]{1,0:T(8,128)(2,1)S(1)}, u32[]{:S(2)}, u32[]{:S(2)}) collective-permute-start(bf16[3328,128]{1,0:T(8,128)(2,1)S(1)} %hidden.2.refs_0_), channel_id=1, source_target_pairs={{0,4},{4,0},{8,12},{12,8},{16,20},{20,16},{24,28},{28,24},{1,5},{5... | collective-permute-start | bytes 2555912 | tf_op jit(solution)/shard_map/ppermute | solution.py:163
  131.2 36.5 %collective-permute-start.16 = (bf16[3328,128]{1,0:T(8,128)(2,1)}, bf16[3328,128]{1,0:T(8,128)(2,1)S(1)}, u32[]{:S(2)}, u32[]{:S(2)}) collective-permute-start(bf16[3328,128]{1,0:T(8,128)(2,1)} %collective-permute-done.12.refs_1_), channel_id=1, source_target_pairs={{0,4},{4,0},{8,12},{12,8},{16,20},{20,16},{24,28},{28,24},{1,5},{5... | collective-permute-start | bytes 2555912 | tf_op jit(solution)/shard_map/ppermute | solution.py:163
  131.6 0.9 copy-start.15
  132.5 34.2 %collective-permute-start.17 = (bf16[3328,128]{1,0:T(8,128)(2,1)}, bf16[3328,128]{1,0:T(8,128)(2,1)S(1)}, u32[]{:S(2)}, u32[]{:S(2)}) collective-permute-start(bf16[3328,128]{1,0:T(8,128)(2,1)} %collective-permute-done.13.refs_2_), channel_id=1, source_target_pairs={{0,4},{4,0},{8,12},{12,8},{16,20},{20,16},{24,28},{28,24},{1,5},{5... | collective-permute-start | bytes 2555912 | tf_op jit(solution)/shard_map/ppermute | solution.py:163
  132.6 0.9 copy-start.17
  133.5 35.5 %collective-permute-start.18 = (bf16[3328,128]{1,0:T(8,128)(2,1)}, bf16[3328,128]{1,0:T(8,128)(2,1)}, u32[]{:S(2)}, u32[]{:S(2)}) collective-permute-start(bf16[3328,128]{1,0:T(8,128)(2,1)} %collective-permute-done.14.refs_3_), channel_id=1, source_target_pairs={{0,4},{4,0},{8,12},{12,8},{16,20},{20,16},{24,28},{28,24},{1,5},{5... | collective-permute-start | bytes 2555912 | tf_op jit(solution)/shard_map/ppermute | solution.py:163
  133.9 56.6 %collective-permute-start.6 = (bf16[512,1536]{1,0:T(8,128)(2,1)}, bf16[512,1536]{1,0:T(8,128)(2,1)}, u32[]{:S(2)}, u32[]{:S(2)}) collective-permute-start(bf16[512,1536]{1,0:T(8,128)(2,1)} %copy-done.14), channel_id=1, source_target_pairs={{0,4},{4,0},{8,12},{12,8},{16,20},{20,16},{24,28},{28,24},{1,5},{5... | collective-permute-start | bytes 4718600 | tf_op jit(solution)/shard_map/ppermute | solution.py:163
  134.1 1.2 copy-start.16
  135.2 1.2 copy-start.18
  164.7 1.7 copy-start.8
  166.3 26.2 %collective-permute-start = (bf16[512,1536]{1,0:T(8,128)(2,1)S(1)}, bf16[512,1536]{1,0:T(8,128)(2,1)}, u32[]{:S(2)}, u32[]{:S(2)}) collective-permute-start(bf16[512,1536]{1,0:T(8,128)(2,1)S(1)} %get-tuple-element.12), channel_id=1, source_target_pairs={{0,4},{4,0},{8,12},{12,8},{16,20},{20,16},{24,28},{28,24},{1,5},{5... | collective-permute-start | bytes 4718600 | tf_op jit(solution)/shard_map/ppermute | solution.py:163
  166.7 0.9 copy-start.12
  167.6 27.8 %collective-permute-start.3 = (bf16[512,1792]{1,0:T(8,128)(2,1)}, bf16[512,1792]{1,0:T(8,128)(2,1)}, u32[]{:S(2)}, u32[]{:S(2)}) collective-permute-start(bf16[512,1792]{1,0:T(8,128)(2,1)} %get-tuple-element.14), channel_id=1, source_target_pairs={{0,4},{4,0},{8,12},{12,8},{16,20},{20,16},{24,28},{28,24},{1,5},{5... | collective-permute-start | bytes 5505032 | tf_op jit(solution)/shard_map/ppermute | solution.py:163
  167.8 0.9 copy-start.10
  168.7 21.8 %copy-start.7 = (f32[512,1536]{1,0:T(8,128)S(1)}, f32[512,1536]{1,0:T(8,128)}, u32[]{:S(2)}) copy-start(f32[512,1536]{1,0:T(8,128)} %copy-done.6) | copy-start | bytes 9437188
  168.7 29.6 %collective-permute-start.9 = (bf16[512,1792]{1,0:T(8,128)(2,1)}, bf16[512,1792]{1,0:T(8,128)(2,1)}, u32[]{:S(2)}, u32[]{:S(2)}) collective-permute-start(bf16[512,1792]{1,0:T(8,128)(2,1)} %get-tuple-element.18), channel_id=1, source_target_pairs={{0,4},{4,0},{8,12},{12,8},{16,20},{20,16},{24,28},{28,24},{1,5},{5... | collective-permute-start | bytes 5505032 | tf_op jit(solution)/shard_map/ppermute | solution.py:163
  169.0 1.3 copy-start.11
  170.4 1.2 copy-start.13
  190.5 2.1 copy-start.9
  191.9 20.5 %collective-permute-start.7 = (bf16[256,1536]{1,0:T(8,128)(2,1)S(1)}, bf16[256,1536]{1,0:T(8,128)(2,1)S(1)}, u32[]{:S(2)}, u32[]{:S(2)}) collective-permute-start(bf16[256,1536]{1,0:T(8,128)(2,1)S(1)} %add_convert_fusion.2), channel_id=1, source_target_pairs={{0,8},{4,12},{8,0},{12,4},{16,24},{20,28},{24,16},{28,20},{1,9},{5... | collective-permute-start | bytes 2359304 | tf_op jit(solution)/shard_map/ppermute | solution.py:163
  193.9 34.5 %collective-permute-start.1 = (bf16[256,1536]{1,0:T(8,128)(2,1)S(1)}, bf16[256,1536]{1,0:T(8,128)(2,1)S(1)}, u32[]{:S(2)}, u32[]{:S(2)}) collective-permute-start(bf16[256,1536]{1,0:T(8,128)(2,1)S(1)} %add_convert_fusion.3), channel_id=1, source_target_pairs={{0,8},{4,12},{8,0},{12,4},{16,24},{20,28},{24,16},{28,20},{1,9},{5... | collective-permute-start | bytes 2359304 | tf_op jit(solution)/shard_map/ppermute | solution.py:163
  196.8 34.3 %collective-permute-start.4 = (bf16[256,1792]{1,0:T(8,128)(2,1)S(1)}, bf16[256,1792]{1,0:T(8,128)(2,1)S(1)}, u32[]{:S(2)}, u32[]{:S(2)}) collective-permute-start(bf16[256,1792]{1,0:T(8,128)(2,1)S(1)} %add_convert_fusion.1), channel_id=1, source_target_pairs={{0,16},{4,20},{8,24},{12,28},{16,0},{20,4},{24,8},{28,12},{1,17},{... | collective-permute-start | bytes 2752520 | tf_op jit(solution)/shard_map/ppermute | solution.py:163
  199.6 40.1 %collective-permute-start.10 = (bf16[256,1792]{1,0:T(8,128)(2,1)S(1)}, bf16[256,1792]{1,0:T(8,128)(2,1)S(1)}, u32[]{:S(2)}, u32[]{:S(2)}) collective-permute-start(bf16[256,1792]{1,0:T(8,128)(2,1)S(1)} %add_convert_fusion), channel_id=1, source_target_pairs={{0,16},{4,20},{8,24},{12,28},{16,0},{20,4},{24,8},{28,12},{1,17},{... | collective-permute-start | bytes 2752520 | tf_op jit(solution)/shard_map/ppermute | solution.py:163
  213.5 34.7 %collective-permute-start.8 = (bf16[128,1536]{1,0:T(8,128)(2,1)S(1)}, bf16[128,1536]{1,0:T(8,128)(2,1)S(1)}, u32[]{:S(2)}, u32[]{:S(2)}) collective-permute-start(bf16[128,1536]{1,0:T(8,128)(2,1)S(1)} %add_convert_fusion.6), channel_id=1, source_target_pairs={{0,16},{4,20},{8,24},{12,28},{16,0},{20,4},{24,8},{28,12},{1,17},{... | collective-permute-start | bytes 1179656 | tf_op jit(solution)/shard_map/ppermute | solution.py:163
  229.5 18.7 %copy-start.3 = (bf16[128,6656]{1,0:T(8,128)(2,1)S(1)}, bf16[128,6656]{1,0:T(8,128)(2,1)}, u32[]{:S(2)}) copy-start(bf16[128,6656]{1,0:T(8,128)(2,1)} %gate_ref.3) | copy-start | bytes 5111812
  229.6 18.6 %copy-start.5 = (bf16[128,6656]{1,0:T(8,128)(2,1)S(1)}, bf16[128,6656]{1,0:T(8,128)(2,1)}, u32[]{:S(2)}) copy-start(bf16[128,6656]{1,0:T(8,128)(2,1)} %up_ref.3) | copy-start | bytes 5111812
  229.6 25.6 %collective-permute-start.2 = (bf16[128,1536]{1,0:T(8,128)(2,1)S(1)}, bf16[128,1536]{1,0:T(8,128)(2,1)S(1)}, u32[]{:S(2)}, u32[]{:S(2)}) collective-permute-start(bf16[128,1536]{1,0:T(8,128)(2,1)S(1)} %add_convert_fusion.7), channel_id=1, source_target_pairs={{0,16},{4,20},{8,24},{12,28},{16,0},{20,4},{24,8},{28,12},{1,17},{... | collective-permute-start | bytes 1179656 | tf_op jit(solution)/shard_map/ppermute | solution.py:163
  232.3 24.4 %collective-permute-start.5 = (bf16[128,1792]{1,0:T(8,128)(2,1)S(1)}, bf16[128,1792]{1,0:T(8,128)(2,1)S(1)}, u32[]{:S(2)}, u32[]{:S(2)}) collective-permute-start(bf16[128,1792]{1,0:T(8,128)(2,1)S(1)} %add_convert_fusion.5), channel_id=1, source_target_pairs={{0,8},{4,12},{8,0},{12,4},{16,24},{20,28},{24,16},{28,20},{1,9},{5... | collective-permute-start | bytes 1376264 | tf_op jit(solution)/shard_map/ppermute | solution.py:163
  241.0 17.4 %collective-permute-start.11 = (bf16[128,1792]{1,0:T(8,128)(2,1)S(1)}, bf16[128,1792]{1,0:T(8,128)(2,1)S(1)}, u32[]{:S(2)}, u32[]{:S(2)}) collective-permute-start(bf16[128,1792]{1,0:T(8,128)(2,1)S(1)} %add_convert_fusion.4), channel_id=1, source_target_pairs={{0,8},{4,12},{8,0},{12,4},{16,24},{20,28},{24,16},{28,20},{1,9},{5... | collective-permute-start | bytes 1376264 | tf_op jit(solution)/shard_map/ppermute | solution.py:163
Sparse Core Ops, SparseCore 0:
  9.6 80.3 all-gather.1

commit v3 on v1

v3 whole, which is shorter than its diff:
```python
import jax
import jax.numpy as jnp
from jax import lax
from jax.experimental import pallas as pl
from jax.experimental.pallas import tpu as pltpu
from jax.sharding import PartitionSpec as P

F32, BF16 = jnp.float32, jnp.bfloat16
VMEM_LIMIT = 63 * 1024 * 1024
CHUNKS = 4
PARTS = 4
UNIT = 256
PLAN = "P0 P1 S0 P2 S1 P3 S2 S3 W0 W1 S0 S1 W2 S2 S3 W3 F0 F1 F2 F3".split()


def divisor(extent, most, step):
    best = extent
    for size in range(step, most + 1, step):
        if extent % size == 0:
            best = size
    return best


def run(kernel, name, grid, ins, outs, deps=(), at=None, flops=0, exps=0):
    held = [(n, o[3]) for n, o in enumerate(outs) if o[3] is not None]
    deps = [d for d in deps if not any(d is x for _, x in held)]
    arrays = [x for x, _ in ins] + [x for _, x in held] + list(deps)
    specs = [s for _, s in ins] + [pl.BlockSpec(memory_space=pl.ANY)] * (len(held) + len(deps))
    lead = 0 if at is None else 1
    first_out = lead + len(arrays)

    def body(*refs):
        kernel(*refs[lead : lead + len(ins)], *refs[first_out:])

    moved = sum(x.size * x.dtype.itemsize for x, _ in ins)
    return pl.pallas_call(
        body,
        grid_spec=pltpu.PrefetchScalarGridSpec(
            num_scalar_prefetch=lead, grid=grid, in_specs=specs, out_specs=[o[2] for o in outs]
        ),
        out_shape=[jax.ShapeDtypeStruct(o[0], o[1]) for o in outs],
        input_output_aliases={lead + len(ins) + k: n for k, (n, _) in enumerate(held)},
        compiler_params=pltpu.CompilerParams(vmem_limit_bytes=VMEM_LIMIT),
        cost_estimate=pl.CostEstimate(flops=flops, bytes_accessed=moved, transcendentals=exps),
        name=name,
    )(*([] if at is None else [at]), *arrays)


def hidden_kernel(gate_ref, up_ref, out_ref):
    gate = gate_ref[...].astype(F32)
    hidden = gate * jax.nn.sigmoid(gate) * up_ref[...].astype(F32)
    out_ref[...] = jnp.transpose(hidden).astype(BF16)


def hidden_transposed(gate, up):
    tokens, width = gate.shape
    step = divisor(width, 1664, 128)
    spec = pl.BlockSpec((tokens, step), lambda i: (0, i))
    out = ((width, tokens), BF16, pl.BlockSpec((step, tokens), lambda i: (i, 0)), None)
    return run(hidden_kernel, "hidden", (width // step,), [(gate, spec), (up, spec)], [out])[0]


def product_kernel(mine_ref, other_ref, weight_ref, keep_ref, send_ref, *copy_ref):
    block = mine_ref.shape[0]
    dy = jnp.concatenate([mine_ref[...], other_ref[...]], axis=0)
    part = lax.dot_general(dy, weight_ref[...], (((1,), (1,)), ((), ())), preferred_element_type=F32)
    keep_ref[...] = part[:block]
    send_ref[...] = part[block:].astype(BF16)
    for ref in copy_ref:
        ref[...] = dy


def hidden_grad_terms(at, dy, weight, first, tiles, held, ordered, total, deps):
    block, depth = dy.shape[0] // 2, dy.shape[1]
    shape = (total // 2, tiles * UNIT)
    ins = [
        (dy, pl.BlockSpec((block, depth), lambda i, at: (at[1], 0))),
        (dy, pl.BlockSpec((block, depth), lambda i, at: (at[2], 0))),
        (weight, pl.BlockSpec((UNIT, depth), lambda i, at: (first + i, 0))),
    ]
    spec = pl.BlockSpec((block, UNIT), lambda i, at: (at[0], i))
    outs = [(shape, F32, spec, held[0]), (shape, BF16, spec, held[1])]
    if first == 0:
        copy = pl.BlockSpec((2 * block, depth), lambda i, at: (at[3], 0))
        outs.append(((total, depth), BF16, copy, ordered))
    flops = 4 * block * depth * tiles * UNIT
    return run(product_kernel, "hidden_grad_terms", (tiles,), ins, outs, deps, at, flops)


def stage_kernel(*refs):
    refs[-1][...] = sum(ref[...].astype(F32) for ref in refs[:-1]).astype(BF16)


def stage_sum(terms, rows, deps):
    width = terms[0].shape[1]
    steps = 2
    tall = rows // steps
    ins = [(t, pl.BlockSpec((tall, width), lambda i: (steps + i, 0))) for t in terms]
    out = ((rows, width), BF16, pl.BlockSpec((tall, width), lambda i: (i, 0)), None)
    return run(stage_kernel, "stage_sum", (steps,), ins, [out], deps)[0]


def finish_kernel(gate_ref, up_ref, *refs):
    grad_hidden = sum(ref[...].astype(F32) for ref in refs[:-2])
    gate, up = gate_ref[...].astype(F32), up_ref[...].astype(F32)
    sig = jax.nn.sigmoid(gate)
    refs[-2][...] = (grad_hidden * up * sig * (1.0 + gate * (1.0 - sig))).astype(BF16)
    refs[-1][...] = (grad_hidden * (gate * sig)).astype(BF16)


def finish(gate, up, terms, first, tiles, held, deps):
    tokens = gate.shape[0]
    width = tiles * UNIT
    window = pl.BlockSpec((pl.Element(tokens), pl.Element(width)), lambda i: (0, first * UNIT))
    ins = [(gate, window), (up, window)]
    ins += [(t, pl.BlockSpec((tokens, width), lambda i: (0, 0))) for t in terms]
    outs = [(gate.shape, BF16, window, x) for x in held]
    return run(finish_kernel, "finish", (1,), ins, outs, deps, exps=tokens * width)


def weight_grad_kernel(*refs):
    hidden = jnp.concatenate([ref[...] for ref in refs[:-2]], axis=1)
    refs[-1][...] = jnp.dot(hidden, refs[-2][...], preferred_element_type=F32).astype(BF16)


def weight_grad(pieces, dy, whole, total, start, rows, deps):
    block = pieces[0][0].shape[1]
    tokens, depth = dy.shape
    tall = divisor(rows, 416, 16)

    def spec(base):
        return pl.BlockSpec((tall, block), lambda i: ((start - base) // tall + i, 0))

    ins = [(x, spec(base)) for x, base in pieces]
    ins.append((dy, pl.BlockSpec((tokens, depth), lambda i: (0, 0))))
    out = ((total, depth), BF16, pl.BlockSpec((tall, depth), lambda i: (start // tall + i, 0)), whole)
    flops = 2 * rows * tokens * depth
    return run(weight_grad_kernel, "weight_grad", (rows // tall,), ins, [out], deps, flops=flops)[0]


def arrivals(z, count):
    found = []
    for s in range(1, count):
        if z - s >= 0:
            found.append(("up", s, z - s))
        if z + s < count:
            found.append(("down", s, z + s))
    return found


def pick(table, index):
    value = jnp.int32(table[0])
    for n in range(1, len(table)):
        value = jnp.where(index == n, jnp.int32(table[n]), value)
    return value


def program(row_count, col_count, grad_out, gate_act, up_act, down_weight):
    assert row_count == 2 * col_count
    row = lax.axis_index("row").astype(jnp.int32)
    col = lax.axis_index("col").astype(jnp.int32)
    core, chip = row % 2, row // 2
    bits = []
    while 2 ** (len(bits) + 1) < row_count:
        bits.append(2 ** (len(bits) + 1))
    streams = (bits, bits[::-1])
    width = down_weight.shape[0]
    block = gate_act.shape[0]
    tokens = row_count * block

    def swap(x, bit):
        pairs = [(r, r ^ bit) for r in range(row_count)]
        return jax.tree.map(lambda x: lax.ppermute(x, "row", pairs), x)

    places = []
    for order in streams:
        found = [0]
        for bit in order[::-1]:
            found = found + [f | bit // 2 for f in found]
        places.append([found.index(m) for m in range(row_count // 2)])

    ways = {"up": [grad_out], "down": [grad_out]}

    def forward(s):
        up, down = ways["up"], ways["down"]
        up.append(lax.ppermute(up[-1], "col", [(i, i + 1) for i in range(s - 1, col_count - 1)]))
        down.append(lax.ppermute(down[-1], "col", [(i, i - 1) for i in range(1, col_count - s + 1)]))

    def arrived(k):
        sources = [arrivals(z, col_count)[k - 1] for z in range(col_count)]
        value = None
        for z, (way, s, _) in enumerate(sources):
            x = ways[way][s]
            value = x if value is None else jnp.where(col == z, x, value)
        return value, pick([c for _, _, c in sources], col)

    units = width // UNIT
    edges = [units * k // CHUNKS for k in range(CHUNKS + 1)]
    terms = [(None, None)] * CHUNKS
    ordered = None

    def product(q, dy, source, deps):
        nonlocal ordered
        flip = chip ^ source
        at = jnp.stack([pick(places[q % 2], flip), core, 1 - core, flip])
        out = hidden_grad_terms(
            at, dy, down_weight, edges[q], edges[q + 1] - edges[q], terms[q], ordered, tokens, deps
        )
        terms[q] = tuple(out[:2])
        if q == 0:
            ordered = out[2]
        return out[0]

    forward(1)
    hidden = hidden_transposed(gate_act, up_act)
    held, base = {0: [hidden]}, {0: [0]}
    first_bits = bits[:2]
    for bit in first_bits + [1]:
        held[bit], base[bit] = swap([hidden], bit), [0]
    half = width // 2

    last = hidden
    early = {(1, 0): held[1]}
    dy, source = grad_out, col
    for k in range(col_count):
        for q in range(CHUNKS):
            if k == col_count - 1:
                break
            last = product(q, dy, source, [last] + early.pop((k, q), []))
        if k + 1 < col_count:
            ways["up"][k + 1], ways["down"][k + 1], last = lax.optimization_barrier(
                (ways["up"][k + 1], ways["down"][k + 1], last)
            )
            if k + 2 < col_count:
                forward(k + 2)
            dy, source = arrived(k + 1)
        if k == 1 and len(first_bits) == 2:
            a, b = first_bits
            held[a], held[b], held[1], dy, last = lax.optimization_barrier(
                (held[a], held[b], held[1], dy, last)
            )
            held[a | b] = [swap(held[a][0][:half], b), swap(held[b][0][half:], a)]
            base[a | b] = [0, half]
            both = swap(jnp.concatenate(held[a] + held[b]), 1)
            held[a | 1] = held[b | 1] = [both]
            base[a | 1], base[b | 1] = [0], [-width]
            early[k + 1, 1] = [both]

    held, last = lax.optimization_barrier((held, last))
    for bit in bits[2:]:
        for f in [f for f in held if f | bit not in held]:
            held[f | bit], base[f | bit] = swap(held[f], bit), base[f]
    ready = jax.tree.leaves(held)
    for f in [f for f in held if f | 1 not in held]:
        held[f | 1], base[f | 1] = swap(held[f], 1), base[f]

    grad_gate = grad_up = grad_down = None
    sums, stages = [None] * CHUNKS, [0] * CHUNKS
    part = width // PARTS

    def step(kind, n, last):
        nonlocal grad_gate, grad_up, grad_down
        if kind == "P":
            deps = ready if n == 0 else jax.tree.leaves(held) if n == 1 else []
            keep = product(n, dy, source, [last] + deps)
            sums[n] = [keep, swap(terms[n][1], 1)]
            return keep
        if kind == "S":
            bit = streams[n % 2][stages[n]]
            stages[n] += 1
            send = stage_sum(sums[n], (tokens // 2) >> stages[n], [last])
            sums[n] = sums[n] + [swap(send, bit)]
            return send
        if kind == "F":
            grad_gate, grad_up = finish(
                gate_act, up_act, sums[n], edges[n], edges[n + 1] - edges[n], (grad_gate, grad_up), [last]
            )
            return grad_up
        pieces = []
        for f in range(row_count):
            side = -1 if n * part >= half else 0
            pieces.append((held[f][side], base[f][side]))
        grad_down = weight_grad(pieces, ordered, grad_down, width, n * part, part, [last])
        return grad_down

    for item in PLAN:
        kind, n = item[0], int(item[1:])
        while kind == "F" and stages[n] < len(bits):
            last = step("S", n, last)
        last = step(kind, n, last)
    return grad_gate, grad_up, grad_down


def solution(mesh):
    def local(*args):
        return program(mesh.shape["row"], mesh.shape["col"], *args)

    return jax.shard_map(
        local,
        mesh=mesh,
        in_specs=(P("col", "row"), P("row", "col"), P("row", "col"), P("col", "row")),
        out_specs=(P("row", "col"), P("row", "col"), P("col", "row")),
        check_vma=False,
    )
```

time: 396 us -> 283 us (0.71)
  waiting for transfers between devices: 284 us -> 8.82 us
  Pallas kernels: 0 us -> 214 us
  matrix products: 87.1 us -> 0 us
  starting transfers between devices: 0.42 us -> 34.3 us
  between operations: 14.1 us -> 0.76 us
  other arithmetic: 9.25 us -> 16.6 us
  local copies, waits for them, and re-layouts: 0.01 us -> 5.78 us
    pallas_call x0 -> x33, Pallas kernels: none -> 214 us  [run(): pl.pallas_call(body, grid_spec=pltpu.PrefetchScalarGridSpec(num_scalar_pr...]
    all_gather x2 -> x0, waiting for transfers between devices: 157 us -> none  [the longest x1 79 us: local(): hidden = lax.all_gather(hidden, 'row', axis=0, tiled=True)]
    reduce_scatter x4 -> x0, waiting for transfers between devices: 126 us -> none  [local(): lax.psum_scatter(part, 'row', scatter_dimension=0, tiled=True).astype(f32)]
    dot_general x5 -> x0, matrix products: 87.1 us -> none  [the longest x4 51.3 us: local(): lax.dot_general(dy, down_weight[cut], (((1,), (1,)), ((), ())), preferred...]
    ppermute x0 -> x26, starting transfers between devices: none -> 34.3 us  [the longest x20 15.7 us: swap(): return jax.tree.map(lambda x: lax.ppermute(x, 'row', pairs), x)]
    ppermute x0 -> x26, waiting for transfers between devices: none -> 8.82 us  [the longest x20 8.8 us: swap(): return jax.tree.map(lambda x: lax.ppermute(x, 'row', pairs), x)]
    select_n x0 -> x3, other arithmetic: none -> 8.01 us  [arrived(): value = x if value is None else jnp.where(col == z, x, value)]
    convert_element_type x2 -> x0, other arithmetic: 7.36 us -> none  [the longest x1 4.16 us: local(): hidden = (gate * jax.nn.sigmoid(gate) * up_act.astype(f32)).astype(bf16)]
  transfers between devices with their start and end apart: 6 -> 26, of which waited for: 5 -> 2; matrix products, arithmetic and copies ran while one was open for 20% -> 6% of each run, Pallas kernels for 0% -> 66%
where the time goes in v3:
time: 283 us; the launch traced here: 280 us
  Pallas kernels  214 us (76%)
  starting transfers between devices  34.3 us (12%)
  other arithmetic  16.6 us (6%)
  waiting for transfers between devices  8.82 us (3%)
  local copies, waits for them, and re-layouts  5.78 us (2%)
    pallas_call x33, Pallas kernels, run(): pl.pallas_call(body, grid_spec=pltpu.PrefetchScalarGridSpec(num_scalar_pr...  214 us
    ppermute x20, starting transfers between devices, swap(): return jax.tree.map(lambda x: lax.ppermute(x, 'row', pairs), x)  15.7 us
    ppermute x3, starting transfers between devices, forward(): lax.ppermute(down[-1], 'col', [(i, i - 1) for i in range(1, col_count - s...  9.91 us
    ppermute x20, waiting for transfers between devices, swap(): return jax.tree.map(lambda x: lax.ppermute(x, 'row', pairs), x)  8.8 us
    ppermute x3, starting transfers between devices, forward(): lax.ppermute(up[-1], 'col', [(i, i + 1) for i in range(s - 1, col_count -...  8.67 us
    select_n x3, other arithmetic, arrived(): value = x if value is None else jnp.where(col == z, x, value)  8.01 us
  transfers between devices with their start and end apart: 26, of which 2 were waited for; matrix products, arithmetic and copies ran while one was open for 6% of the time, Pallas kernels for 66%

profile of v3, /device:TPU:16, one launch (start us, length us, event | category | flops | bytes accessed | tf_op | source)
XLA Modules:
  0.0 280.4 jit_solution(460811024247407502)
XLA Ops:
  0.6 4.4 %hidden.1.refs_4_.refs_8_.refs_7_.refs_0_ = bf16[6656,128]{1,0:T(8,128)(2,1)} custom-call(bf16[128,6656]{1,0:T(8,128)(2,1)} %refs_0_.9, bf16[128,6656]{1,0:T(8,128)(2,1)} %refs_1_.17), custom_call_target="tpu_custom_call" | custom-call | bytes 3407872 | tf_op jit(solution)/shard_map/hidden/pallas_call | solution.py:36
  5.0 2.3 collective-permute-start.1
  7.4 4.5 %collective-permute-start = (bf16[256,2048]{1,0:T(8,128)(2,1)}, bf16[256,2048]{1,0:T(8,128)(2,1)}, u32[]{:S(2)}, u32[]{:S(2)}) collective-permute-start(bf16[256,2048]{1,0:T(8,128)(2,1)} %refs_2_.7), channel_id=1, source_target_pairs={{0,1},{1,2},{2,3},{4,5},{5,6},{6,7},{8,9},{9,10},{10,11},{12,13},{... | collective-permute-start | bytes 3145736 | tf_op jit(solution)/shard_map/ppermute | solution.py:186
  11.9 1.6 collective-permute-start.8
  16.2 7.8 %hidden_grad_terms.16 = (f32[512,1536]{1,0:T(8,128)}, bf16[512,1536]{1,0:T(8,128)(2,1)}, bf16[1024,2048]{1,0:T(8,128)(2,1)}) custom-call(s32[4]{0:T(128)} %get-tuple-element.138.refs_0_, bf16[256,2048]{1,0:T(8,128)(2,1)} %refs_2_.7, bf16[256,2048]{1,0:T(8,128)(2,1)} %refs_2_.7, bf16[6656,2048]{1,0:T(8,128)(2,1)} %refs_3_.31, ...), custom_call_target="tpu_custom_call" | custom-call | flops 1610612736 | bytes 29360128 | tf_op jit(solution)/shard_map/hidden_grad_terms/pallas_call | solution.py:36
  24.0 8.7 %hidden_grad_terms.17 = (f32[512,1792]{1,0:T(8,128)}, bf16[512,1792]{1,0:T(8,128)(2,1)}) custom-call(s32[4]{0:T(128)} %get-tuple-element.137.refs_0_, bf16[256,2048]{1,0:T(8,128)(2,1)} %refs_2_.7, bf16[256,2048]{1,0:T(8,128)(2,1)} %refs_2_.7, bf16[6656,2048]{1,0:T(8,128)(2,1)} %refs_3_.31, f32[512,1536]{1,0:T(8,128)} %get-tuple-element.70.refs_4_), custom_call_target="tpu_custom_call" | custom-call | flops 1879048192 | bytes 29360128 | tf_op jit(solution)/shard_map/hidden_grad_terms/pallas_call | solution.py:36
  32.7 7.6 %hidden_grad_terms.18 = (f32[512,1536]{1,0:T(8,128)}, bf16[512,1536]{1,0:T(8,128)(2,1)}) custom-call(s32[4]{0:T(128)} %get-tuple-element.138.refs_0_, bf16[256,2048]{1,0:T(8,128)(2,1)} %refs_2_.7, bf16[256,2048]{1,0:T(8,128)(2,1)} %refs_2_.7, bf16[6656,2048]{1,0:T(8,128)(2,1)} %refs_3_.31, f32[512,1792]{1,0:T(8,128)} %get-tuple-element.71.refs_4_), custom_call_target="tpu_custom_call" | custom-call | flops 1610612736 | bytes 29360128 | tf_op jit(solution)/shard_map/hidden_grad_terms/pallas_call | solution.py:36
  40.3 8.7 %hidden_grad_terms.19 = (f32[512,1792]{1,0:T(8,128)}, bf16[512,1792]{1,0:T(8,128)(2,1)}) custom-call(s32[4]{0:T(128)} %get-tuple-element.137.refs_0_, bf16[256,2048]{1,0:T(8,128)(2,1)} %refs_2_.7, bf16[256,2048]{1,0:T(8,128)(2,1)} %refs_2_.7, bf16[6656,2048]{1,0:T(8,128)(2,1)} %refs_3_.31, f32[512,1536]{1,0:T(8,128)} %get-tuple-element.72.refs_4_), custom_call_target="tpu_custom_call" | custom-call | flops 1879048192 | bytes 29360128 | tf_op jit(solution)/shard_map/hidden_grad_terms/pallas_call | solution.py:36
  49.0 1.9 collective-permute-start.2
  51.0 5.9 %collective-permute-start.3 = (bf16[256,2048]{1,0:T(8,128)(2,1)}, bf16[256,2048]{1,0:T(8,128)(2,1)}, u32[]{:S(2)}, u32[]{:S(2)}) collective-permute-start(bf16[256,2048]{1,0:T(8,128)(2,1)} %collective-permute-done.1), channel_id=1, source_target_pairs={{1,0},{2,1},{5,4},{6,5},{9,8},{10,9},{13,12},{14,13},{17,16},{18,1... | collective-permute-start | bytes 3145736 | tf_op jit(solution)/shard_map/ppermute | solution.py:187
  56.9 2.6 select_select_fusion.1.refs_1_.refs_2_
  59.5 7.8 %hidden_grad_terms.20 = (f32[512,1536]{1,0:T(8,128)}, bf16[512,1536]{1,0:T(8,128)(2,1)}, bf16[1024,2048]{1,0:T(8,128)(2,1)}) custom-call(s32[4]{0:T(128)} %get-tuple-element.140.refs_0_, bf16[256,2048]{1,0:T(8,128)(2,1)} %select_select_fusion.1.refs_1_.refs_2_, ...), custom_call_target="tpu_custom_call", output_to_operand_aliasing={{0}: (4, {}), {1}: (5, {}), {2}: (6, {})} | custom-call | flops 1610612736 | bytes 29360128 | tf_op jit(solution)/shard_map/hidden_grad_terms/pallas_call | solution.py:36
  67.3 8.7 %hidden_grad_terms.21 = (f32[512,1792]{1,0:T(8,128)}, bf16[512,1792]{1,0:T(8,128)(2,1)}) custom-call(s32[4]{0:T(128)} %get-tuple-element.139.refs_0_, bf16[256,2048]{1,0:T(8,128)(2,1)} %select_select_fusion.1.refs_1_.refs_2_, bf16[256,2048]{1,0:T(8,128)(2,1)} %select_select_fusion.1.refs_1_.refs_2_, ...), custom_call_target="tpu_custom_call", output_to_operand_aliasing={{0}: (4, {}), {1}: (5, {})} | custom-call | flops 1879048192 | bytes 29360128 | tf_op jit(solution)/shard_map/hidden_grad_terms/pallas_call | solution.py:36
  76.0 7.7 %hidden_grad_terms.22 = (f32[512,1536]{1,0:T(8,128)}, bf16[512,1536]{1,0:T(8,128)(2,1)}) custom-call(s32[4]{0:T(128)} %get-tuple-element.140.refs_0_, bf16[256,2048]{1,0:T(8,128)(2,1)} %select_select_fusion.1.refs_1_.refs_2_, bf16[256,2048]{1,0:T(8,128)(2,1)} %select_select_fusion.1.refs_1_.refs_2_, ...), custom_call_target="tpu_custom_call", output_to_operand_aliasing={{0}: (4, {}), {1}: (5, {})} | custom-call | flops 1610612736 | bytes 29360128 | tf_op jit(solution)/shard_map/hidden_grad_terms/pallas_call | solution.py:36
  83.7 8.7 %hidden_grad_terms.23 = (f32[512,1792]{1,0:T(8,128)}, bf16[512,1792]{1,0:T(8,128)(2,1)}) custom-call(s32[4]{0:T(128)} %get-tuple-element.139.refs_0_, bf16[256,2048]{1,0:T(8,128)(2,1)} %select_select_fusion.1.refs_1_.refs_2_, bf16[256,2048]{1,0:T(8,128)(2,1)} %select_select_fusion.1.refs_1_.refs_2_, ...), custom_call_target="tpu_custom_call", output_to_operand_aliasing={{0}: (4, {}), {1}: (5, {})} | custom-call | flops 1879048192 | bytes 29360128 | tf_op jit(solution)/shard_map/hidden_grad_terms/pallas_call | solution.py:36
  92.3 2.7 fusion.refs_1_.refs_2_
  95.0 4.9 %pad_maximum_fusion = bf16[13312,128]{1,0:T(8,128)(2,1)} fusion(bf16[6656,128]{1,0:T(8,128)(2,1)} %collective-permute-done.8.refs_12_.refs_11_.refs_4_, bf16[6656,128]{1,0:T(8,128)(2,1)} %collective-permute-done.7.refs_10_.refs_9_.refs_2_), kind=kLoop, calls=%fused_computation | loop fusion | flops 6815744 | bytes 6815744 | tf_op jit(solution)/shard_map/concatenate | solution.py:244
  99.9 2.3 collective-permute-start.5
  102.2 1.7 collective-permute-start.6
  103.9 2.1 slice.6
  106.0 2.1 slice.7
  110.3 7.8 %hidden_grad_terms.24 = (f32[512,1536]{1,0:T(8,128)}, bf16[512,1536]{1,0:T(8,128)(2,1)}, bf16[1024,2048]{1,0:T(8,128)(2,1)}) custom-call(s32[4]{0:T(128)} %add_add_fusion.6.refs_0_, bf16[256,2048]{1,0:T(8,128)(2,1)} %fusion.refs_1_.refs_2_, bf16[256,2048]{1,0:T(8,128)(2,1)} %fusion.refs_1_.refs_2_, ...), custom_call_target="tpu_custom_call", output_to_operand_aliasing={{0}: (4, {}), {1}: (5, {}), {2}: (6, {})} | custom-call | flops 1610612736 | bytes 29360128 | tf_op jit(solution)/shard_map/hidden_grad_terms/pallas_call | solution.py:36
  118.1 8.7 %hidden_grad_terms.25 = (f32[512,1792]{1,0:T(8,128)}, bf16[512,1792]{1,0:T(8,128)(2,1)}) custom-call(s32[4]{0:T(128)} %add_add_fusion.5.refs_0_, bf16[256,2048]{1,0:T(8,128)(2,1)} %fusion.refs_1_.refs_2_, bf16[256,2048]{1,0:T(8,128)(2,1)} %fusion.refs_1_.refs_2_, bf16[6656,2048]{1,0:T(8,128)(2,1)} %refs_3_.31, ...), custom_call_target="tpu_custom_call", output_to_operand_aliasing={{0}: (4, {}), {1}: (5, {})} | custom-call | flops 1879048192 | bytes 29360128 | tf_op jit(solution)/shard_map/hidden_grad_terms/pallas_call | solution.py:36
  126.8 7.6 %hidden_grad_terms.26 = (f32[512,1536]{1,0:T(8,128)}, bf16[512,1536]{1,0:T(8,128)(2,1)}) custom-call(s32[4]{0:T(128)} %add_add_fusion.6.refs_0_, bf16[256,2048]{1,0:T(8,128)(2,1)} %fusion.refs_1_.refs_2_, bf16[256,2048]{1,0:T(8,128)(2,1)} %fusion.refs_1_.refs_2_, bf16[6656,2048]{1,0:T(8,128)(2,1)} %refs_3_.31, ...), custom_call_target="tpu_custom_call", output_to_operand_aliasing={{0}: (4, {}), {1}: (5, {})} | custom-call | flops 1610612736 | bytes 29360128 | tf_op jit(solution)/shard_map/hidden_grad_terms/pallas_call | solution.py:36
  134.4 8.7 %hidden_grad_terms.27 = (f32[512,1792]{1,0:T(8,128)}, bf16[512,1792]{1,0:T(8,128)(2,1)}) custom-call(s32[4]{0:T(128)} %add_add_fusion.5.refs_0_, bf16[256,2048]{1,0:T(8,128)(2,1)} %fusion.refs_1_.refs_2_, bf16[256,2048]{1,0:T(8,128)(2,1)} %fusion.refs_1_.refs_2_, bf16[6656,2048]{1,0:T(8,128)(2,1)} %refs_3_.31, ...), custom_call_target="tpu_custom_call", output_to_operand_aliasing={{0}: (4, {}), {1}: (5, {})} | custom-call | flops 1879048192 | bytes 29360128 | tf_op jit(solution)/shard_map/hidden_grad_terms/pallas_call | solution.py:36
  145.0 2.7 select_select_fusion.2.refs_1_.refs_2_
  147.7 7.8 %hidden_grad_terms.28 = (f32[512,1536]{1,0:T(8,128)}, bf16[512,1536]{1,0:T(8,128)(2,1)}, bf16[1024,2048]{1,0:T(8,128)(2,1)}) custom-call(s32[4]{0:T(128)} %add_add_fusion.7.refs_0_, bf16[256,2048]{1,0:T(8,128)(2,1)} %select_select_fusion.2.refs_1_.refs_2_, ...), custom_call_target="tpu_custom_call", output_to_operand_aliasing={{0}: (4, {}), {1}: (5, {}), {2}: (6, {})} | custom-call | flops 1610612736 | bytes 29360128 | tf_op jit(solution)/shard_map/hidden_grad_terms/pallas_call | solution.py:36
  155.6 8.7 %hidden_grad_terms.29 = (f32[512,1792]{1,0:T(8,128)}, bf16[512,1792]{1,0:T(8,128)(2,1)}) custom-call(s32[4]{0:T(128)} %add_add_fusion.refs_0_, bf16[256,2048]{1,0:T(8,128)(2,1)} %select_select_fusion.2.refs_1_.refs_2_, bf16[256,2048]{1,0:T(8,128)(2,1)} %select_select_fusion.2.refs_1_.refs_2_, ...), custom_call_target="tpu_custom_call", output_to_operand_aliasing={{0}: (4, {}), {1}: (5, {})} | custom-call | flops 1879048192 | bytes 29360128 | tf_op jit(solution)/shard_map/hidden_grad_terms/pallas_call | solution.py:36
  164.8 5.9 %collective-permute-done.15.refs_1_.refs_3_ = bf16[512,1536]{1,0:T(8,128)(2,1)} collective-permute-done((bf16[512,1536]{1,0:T(8,128)(2,1)}, bf16[512,1536]{1,0:T(8,128)(2,1)}, u32[]{:S(2)}, u32[]{:S(2)}) %collective-permute-start.15) | collective-permute-done | bytes 1572896 | tf_op jit(solution)/shard_map/ppermute | solution.py:173
  170.6 2.4 stage_sum.8.refs_6_
  173.0 7.6 %hidden_grad_terms.30 = (f32[512,1536]{1,0:T(8,128)}, bf16[512,1536]{1,0:T(8,128)(2,1)}) custom-call(s32[4]{0:T(128)} %add_add_fusion.7.refs_0_, bf16[256,2048]{1,0:T(8,128)(2,1)} %select_select_fusion.2.refs_1_.refs_2_, bf16[256,2048]{1,0:T(8,128)(2,1)} %select_select_fusion.2.refs_1_.refs_2_, ...), custom_call_target="tpu_custom_call", output_to_operand_aliasing={{0}: (4, {}), {1}: (5, {})} | custom-call | flops 1610612736 | bytes 29360128 | tf_op jit(solution)/shard_map/hidden_grad_terms/pallas_call | solution.py:36
  180.6 2.6 stage_sum.9.refs_6_
  183.2 8.8 %hidden_grad_terms.31 = (f32[512,1792]{1,0:T(8,128)}, bf16[512,1792]{1,0:T(8,128)(2,1)}) custom-call(s32[4]{0:T(128)} %add_add_fusion.refs_0_, bf16[256,2048]{1,0:T(8,128)(2,1)} %select_select_fusion.2.refs_1_.refs_2_, bf16[256,2048]{1,0:T(8,128)(2,1)} %select_select_fusion.2.refs_1_.refs_2_, ...), custom_call_target="tpu_custom_call", output_to_operand_aliasing={{0}: (4, {}), {1}: (5, {})} | custom-call | flops 1879048192 | bytes 29360128 | tf_op jit(solution)/shard_map/hidden_grad_terms/pallas_call | solution.py:36
  195.5 2.9 %collective-permute-done.17.refs_1_.refs_3_ = bf16[512,1536]{1,0:T(8,128)(2,1)} collective-permute-done((bf16[512,1536]{1,0:T(8,128)(2,1)}, bf16[512,1536]{1,0:T(8,128)(2,1)}, u32[]{:S(2)}, u32[]{:S(2)}) %collective-permute-start.17) | collective-permute-done | bytes 1572896 | tf_op jit(solution)/shard_map/ppermute | solution.py:173
  198.4 2.4 stage_sum.10.refs_2_
  202.3 2.6 stage_sum.11.refs_9_
  206.4 11.7 %weight_grad.4.refs_9_ = bf16[6656,2048]{1,0:T(8,128)(2,1)} custom-call(bf16[6656,128]{1,0:T(8,128)(2,1)} %hidden.1.refs_4_.refs_8_.refs_7_.refs_0_, bf16[6656,128]{1,0:T(8,128)(2,1)} %collective-permute-done.4.refs_8_.refs_9_.refs_1_, bf16[6656,128]{1,0:T(8,128)(2,1)} %collective-permute-done.7.refs_10_.refs_9_.refs_2_, ...), custom_call_target="tpu_custom_call" | custom-call | flops 6979321856 | bytes 19529728 | tf_op jit(solution)/shard_map/weight_grad/pallas_call | solution.py:36
  218.1 11.8 %weight_grad.5.refs_3_.refs_9_ = bf16[6656,2048]{1,0:T(8,128)(2,1)} custom-call(bf16[6656,128]{1,0:T(8,128)(2,1)} %hidden.1.refs_4_.refs_8_.refs_7_.refs_0_, bf16[6656,128]{1,0:T(8,128)(2,1)} %collective-permute-done.4.refs_8_.refs_9_.refs_1_, bf16[6656,128]{1,0:T(8,128)(2,1)} %collective-permute-done.7.refs_10_.refs_9_.refs_2_, ...), custom_call_target="tpu_custom_call", output_to_operand_aliasing={{}: (9, {})} | custom-call | flops 6979321856 | bytes 19529728 | tf_op jit(solution)/shard_map/weight_grad/pallas_call | solution.py:36
  229.9 2.2 stage_sum.12.refs_3_
  232.5 2.2 stage_sum.13.refs_10_
  235.3 11.8 %weight_grad.6.refs_3_.refs_9_ = bf16[6656,2048]{1,0:T(8,128)(2,1)} custom-call(bf16[6656,128]{1,0:T(8,128)(2,1)} %hidden.1.refs_4_.refs_8_.refs_7_.refs_0_, bf16[6656,128]{1,0:T(8,128)(2,1)} %collective-permute-done.4.refs_8_.refs_9_.refs_1_, bf16[6656,128]{1,0:T(8,128)(2,1)} %collective-permute-done.7.refs_10_.refs_9_.refs_2_, ...), custom_call_target="tpu_custom_call", output_to_operand_aliasing={{}: (9, {})} | custom-call | flops 6979321856 | bytes 19529728 | tf_op jit(solution)/shard_map/weight_grad/pallas_call | solution.py:36
  247.1 2.1 stage_sum.14.refs_3_
  250.8 2.3 stage_sum.15.refs_10_
  254.5 11.8 %weight_grad.7.refs_6_ = bf16[6656,2048]{1,0:T(8,128)(2,1)} custom-call(bf16[6656,128]{1,0:T(8,128)(2,1)} %hidden.1.refs_4_.refs_8_.refs_7_.refs_0_, bf16[6656,128]{1,0:T(8,128)(2,1)} %collective-permute-done.4.refs_8_.refs_9_.refs_1_, bf16[6656,128]{1,0:T(8,128)(2,1)} %collective-permute-done.7.refs_10_.refs_9_.refs_2_, ...), custom_call_target="tpu_custom_call", output_to_operand_aliasing={{}: (9, {})} | custom-call | flops 6979321856 | bytes 19529728 | tf_op jit(solution)/shard_map/weight_grad/pallas_call | solution.py:36
  266.3 3.0 %finish.4 = (bf16[128,6656]{1,0:T(8,128)(2,1)}, bf16[128,6656]{1,0:T(8,128)(2,1)}) custom-call(bf16[128,6656]{1,0:T(8,128)(2,1)} %refs_0_.9, bf16[128,6656]{1,0:T(8,128)(2,1)} %refs_1_.17, f32[512,1536]{1,0:T(8,128)} %get-tuple-element.119.refs_6_.refs_0_.refs_2_, bf16[512,1536]{1,0:T(8,128)(2,1)} %collective-permute-done.15.refs_1_.refs_3_, ...), custom_call_target="tpu_custom_call" | custom-call | bytes 9306112 | tf_op jit(solution)/shard_map/finish/pallas_call | solution.py:36
  270.1 3.3 %finish.5 = (bf16[128,6656]{1,0:T(8,128)(2,1)}, bf16[128,6656]{1,0:T(8,128)(2,1)}) custom-call(bf16[128,6656]{1,0:T(8,128)(2,1)} %refs_0_.9, bf16[128,6656]{1,0:T(8,128)(2,1)} %refs_1_.17, f32[512,1792]{1,0:T(8,128)} %get-tuple-element.120.refs_2_.refs_0_, ...), custom_call_target="tpu_custom_call", output_to_operand_aliasing={{0}: (6, {}), {1}: (7, {})} | custom-call | bytes 10289152 | tf_op jit(solution)/shard_map/finish/pallas_call | solution.py:36
  273.4 3.0 %finish.6 = (bf16[128,6656]{1,0:T(8,128)(2,1)}, bf16[128,6656]{1,0:T(8,128)(2,1)}) custom-call(bf16[128,6656]{1,0:T(8,128)(2,1)} %refs_0_.9, bf16[128,6656]{1,0:T(8,128)(2,1)} %refs_1_.17, f32[512,1536]{1,0:T(8,128)} %get-tuple-element.124.refs_2_.refs_0_, ...), custom_call_target="tpu_custom_call", output_to_operand_aliasing={{0}: (6, {}), {1}: (7, {})} | custom-call | bytes 9306112 | tf_op jit(solution)/shard_map/finish/pallas_call | solution.py:36
  277.2 3.3 %finish.7 = (bf16[128,6656]{1,0:T(8,128)(2,1)}, bf16[128,6656]{1,0:T(8,128)(2,1)}) custom-call(bf16[128,6656]{1,0:T(8,128)(2,1)} %refs_0_.9, bf16[128,6656]{1,0:T(8,128)(2,1)} %refs_1_.17, f32[512,1792]{1,0:T(8,128)} %get-tuple-element.125.refs_2_.refs_0_, ...), custom_call_target="tpu_custom_call", output_to_operand_aliasing={{0}: (6, {}), {1}: (7, {})} | custom-call | bytes 10289152 | tf_op jit(solution)/shard_map/finish/pallas_call | solution.py:36
  (57 shorter events, 19.5 us)
Async XLA Ops:
  5.0 54.4 %collective-permute-start.4 = (bf16[6656,128]{1,0:T(8,128)(2,1)}, bf16[6656,128]{1,0:T(8,128)(2,1)}, u32[]{:S(2)}, u32[]{:S(2)}) collective-permute-start(bf16[6656,128]{1,0:T(8,128)(2,1)} %hidden.1.refs_4_.refs_8_.refs_7_.refs_0_), channel_id=1, source_target_pairs={{0,4},{4,0},{8,12},{12,8},{16,20},{20,16},{24,28},{28,24},{1,5},{5... | collective-permute-start | bytes 5111816 | tf_op jit(solution)/shard_map/ppermute | solution.py:173
  5.0 44.0 %collective-permute-start.1 = (bf16[256,2048]{1,0:T(8,128)(2,1)}, bf16[256,2048]{1,0:T(8,128)(2,1)}, u32[]{:S(2)}, u32[]{:S(2)}) collective-permute-start(bf16[256,2048]{1,0:T(8,128)(2,1)} %refs_2_.7), channel_id=1, source_target_pairs={{1,0},{2,1},{3,2},{5,4},{6,5},{7,6},{9,8},{10,9},{11,10},{13,12},{... | collective-permute-start | bytes 3145736 | tf_op jit(solution)/shard_map/ppermute | solution.py:187
  7.4 41.6 %collective-permute-start = (bf16[256,2048]{1,0:T(8,128)(2,1)}, bf16[256,2048]{1,0:T(8,128)(2,1)}, u32[]{:S(2)}, u32[]{:S(2)}) collective-permute-start(bf16[256,2048]{1,0:T(8,128)(2,1)} %refs_2_.7), channel_id=1, source_target_pairs={{0,1},{1,2},{2,3},{4,5},{5,6},{6,7},{8,9},{9,10},{10,11},{12,13},{... | collective-permute-start | bytes 3145736 | tf_op jit(solution)/shard_map/ppermute | solution.py:186
  11.9 83.2 %collective-permute-start.8 = (bf16[6656,128]{1,0:T(8,128)(2,1)}, bf16[6656,128]{1,0:T(8,128)(2,1)}, u32[]{:S(2)}, u32[]{:S(2)}) collective-permute-start(bf16[6656,128]{1,0:T(8,128)(2,1)} %hidden.1.refs_4_.refs_8_.refs_7_.refs_0_), channel_id=1, source_target_pairs={{0,16},{4,20},{8,24},{12,28},{16,0},{20,4},{24,8},{28,12},{1,17},{... | collective-permute-start | bytes 5111816 | tf_op jit(solution)/shard_map/ppermute | solution.py:173
  13.5 81.6 %collective-permute-start.7 = (bf16[6656,128]{1,0:T(8,128)(2,1)}, bf16[6656,128]{1,0:T(8,128)(2,1)}, u32[]{:S(2)}, u32[]{:S(2)}) collective-permute-start(bf16[6656,128]{1,0:T(8,128)(2,1)} %hidden.1.refs_4_.refs_8_.refs_7_.refs_0_), channel_id=1, source_target_pairs={{0,8},{4,12},{8,0},{12,4},{16,24},{20,28},{24,16},{28,20},{1,9},{5... | collective-permute-start | bytes 5111816 | tf_op jit(solution)/shard_map/ppermute | solution.py:173
  49.0 43.3 %collective-permute-start.2 = (bf16[256,2048]{1,0:T(8,128)(2,1)}, bf16[256,2048]{1,0:T(8,128)(2,1)}, u32[]{:S(2)}, u32[]{:S(2)}) collective-permute-start(bf16[256,2048]{1,0:T(8,128)(2,1)} %collective-permute-done), channel_id=1, source_target_pairs={{1,2},{2,3},{5,6},{6,7},{9,10},{10,11},{13,14},{14,15},{17,18},{18... | collective-permute-start | bytes 3145736 | tf_op jit(solution)/shard_map/ppermute | solution.py:186
  51.0 41.4 %collective-permute-start.3 = (bf16[256,2048]{1,0:T(8,128)(2,1)}, bf16[256,2048]{1,0:T(8,128)(2,1)}, u32[]{:S(2)}, u32[]{:S(2)}) collective-permute-start(bf16[256,2048]{1,0:T(8,128)(2,1)} %collective-permute-done.1), channel_id=1, source_target_pairs={{1,0},{2,1},{5,4},{6,5},{9,8},{10,9},{13,12},{14,13},{17,16},{18,1... | collective-permute-start | bytes 3145736 | tf_op jit(solution)/shard_map/ppermute | solution.py:187
  99.9 18.2 %collective-permute-start.9 = (bf16[13312,128]{1,0:T(8,128)(2,1)}, bf16[13312,128]{1,0:T(8,128)(2,1)}, u32[]{:S(2)}, u32[]{:S(2)}) collective-permute-start(bf16[13312,128]{1,0:T(8,128)(2,1)} %pad_maximum_fusion), channel_id=1, source_target_pairs={{0,4},{4,0},{8,12},{12,8},{16,20},{20,16},{24,28},{28,24},{1,5},{5... | collective-permute-start | bytes 10223624 | tf_op jit(solution)/shard_map/ppermute | solution.py:173
  99.9 43.3 %collective-permute-start.5 = (bf16[256,2048]{1,0:T(8,128)(2,1)}, bf16[256,2048]{1,0:T(8,128)(2,1)}, u32[]{:S(2)}, u32[]{:S(2)}) collective-permute-start(bf16[256,2048]{1,0:T(8,128)(2,1)} %collective-permute-done.2), channel_id=1, source_target_pairs={{2,3},{6,7},{10,11},{14,15},{18,19},{22,23},{26,27},{30,31}} | collective-permute-start | bytes 3145736 | tf_op jit(solution)/shard_map/ppermute | solution.py:186
  102.2 41.0 %collective-permute-start.6 = (bf16[256,2048]{1,0:T(8,128)(2,1)}, bf16[256,2048]{1,0:T(8,128)(2,1)}, u32[]{:S(2)}, u32[]{:S(2)}) collective-permute-start(bf16[256,2048]{1,0:T(8,128)(2,1)} %collective-permute-done.3), channel_id=1, source_target_pairs={{1,0},{5,4},{9,8},{13,12},{17,16},{21,20},{25,24},{29,28}} | collective-permute-start | bytes 3145736 | tf_op jit(solution)/shard_map/ppermute | solution.py:187
  108.1 35.1 %collective-permute-start.11 = (bf16[3328,128]{1,0:T(8,128)(2,1)}, bf16[3328,128]{1,0:T(8,128)(2,1)}, u32[]{:S(2)}, u32[]{:S(2)}) collective-permute-start(bf16[3328,128]{1,0:T(8,128)(2,1)} %slice.7), channel_id=1, source_target_pairs={{0,8},{4,12},{8,0},{12,4},{16,24},{20,28},{24,16},{28,20},{1,9},{5... | collective-permute-start | bytes 2555912 | tf_op jit(solution)/shard_map/ppermute | solution.py:173
  108.6 34.6 %collective-permute-start.10 = (bf16[3328,128]{1,0:T(8,128)(2,1)}, bf16[3328,128]{1,0:T(8,128)(2,1)S(1)}, u32[]{:S(2)}, u32[]{:S(2)}) collective-permute-start(bf16[3328,128]{1,0:T(8,128)(2,1)} %slice.6), channel_id=1, source_target_pairs={{0,16},{4,20},{8,24},{12,28},{16,0},{20,4},{24,8},{28,12},{1,17},{... | collective-permute-start | bytes 2555912 | tf_op jit(solution)/shard_map/ppermute | solution.py:173
  143.2 4.5 %copy-start = (bf16[3328,128]{1,0:T(8,128)(2,1)}, bf16[3328,128]{1,0:T(8,128)(2,1)S(1)}, u32[]{:S(2)}) copy-start(bf16[3328,128]{1,0:T(8,128)(2,1)S(1)} %collective-permute-done.10.refs_14_.refs_13_.refs_6_) | copy-start | bytes 2555908
  143.2 12.3 %collective-permute-start.12 = (bf16[3328,128]{1,0:T(8,128)(2,1)S(1)}, bf16[3328,128]{1,0:T(8,128)(2,1)}, u32[]{:S(2)}, u32[]{:S(2)}) collective-permute-start(bf16[3328,128]{1,0:T(8,128)(2,1)S(1)} %collective-permute-done.10.refs_14_.refs_13_.refs_6_), channel_id=1, source_target_pairs={{0,4},{4,0},{8,12},{12,8},{16,20},{20,16},{24,28},{28,24},{1,5},{5... | collective-permute-start | bytes 2555912 | tf_op jit(solution)/shard_map/ppermute | solution.py:173
  143.3 12.2 %collective-permute-start.13 = (bf16[3328,128]{1,0:T(8,128)(2,1)}, bf16[3328,128]{1,0:T(8,128)(2,1)}, u32[]{:S(2)}, u32[]{:S(2)}) collective-permute-start(bf16[3328,128]{1,0:T(8,128)(2,1)} %collective-permute-done.11.refs_15_.refs_14_.refs_6_), channel_id=1, source_target_pairs={{0,4},{4,0},{8,12},{12,8},{16,20},{20,16},{24,28},{28,24},{1,5},{5... | collective-permute-start | bytes 2555912 | tf_op jit(solution)/shard_map/ppermute | solution.py:173
  164.3 16.4 %collective-permute-start.14 = (bf16[512,1792]{1,0:T(8,128)(2,1)}, bf16[512,1792]{1,0:T(8,128)(2,1)}, u32[]{:S(2)}, u32[]{:S(2)}) collective-permute-start(bf16[512,1792]{1,0:T(8,128)(2,1)} %get-tuple-element.121), channel_id=1, source_target_pairs={{0,4},{4,0},{8,12},{12,8},{16,20},{20,16},{24,28},{28,24},{1,5},{5... | collective-permute-start | bytes 5505032 | tf_op jit(solution)/shard_map/ppermute | solution.py:173
  164.3 6.3 %collective-permute-start.15 = (bf16[512,1536]{1,0:T(8,128)(2,1)}, bf16[512,1536]{1,0:T(8,128)(2,1)}, u32[]{:S(2)}, u32[]{:S(2)}) collective-permute-start(bf16[512,1536]{1,0:T(8,128)(2,1)} %get-tuple-element.123), channel_id=1, source_target_pairs={{0,4},{4,0},{8,12},{12,8},{16,20},{20,16},{24,28},{28,24},{1,5},{5... | collective-permute-start | bytes 4718600 | tf_op jit(solution)/shard_map/ppermute | solution.py:173
  183.2 10.8 %copy-start.1 = (bf16[256,1792]{1,0:T(8,128)(2,1)S(1)}, bf16[256,1792]{1,0:T(8,128)(2,1)}, u32[]{:S(2)}) copy-start(bf16[256,1792]{1,0:T(8,128)(2,1)} %stage_sum.9.refs_6_) | copy-start | bytes 2752516
  192.0 10.3 %collective-permute-start.16 = (bf16[512,1792]{1,0:T(8,128)(2,1)}, bf16[512,1792]{1,0:T(8,128)(2,1)}, u32[]{:S(2)}, u32[]{:S(2)}) collective-permute-start(bf16[512,1792]{1,0:T(8,128)(2,1)} %get-tuple-element.126), channel_id=1, source_target_pairs={{0,4},{4,0},{8,12},{12,8},{16,20},{20,16},{24,28},{28,24},{1,5},{5... | collective-permute-start | bytes 5505032 | tf_op jit(solution)/shard_map/ppermute | solution.py:173
  192.2 6.2 %collective-permute-start.17 = (bf16[512,1536]{1,0:T(8,128)(2,1)}, bf16[512,1536]{1,0:T(8,128)(2,1)}, u32[]{:S(2)}, u32[]{:S(2)}) collective-permute-start(bf16[512,1536]{1,0:T(8,128)(2,1)} %get-tuple-element.127), channel_id=1, source_target_pairs={{0,4},{4,0},{8,12},{12,8},{16,20},{20,16},{24,28},{28,24},{1,5},{5... | collective-permute-start | bytes 4718600 | tf_op jit(solution)/shard_map/ppermute | solution.py:173
  192.5 37.3 %collective-permute-start.21 = (bf16[256,1536]{1,0:T(8,128)(2,1)}, bf16[256,1536]{1,0:T(8,128)(2,1)}, u32[]{:S(2)}, u32[]{:S(2)}) collective-permute-start(bf16[256,1536]{1,0:T(8,128)(2,1)} %stage_sum.8.refs_6_), channel_id=1, source_target_pairs={{0,8},{4,12},{8,0},{12,4},{16,24},{20,28},{24,16},{28,20},{1,9},{5... | collective-permute-start | bytes 2359304 | tf_op jit(solution)/shard_map/ppermute | solution.py:173
  194.0 38.6 %collective-permute-start.20 = (bf16[256,1792]{1,0:T(8,128)(2,1)S(1)}, bf16[256,1792]{1,0:T(8,128)(2,1)}, u32[]{:S(2)}, u32[]{:S(2)}) collective-permute-start(bf16[256,1792]{1,0:T(8,128)(2,1)S(1)} %copy-done.1), channel_id=1, source_target_pairs={{0,16},{4,20},{8,24},{12,28},{16,0},{20,4},{24,8},{28,12},{1,17},{... | collective-permute-start | bytes 2752520 | tf_op jit(solution)/shard_map/ppermute | solution.py:173
  200.8 46.3 %collective-permute-start.19 = (bf16[256,1536]{1,0:T(8,128)(2,1)}, bf16[256,1536]{1,0:T(8,128)(2,1)}, u32[]{:S(2)}, u32[]{:S(2)}) collective-permute-start(bf16[256,1536]{1,0:T(8,128)(2,1)} %stage_sum.10.refs_2_), channel_id=1, source_target_pairs={{0,8},{4,12},{8,0},{12,4},{16,24},{20,28},{24,16},{28,20},{1,9},{5... | collective-permute-start | bytes 2359304 | tf_op jit(solution)/shard_map/ppermute | solution.py:173
  204.9 45.9 %collective-permute-start.18 = (bf16[256,1792]{1,0:T(8,128)(2,1)}, bf16[256,1792]{1,0:T(8,128)(2,1)}, u32[]{:S(2)}, u32[]{:S(2)}) collective-permute-start(bf16[256,1792]{1,0:T(8,128)(2,1)} %stage_sum.11.refs_9_), channel_id=1, source_target_pairs={{0,16},{4,20},{8,24},{12,28},{16,0},{20,4},{24,8},{28,12},{1,17},{... | collective-permute-start | bytes 2752520 | tf_op jit(solution)/shard_map/ppermute | solution.py:173
  232.0 34.2 %collective-permute-start.25 = (bf16[128,1536]{1,0:T(8,128)(2,1)}, bf16[128,1536]{1,0:T(8,128)(2,1)}, u32[]{:S(2)}, u32[]{:S(2)}) collective-permute-start(bf16[128,1536]{1,0:T(8,128)(2,1)} %stage_sum.12.refs_3_), channel_id=1, source_target_pairs={{0,16},{4,20},{8,24},{12,28},{16,0},{20,4},{24,8},{28,12},{1,17},{... | collective-permute-start | bytes 1179656 | tf_op jit(solution)/shard_map/ppermute | solution.py:173
  234.8 34.5 %collective-permute-start.24 = (bf16[128,1792]{1,0:T(8,128)(2,1)}, bf16[128,1792]{1,0:T(8,128)(2,1)S(1)}, u32[]{:S(2)}, u32[]{:S(2)}) collective-permute-start(bf16[128,1792]{1,0:T(8,128)(2,1)} %stage_sum.13.refs_10_), channel_id=1, source_target_pairs={{0,8},{4,12},{8,0},{12,4},{16,24},{20,28},{24,16},{28,20},{1,9},{5... | collective-permute-start | bytes 1376264 | tf_op jit(solution)/shard_map/ppermute | solution.py:173
  249.3 24.1 %collective-permute-start.23 = (bf16[128,1536]{1,0:T(8,128)(2,1)}, bf16[128,1536]{1,0:T(8,128)(2,1)}, u32[]{:S(2)}, u32[]{:S(2)}) collective-permute-start(bf16[128,1536]{1,0:T(8,128)(2,1)} %stage_sum.14.refs_3_), channel_id=1, source_target_pairs={{0,16},{4,20},{8,24},{12,28},{16,0},{20,4},{24,8},{28,12},{1,17},{... | collective-permute-start | bytes 1179656 | tf_op jit(solution)/shard_map/ppermute | solution.py:173
  253.0 23.4 %collective-permute-start.22 = (bf16[128,1792]{1,0:T(8,128)(2,1)}, bf16[128,1792]{1,0:T(8,128)(2,1)S(1)}, u32[]{:S(2)}, u32[]{:S(2)}) collective-permute-start(bf16[128,1792]{1,0:T(8,128)(2,1)} %stage_sum.15.refs_10_), channel_id=1, source_target_pairs={{0,8},{4,12},{8,0},{12,4},{16,24},{20,28},{24,16},{28,20},{1,9},{5... | collective-permute-start | bytes 1376264 | tf_op jit(solution)/shard_map/ppermute | solution.py:173
  269.3 0.8 copy-start.3
  276.4 0.8 copy-start.2

commit v4 on v3

v4 whole, which is shorter than its diff:
```python
import functools
import math

import jax
import jax.numpy as jnp
from jax import lax
from jax.experimental import pallas as pl
from jax.experimental.pallas import tpu as pltpu
from jax.sharding import PartitionSpec as P

F32, BF16 = jnp.float32, jnp.bfloat16
VMEM_LIMIT = 63 * 1024 * 1024
CHUNKS = 4
GROUPS = 2
PARTS = 4
LANES = 128
PLAN = ["P0 P1 S0 S1", "S2 S3 W0 S0", "S1 W1 W2 S2", "S3 W3 F0 F1", "F2 F3"]


def divisor(extent, most, step):
    best = extent
    for size in range(step, most + 1, step):
        if extent % size == 0:
            best = size
    return best


def run(kernel, name, grid, ins, outs, deps=(), at=None, scratch=(), flops=0, exps=0):
    held = [(n, o[3]) for n, o in enumerate(outs) if o[3] is not None]
    deps = [d for d in deps if not any(d is x for _, x in held)]
    arrays = [x for x, _ in ins] + [x for _, x in held] + list(deps)
    specs = [s for _, s in ins] + [pl.BlockSpec(memory_space=pl.ANY)] * (len(held) + len(deps))
    lead = 0 if at is None else 1
    first_out = lead + len(arrays)

    def body(*refs):
        kernel(*refs[: lead + len(ins)], *refs[first_out:])

    moved = sum(x.size * x.dtype.itemsize for x, _ in ins)
    return pl.pallas_call(
        body,
        grid_spec=pltpu.PrefetchScalarGridSpec(
            num_scalar_prefetch=lead,
            grid=grid,
            in_specs=specs,
            out_specs=[o[2] for o in outs],
            scratch_shapes=scratch,
        ),
        out_shape=[jax.ShapeDtypeStruct(o[0], o[1]) for o in outs],
        input_output_aliases={lead + len(ins) + k: n for k, (n, _) in enumerate(held)},
        compiler_params=pltpu.CompilerParams(vmem_limit_bytes=VMEM_LIMIT),
        cost_estimate=pl.CostEstimate(flops=flops, bytes_accessed=moved, transcendentals=exps),
        name=name,
    )(*([] if at is None else [at]), *arrays)


def hidden_kernel(gate_ref, up_ref, out_ref):
    gate = gate_ref[...].astype(F32)
    hidden = gate * jax.nn.sigmoid(gate) * up_ref[...].astype(F32)
    out_ref[...] = jnp.transpose(hidden).astype(BF16)


def hidden_transposed(gate, up):
    tokens, width = gate.shape
    step = divisor(width, 1664, 128)
    spec = pl.BlockSpec((tokens, step), lambda i: (0, i))
    out = ((width, tokens), BF16, pl.BlockSpec((step, tokens), lambda i: (i, 0)), None)
    return run(hidden_kernel, "hidden", (width // step,), [(gate, spec), (up, spec)], [out])[0]


def product_kernel(choices, counts, ordering, at_ref, weight_ref, *refs):
    sources, outs = refs[:choices], refs[choices:-3]
    dy_ref, sems, out_sem = refs[-3:]
    step = pl.program_id(0)
    block = dy_ref.shape[0] // 2
    to_order = None
    if ordering:
        place = outs[-1].at[pl.ds(pl.multiple_of(at_ref[3] * 2 * block, 2 * block), 2 * block)]
        to_order = pltpu.make_async_copy(dy_ref, place, out_sem)

    @pl.when(step == 0)
    def _():
        for n, source in enumerate(sources):

            @pl.when(at_ref[4] == n)
            def _():
                copies = []
                for side in range(2):
                    rows = pl.ds(pl.multiple_of(at_ref[1 + side] * block, block), block)
                    copies.append(
                        pltpu.make_async_copy(
                            source.at[rows], dy_ref.at[pl.ds(side * block, block)], sems.at[side]
                        )
                    )
                for copy in copies:
                    copy.start()
                for copy in copies:
                    copy.wait()

        if ordering:
            to_order.start()

    part = lax.dot_general(
        weight_ref[...], dy_ref[...], (((1,), (1,)), ((), ())), preferred_element_type=F32
    )
    first = 0
    for q, count in enumerate(counts):

        @pl.when((step >= first) & (step < first + count))
        def _():
            outs[2 * q][...] = part[:, :block][None]
            outs[2 * q + 1][...] = part[:, block:].astype(BF16)[None]

        first += count

    if ordering:

        @pl.when(step == pl.num_programs(0) - 1)
        def _():
            to_order.wait()


def hidden_grad_terms(at, sources, weight, first, widths, held, ordered, total, deps):
    block, depth = sources[0].shape[0] // 2, sources[0].shape[1]
    tall = divisor(math.gcd(first, *widths), 832, 16)
    counts = [w // tall for w in widths]
    ins = [(weight, pl.BlockSpec((tall, depth), lambda i, at: (first // tall + i, 0)))]
    ins += [(x, pl.BlockSpec(memory_space=pl.ANY)) for x in sources]
    outs, start = [], 0
    for q, (w, count) in enumerate(zip(widths, counts)):

        def place(i, at, where=0 if q % 2 == 0 else 5, start=start, count=count):
            return (at[where], jnp.clip(i - start, 0, count - 1), 0)

        spec = pl.BlockSpec((1, tall, block), place)
        shape = (total // (2 * block), w, block)
        outs += [(shape, F32, spec, held[q][0]), (shape, BF16, spec, held[q][1])]
        start += count
    if ordered is not None:
        outs.append(((total, depth), BF16, pl.BlockSpec(memory_space=pl.ANY), ordered[0]))
    kernel = functools.partial(product_kernel, len(sources), counts, ordered is not None)
    scratch = [
        pltpu.VMEM((2 * block, depth), BF16),
        pltpu.SemaphoreType.DMA((2,)),
        pltpu.SemaphoreType.DMA,
    ]
    flops = 4 * block * depth * sum(widths)
    return run(kernel, "hidden_grad_terms", (start,), ins, outs, deps, at, scratch, flops)


def stage_kernel(*refs):
    refs[-1][...] = sum(ref[...].astype(F32) for ref in refs[:-1]).astype(BF16)


def stage_sum(terms, rows, deps):
    width, block = terms[0].shape[1:]
    tall = divisor(width, 416, 16)
    ins = [(t, pl.BlockSpec((rows, tall, block), lambda i: (1, i, 0))) for t in terms]
    out = ((rows, width, block), BF16, pl.BlockSpec((rows, tall, block), lambda i: (0, i, 0)), None)
    return run(stage_kernel, "stage_sum", (width // tall,), ins, [out], deps)[0]


def finish_kernel(gate_ref, up_ref, *refs):
    grad_hidden = jnp.transpose(sum(ref[0].astype(F32) for ref in refs[:-2]))
    gate, up = gate_ref[...].astype(F32), up_ref[...].astype(F32)
    sig = jax.nn.sigmoid(gate)
    refs[-2][...] = (grad_hidden * up * sig * (1.0 + gate * (1.0 - sig))).astype(BF16)
    refs[-1][...] = (grad_hidden * (gate * sig)).astype(BF16)


def finish(gate, up, terms, first, width, held, deps):
    tokens = gate.shape[0]
    window = pl.BlockSpec((pl.Element(tokens), pl.Element(width)), lambda i: (0, first))
    ins = [(gate, window), (up, window)]
    ins += [(t, pl.BlockSpec((1, width, tokens), lambda i: (0, 0, 0))) for t in terms]
    outs = [(gate.shape, BF16, window, x) for x in held]
    return run(finish_kernel, "finish", (1,), ins, outs, deps, exps=tokens * width)


def weight_grad_kernel(*refs):
    hidden = jnp.concatenate([ref[...] for ref in refs[:-2]], axis=1)
    refs[-1][...] = jnp.dot(hidden, refs[-2][...], preferred_element_type=F32).astype(BF16)


def weight_grad(pieces, dy, whole, total, start, rows, deps):
    block = pieces[0][0].shape[1]
    tokens, depth = dy.shape
    wide = divisor(depth, 256, 128)

    def spec(base):
        return pl.BlockSpec((rows, block), lambda i: ((start - base) // rows, 0))

    ins = [(x, spec(base)) for x, base in pieces]
    ins.append((dy, pl.BlockSpec((tokens, wide), lambda i: (0, i))))
    out = ((total, depth), BF16, pl.BlockSpec((rows, wide), lambda i: (start // rows, i)), whole)
    flops = 2 * rows * tokens * depth
    return run(weight_grad_kernel, "weight_grad", (depth // wide,), ins, [out], deps, flops=flops)[0]


def arrivals(z, count):
    found = []
    for s in range(1, count):
        if z - s >= 0:
            found.append(("up", s, z - s))
        if z + s < count:
            found.append(("down", s, z + s))
    return found


def pick(table, index):
    value = jnp.int32(table[0])
    for n in range(1, len(table)):
        value = jnp.where(index == n, jnp.int32(table[n]), value)
    return value


def program(row_count, col_count, grad_out, gate_act, up_act, down_weight):
    assert row_count == 2 * col_count
    row = lax.axis_index("row").astype(jnp.int32)
    col = lax.axis_index("col").astype(jnp.int32)
    core, chip = row % 2, row // 2
    bits = []
    while 2 ** (len(bits) + 1) < row_count:
        bits.append(2 ** (len(bits) + 1))
    streams = (bits, bits[::-1])
    width = down_weight.shape[0]
    block = gate_act.shape[0]
    tokens = row_count * block

    def swap(x, bit):
        pairs = [(r, r ^ bit) for r in range(row_count)]
        return jax.tree.map(lambda x: lax.ppermute(x, "row", pairs), x)

    places = []
    for order in streams:
        found = [0]
        for bit in order[::-1]:
            found = found + [f | bit // 2 for f in found]
        places.append([found.index(m) for m in range(row_count // 2)])

    ways = {"up": [grad_out], "down": [grad_out]}

    def forward(s):
        up, down = ways["up"], ways["down"]
        up.append(lax.ppermute(up[-1], "col", [(i, i + 1) for i in range(s - 1, col_count - 1)]))
        down.append(lax.ppermute(down[-1], "col", [(i, i - 1) for i in range(1, col_count - s + 1)]))

    def arrived(k):
        sources = [arrivals(z, col_count)[k - 1] for z in range(col_count)]
        kinds = sorted(set((way, s) for way, s, _ in sources))
        which = pick([kinds.index((way, s)) for way, s, _ in sources], col)
        return [ways[way][s] for way, s in kinds], which, pick([c for _, _, c in sources], col)

    units = width // LANES
    edges = [units * q // CHUNKS * LANES for q in range(CHUNKS + 1)]
    widths = [b - a for a, b in zip(edges, edges[1:])]
    terms = [(None, None)] * CHUNKS
    ordered = None

    def product(chunks, dy, deps):
        nonlocal ordered
        sources, which, place = dy
        flip = chip ^ place
        at = jnp.stack([pick(places[0], flip), core, 1 - core, flip, which, pick(places[1], flip)])
        first, last = chunks[0], chunks[-1] + 1
        out = hidden_grad_terms(
            at,
            sources,
            down_weight,
            edges[first],
            widths[first:last],
            terms[first:last],
            (ordered,) if first == 0 else None,
            tokens,
            deps,
        )
        for n, q in enumerate(chunks):
            terms[q] = (out[2 * n], out[2 * n + 1])
        if first == 0:
            ordered = out[-1]
        return out[0]

    forward(1)
    hidden = hidden_transposed(gate_act, up_act)
    held, base = {0: [hidden]}, {0: [0]}
    first_bits = bits[:2]
    for bit in first_bits + [1]:
        held[bit], base[bit] = swap([hidden], bit), [0]
    half = width // 2

    last = hidden
    dy = [grad_out], jnp.int32(0), col
    both = []
    for k in range(1, col_count):
        last = product(range(CHUNKS), dy, [last] + (held[1] if k == 2 else []))
        if k == 2 and len(first_bits) == 2:
            a, b = first_bits
            held[a], held[b], last = lax.optimization_barrier((held[a], held[b], last))
            both = [jnp.concatenate(held[a] + held[b])]
        ways["up"][k], ways["down"][k], last, both = lax.optimization_barrier(
            (ways["up"][k], ways["down"][k], last, both)
        )
        terms[0] = (last, terms[0][1])
        if k + 1 < col_count:
            forward(k + 1)
        dy = arrived(k)
        if k == 2 and len(first_bits) == 2:
            held[a | b] = [swap(held[a][0][:half], b), swap(held[b][0][half:], a)]
            base[a | b] = [0, half]
            held[a | 1] = held[b | 1] = swap(both, 1)
            base[a | 1], base[b | 1] = [0], [-width]

    held, last = lax.optimization_barrier((held, last))
    terms[0] = (last, terms[0][1])
    for bit in bits[2:]:
        for f in [f for f in held if f | bit not in held]:
            held[f | bit], base[f | bit] = swap(held[f], bit), base[f]
    ready = jax.tree.leaves(held)
    for f in [f for f in held if f | 1 not in held]:
        held[f | 1], base[f | 1] = swap(held[f], 1), base[f]

    grad_gate = grad_up = grad_down = None
    sums, stages = [None] * CHUNKS, [0] * CHUNKS
    part = width // PARTS

    def step(kind, n, last):
        nonlocal grad_gate, grad_up, grad_down
        if kind == "P":
            chunks = range(CHUNKS * n // GROUPS, CHUNKS * (n + 1) // GROUPS)
            deps = ready if n == 0 else jax.tree.leaves(held) if n == 1 else []
            last = product(chunks, dy, [last] + deps)
            for q in chunks:
                sums[q] = [terms[q][0], swap(terms[q][1], 1)]
            return last
        if kind == "S":
            bit = streams[n % 2][stages[n]]
            stages[n] += 1
            send = stage_sum(sums[n], (row_count // 2) >> stages[n], [last])
            sums[n] = sums[n] + [swap(send, bit)]
            return send
        if kind == "F":
            grad_gate, grad_up = finish(
                gate_act, up_act, sums[n], edges[n], widths[n], (grad_gate, grad_up), [last]
            )
            return grad_up
        pieces = []
        for f in range(row_count):
            side = -1 if n * part >= half else 0
            pieces.append((held[f][side], base[f][side]))
        grad_down = weight_grad(pieces, ordered, grad_down, width, n * part, part, [last])
        return grad_down

    for item in " ".join(PLAN).split():
        kind, n = item[0], int(item[1:])
        while kind == "F" and stages[n] < len(bits):
            last = step("S", n, last)
        last = step(kind, n, last)
    return grad_gate, grad_up, grad_down


def solution(mesh):
    def local(*args):
        return program(mesh.shape["row"], mesh.shape["col"], *args)

    return jax.shard_map(
        local,
        mesh=mesh,
        in_specs=(P("col", "row"), P("row", "col"), P("row", "col"), P("col", "row")),
        out_specs=(P("row", "col"), P("row", "col"), P("col", "row")),
        check_vma=False,
    )
```

time: 283 us -> 227 us (0.80)
  Pallas kernels: 214 us -> 172 us
  other arithmetic: 16.6 us -> 4.87 us
    pallas_call x33 -> x22, Pallas kernels: 214 us -> 172 us  [run(): pl.pallas_call(body, grid_spec=pltpu.PrefetchScalarGridSpec(num_scalar_pr...]
    select_n x3 -> x0, other arithmetic: 8.01 us -> none  [arrived(): value = x if value is None else jnp.where(col == z, x, value)]
    ppermute x20, waiting for transfers between devices: 8.8 us -> 1.8 us  [swap(): return jax.tree.map(lambda x: lax.ppermute(x, 'row', pairs), x)]
    another operation x6 -> x0, other arithmetic: 3.68 us -> none  [product(): at = jnp.stack([pick(places[q % 2], flip), core, 1 - core, flip])]
    ppermute x3, waiting for transfers between devices: 0.01 us -> 3.22 us  [forward(): lax.ppermute(down[-1], 'col', [(i, i - 1) for i in range(1, col_count - s...]
  transfers between devices with their start and end apart: 26 -> 26, of which waited for: 2 -> 4; matrix products, arithmetic and copies ran while one was open for 6% -> 5% of each run, Pallas kernels for 66% -> 73%
where the time goes in v4:
time: 227 us; the launch traced here: 225 us
  Pallas kernels  172 us (76%)
  starting transfers between devices  31.5 us (14%)
  local copies, waits for them, and re-layouts  8.34 us (4%)
  waiting for transfers between devices  6.82 us (3%)
  other arithmetic  4.87 us (2%)
    pallas_call x22, Pallas kernels, run(): pl.pallas_call(body, grid_spec=pltpu.PrefetchScalarGridSpec(num_scalar_pr...  172 us
    ppermute x20, starting transfers between devices, swap(): return jax.tree.map(lambda x: lax.ppermute(x, 'row', pairs), x)  13.9 us
    ppermute x3, starting transfers between devices, forward(): lax.ppermute(down[-1], 'col', [(i, i - 1) for i in range(1, col_count - s...  9.93 us
    ppermute x3, starting transfers between devices, forward(): lax.ppermute(up[-1], 'col', [(i, i + 1) for i in range(s - 1, col_count -...  7.69 us
    concatenate x1, other arithmetic, program(): both = [jnp.concatenate(held[a] + held[b])]  4.87 us
  transfers between devices with their start and end apart: 26, of which 4 were waited for; matrix products, arithmetic and copies ran while one was open for 5% of the time, Pallas kernels for 73%

profile of v4, /device:TPU:16, one launch (start us, length us, event | category | flops | bytes accessed | tf_op | source)
XLA Modules:
  0.0 224.8 jit_solution(18076725828780155282)
XLA Ops:
  0.6 4.4 %hidden.1.refs_3_.refs_11_.refs_0_ = bf16[6656,128]{1,0:T(8,128)(2,1)} custom-call(bf16[128,6656]{1,0:T(8,128)(2,1)} %refs_0_.9, bf16[128,6656]{1,0:T(8,128)(2,1)} %refs_1_.19), custom_call_target="tpu_custom_call" | custom-call | bytes 3407872 | tf_op jit(solution)/shard_map/hidden/pallas_call | solution.py:40
  5.0 1.5 collective-permute-start.5
  6.6 1.5 collective-permute-start.4
  8.1 3.5 %collective-permute-start = (bf16[256,2048]{1,0:T(8,128)(2,1)}, bf16[256,2048]{1,0:T(8,128)(2,1)}, u32[]{:S(2)}, u32[]{:S(2)}) collective-permute-start(bf16[256,2048]{1,0:T(8,128)(2,1)} %refs_2_.1), channel_id=1, source_target_pairs={{0,1},{1,2},{2,3},{4,5},{5,6},{6,7},{8,9},{9,10},{10,11},{12,13},{... | collective-permute-start | bytes 3145736 | tf_op jit(solution)/shard_map/ppermute | solution.py:245
  11.5 2.4 %collective-permute-start.1 = (bf16[256,2048]{1,0:T(8,128)(2,1)}, bf16[256,2048]{1,0:T(8,128)(2,1)}, u32[]{:S(2)}, u32[]{:S(2)}) collective-permute-start(bf16[256,2048]{1,0:T(8,128)(2,1)} %refs_2_.1), channel_id=1, source_target_pairs={{1,0},{2,1},{3,2},{5,4},{6,5},{7,6},{9,8},{10,9},{11,10},{13,12},{... | collective-permute-start | bytes 3145736 | tf_op jit(solution)/shard_map/ppermute | solution.py:246
  14.0 0.6 stack.91.refs_0_
  14.6 0.6 stack.86.refs_0_
  15.2 18.3 %hidden_grad_terms.5 = (f32[4,1664,128]{2,1,0:T(8,128)}, bf16[4,1664,128]{2,1,0:T(8,128)(2,1)}, f32[4,1664,128]{2,1,0:T(8,128)}, bf16[4,1664,128]{2,1,0:T(8,128)...) custom-call(s32[6]{0:T(128)} %stack.86.refs_0_, ...), custom_call_target="tpu_custom_call" | custom-call | flops 6979321856 | bytes 28311552 | tf_op jit(solution)/shard_map/hidden_grad_terms/pallas_call | solution.py:40
  33.5 1.8 collective-permute-done.refs_3_
  35.3 3.2 %collective-permute-done.1.refs_2_ = bf16[256,2048]{1,0:T(8,128)(2,1)} collective-permute-done((bf16[256,2048]{1,0:T(8,128)(2,1)}, bf16[256,2048]{1,0:T(8,128)(2,1)}, u32[]{:S(2)}, u32[]{:S(2)}) %collective-permute-start.1) | collective-permute-done | bytes 1048608 | tf_op jit(solution)/shard_map/ppermute | solution.py:246
  38.5 1.9 collective-permute-start.2
  40.4 5.9 %collective-permute-start.3 = (bf16[256,2048]{1,0:T(8,128)(2,1)}, bf16[256,2048]{1,0:T(8,128)(2,1)}, u32[]{:S(2)}, u32[]{:S(2)}) collective-permute-start(bf16[256,2048]{1,0:T(8,128)(2,1)} %collective-permute-done.1.refs_2_), channel_id=1, source_target_pairs={{1,0},{2,1},{5,4},{6,5},{9,8},{10,9},{13,12},{14,13},{17,16},{18,1... | collective-permute-start | bytes 3145736 | tf_op jit(solution)/shard_map/ppermute | solution.py:246
  46.3 18.3 %hidden_grad_terms.6 = (f32[4,1664,128]{2,1,0:T(8,128)}, bf16[4,1664,128]{2,1,0:T(8,128)(2,1)}, f32[4,1664,128]{2,1,0:T(8,128)}, bf16[4,1664,128]{2,1,0:T(8,128)...) custom-call(s32[6]{0:T(128)} %stack.91.refs_0_, ...), custom_call_target="tpu_custom_call", output_to_operand_aliasing={{0}: (4, {}), {1}: (5, {}), {2}: (6, {}), {3}: (7, {}), {4}... | custom-call | flops 6979321856 | bytes 29360128 | tf_op jit(solution)/shard_map/hidden_grad_terms/pallas_call | solution.py:40
  64.6 4.9 %pad_maximum_fusion = bf16[13312,128]{1,0:T(8,128)(2,1)} fusion(bf16[6656,128]{1,0:T(8,128)(2,1)} %collective-permute-done.5.refs_15_.refs_4_, bf16[6656,128]{1,0:T(8,128)(2,1)} %collective-permute-done.4.refs_13_.refs_2_), kind=kLoop, calls=%fused_computation | loop fusion | flops 6815744 | bytes 6815744 | tf_op jit(solution)/shard_map/concatenate | solution.py:299
  69.6 1.7 collective-permute-start.8
  71.2 2.3 %collective-permute-start.7 = (bf16[256,2048]{1,0:T(8,128)(2,1)}, bf16[256,2048]{1,0:T(8,128)(2,1)}, u32[]{:S(2)}, u32[]{:S(2)}) collective-permute-start(bf16[256,2048]{1,0:T(8,128)(2,1)} %collective-permute-done.2.refs_4_), channel_id=1, source_target_pairs={{2,3},{6,7},{10,11},{14,15},{18,19},{22,23},{26,27},{30,31}} | collective-permute-start | bytes 3145736 | tf_op jit(solution)/shard_map/ppermute | solution.py:245
  73.5 2.1 slice.6
  75.7 2.1 slice.7
  78.8 0.6 stack.96.refs_0_
  79.4 18.5 %hidden_grad_terms.7 = (f32[4,1664,128]{2,1,0:T(8,128)}, bf16[4,1664,128]{2,1,0:T(8,128)(2,1)}, f32[4,1664,128]{2,1,0:T(8,128)}, bf16[4,1664,128]{2,1,0:T(8,128)...) custom-call(s32[6]{0:T(128)} %stack.96.refs_0_, ...), custom_call_target="tpu_custom_call", output_to_operand_aliasing={{0}: (5, {}), {1}: (6, {}), {2}: (7, {}), {3}: (8, {}), {4}... | custom-call | flops 6979321856 | bytes 30408704 | tf_op jit(solution)/shard_map/hidden_grad_terms/pallas_call | solution.py:40
  97.9 1.4 collective-permute-done.11.refs_18_.refs_6_
  100.2 0.6 stack.82.refs_0_
  100.8 11.1 %hidden_grad_terms.8 = (f32[4,1664,128]{2,1,0:T(8,128)}, bf16[4,1664,128]{2,1,0:T(8,128)(2,1)}, f32[4,1664,128]{2,1,0:T(8,128)}, bf16[4,1664,128]{2,1,0:T(8,128)(2,1)}, bf16[1024,2048]{1,0:T(8,128)(2,1)}) custom-call(s32[6]{0:T(128)} %stack.82.refs_0_, ...), custom_call_target="tpu_custom_call", output_to_operand_aliasing={{0}: (6, {}), {1}: (7, {}), {2}: (8, {}), {3}: (9, {}), {4}... | custom-call | flops 3489660928 | bytes 31457280 | tf_op jit(solution)/shard_map/hidden_grad_terms/pallas_call | solution.py:40
  112.5 10.9 %hidden_grad_terms.9 = (f32[4,1664,128]{2,1,0:T(8,128)}, bf16[4,1664,128]{2,1,0:T(8,128)(2,1)}, f32[4,1664,128]{2,1,0:T(8,128)}, bf16[4,1664,128]{2,1,0:T(8,128)(2,1)}) custom-call(s32[6]{0:T(128)} %stack.82.refs_0_, bf16[6656,2048]{1,0:T(8,128)(2,1)} %refs_1_.15, ...), custom_call_target="tpu_custom_call", output_to_operand_aliasing={{0}: (6, {}), {1}: (7, {}), {2}: (8, {}), {3}: (9, {})} | custom-call | flops 3489660928 | bytes 31457280 | tf_op jit(solution)/shard_map/hidden_grad_terms/pallas_call | solution.py:40
  124.0 3.6 %stage_sum.8.refs_2_ = bf16[2,1664,128]{2,1,0:T(8,128)(2,1)} custom-call(f32[4,1664,128]{2,1,0:T(8,128)} %get-tuple-element.118.refs_10_.refs_0_.refs_2_, bf16[4,1664,128]{2,1,0:T(8,128)(2,1)} %collective-permute-done.17.refs_1_.refs_3_, f32[4,1664,128]{2,1,0:T(8,128)} %get-tuple-element.121.refs_2_.refs_0_), custom_call_target="tpu_custom_call" | custom-call | bytes 5111808 | tf_op jit(solution)/shard_map/stage_sum/pallas_call | solution.py:40
  127.6 1.5 collective-permute-start.21
  129.1 3.6 %stage_sum.9.refs_2_ = bf16[2,1664,128]{2,1,0:T(8,128)(2,1)} custom-call(f32[4,1664,128]{2,1,0:T(8,128)} %get-tuple-element.123.refs_0_.refs_2_, bf16[4,1664,128]{2,1,0:T(8,128)(2,1)} %collective-permute-done.16.refs_1_.refs_3_, bf16[2,1664,128]{2,1,0:T(8,128)(2,1)} %stage_sum.8.refs_2_), custom_call_target="tpu_custom_call" | custom-call | bytes 5111808 | tf_op jit(solution)/shard_map/stage_sum/pallas_call | solution.py:40
  132.7 0.6 collective-permute-start.20
  133.3 3.6 %stage_sum.10.refs_2_ = bf16[2,1664,128]{2,1,0:T(8,128)(2,1)} custom-call(f32[4,1664,128]{2,1,0:T(8,128)} %get-tuple-element.121.refs_2_.refs_0_, bf16[4,1664,128]{2,1,0:T(8,128)(2,1)} %collective-permute-done.15.refs_1_.refs_3_, bf16[2,1664,128]{2,1,0:T(8,128)(2,1)} %stage_sum.9.refs_2_), custom_call_target="tpu_custom_call" | custom-call | bytes 5111808 | tf_op jit(solution)/shard_map/stage_sum/pallas_call | solution.py:40
  137.4 3.6 %stage_sum.11.refs_9_ = bf16[2,1664,128]{2,1,0:T(8,128)(2,1)} custom-call(f32[4,1664,128]{2,1,0:T(8,128)} %get-tuple-element.119.refs_0_.refs_2_, bf16[4,1664,128]{2,1,0:T(8,128)(2,1)} %collective-permute-done.14.refs_1_.refs_3_, bf16[2,1664,128]{2,1,0:T(8,128)(2,1)} %stage_sum.10.refs_2_), custom_call_target="tpu_custom_call" | custom-call | bytes 5111808 | tf_op jit(solution)/shard_map/stage_sum/pallas_call | solution.py:40
  141.0 1.5 collective-permute-start.18
  142.5 12.5 %weight_grad.4.refs_3_.refs_9_ = bf16[6656,2048]{1,0:T(8,128)(2,1)} custom-call(bf16[6656,128]{1,0:T(8,128)(2,1)} %hidden.1.refs_3_.refs_11_.refs_0_, bf16[6656,128]{1,0:T(8,128)(2,1)} %collective-permute-done.6.refs_13_.refs_12_.refs_1_, bf16[6656,128]{1,0:T(8,128)(2,1)} %collective-permute-done.4.refs_13_.refs_2_, ...), custom_call_target="tpu_custom_call" | custom-call | flops 6979321856 | bytes 19529728 | tf_op jit(solution)/shard_map/weight_grad/pallas_call | solution.py:40
  155.0 3.5 %stage_sum.12.refs_3_ = bf16[1,1664,128]{2,1,0:T(8,128)(2,1)} custom-call(f32[4,1664,128]{2,1,0:T(8,128)} %get-tuple-element.118.refs_10_.refs_0_.refs_2_, bf16[4,1664,128]{2,1,0:T(8,128)(2,1)} %collective-permute-done.17.refs_1_.refs_3_, bf16[2,1664,128]{2,1,0:T(8,128)(2,1)} %collective-permute-done.21.refs_2_.refs_4_, ...), custom_call_target="tpu_custom_call" | custom-call | bytes 5963776 | tf_op jit(solution)/shard_map/stage_sum/pallas_call | solution.py:40
  158.4 0.5 collective-permute-start.25
  159.0 3.5 %stage_sum.13.refs_10_ = bf16[1,1664,128]{2,1,0:T(8,128)(2,1)} custom-call(f32[4,1664,128]{2,1,0:T(8,128)} %get-tuple-element.123.refs_0_.refs_2_, bf16[4,1664,128]{2,1,0:T(8,128)(2,1)} %collective-permute-done.16.refs_1_.refs_3_, bf16[2,1664,128]{2,1,0:T(8,128)(2,1)} %collective-permute-done.20.refs_2_.refs_4_, bf16[1,1664,128]{2,1,0:T(8,128)(2,1)} %stage_sum.12.refs_3_), custom_call_target="tpu_custom_call" | custom-call | bytes 5963776 | tf_op jit(solution)/shard_map/stage_sum/pallas_call | solution.py:40
  162.4 1.5 collective-permute-start.24
  164.0 12.5 %weight_grad.5.refs_9_ = bf16[6656,2048]{1,0:T(8,128)(2,1)} custom-call(bf16[6656,128]{1,0:T(8,128)(2,1)} %hidden.1.refs_3_.refs_11_.refs_0_, bf16[6656,128]{1,0:T(8,128)(2,1)} %collective-permute-done.6.refs_13_.refs_12_.refs_1_, bf16[6656,128]{1,0:T(8,128)(2,1)} %collective-permute-done.4.refs_13_.refs_2_, ...), custom_call_target="tpu_custom_call", output_to_operand_aliasing={{}: (9, {})} | custom-call | flops 6979321856 | bytes 19529728 | tf_op jit(solution)/shard_map/weight_grad/pallas_call | solution.py:40
  176.4 12.5 %weight_grad.6.refs_3_.refs_9_ = bf16[6656,2048]{1,0:T(8,128)(2,1)} custom-call(bf16[6656,128]{1,0:T(8,128)(2,1)} %hidden.1.refs_3_.refs_11_.refs_0_, bf16[6656,128]{1,0:T(8,128)(2,1)} %collective-permute-done.6.refs_13_.refs_12_.refs_1_, bf16[6656,128]{1,0:T(8,128)(2,1)} %collective-permute-done.4.refs_13_.refs_2_, ...), custom_call_target="tpu_custom_call", output_to_operand_aliasing={{}: (9, {})} | custom-call | flops 6979321856 | bytes 19529728 | tf_op jit(solution)/shard_map/weight_grad/pallas_call | solution.py:40
  188.9 3.5 %stage_sum.14.refs_3_ = bf16[1,1664,128]{2,1,0:T(8,128)(2,1)} custom-call(f32[4,1664,128]{2,1,0:T(8,128)} %get-tuple-element.121.refs_2_.refs_0_, bf16[4,1664,128]{2,1,0:T(8,128)(2,1)} %collective-permute-done.15.refs_1_.refs_3_, bf16[2,1664,128]{2,1,0:T(8,128)(2,1)} %collective-permute-done.19.refs_2_.refs_4_, bf16[6656,2048]{1,0:T(8,128)(2,1)} %weight_grad.6.refs_3_.refs_9_), custom_call_target="tpu_custom_call" | custom-call | bytes 5963776 | tf_op jit(solution)/shard_map/stage_sum/pallas_call | solution.py:40
  192.4 1.5 collective-permute-start.23
  193.8 0.9 copy-done.1
  194.7 3.5 %stage_sum.15.refs_10_ = bf16[1,1664,128]{2,1,0:T(8,128)(2,1)} custom-call(f32[4,1664,128]{2,1,0:T(8,128)} %get-tuple-element.119.refs_0_.refs_2_, bf16[4,1664,128]{2,1,0:T(8,128)(2,1)} %collective-permute-done.14.refs_1_.refs_3_, bf16[2,1664,128]{2,1,0:T(8,128)(2,1)} %copy-done.1, bf16[1,1664,128]{2,1,0:T(8,128)(2,1)} %stage_sum.14.refs_3_), custom_call_target="tpu_custom_call" | custom-call | bytes 5963776 | tf_op jit(solution)/shard_map/stage_sum/pallas_call | solution.py:40
  198.7 12.5 %weight_grad.7.refs_6_ = bf16[6656,2048]{1,0:T(8,128)(2,1)} custom-call(bf16[6656,128]{1,0:T(8,128)(2,1)} %hidden.1.refs_3_.refs_11_.refs_0_, bf16[6656,128]{1,0:T(8,128)(2,1)} %collective-permute-done.6.refs_13_.refs_12_.refs_1_, bf16[6656,128]{1,0:T(8,128)(2,1)} %collective-permute-done.4.refs_13_.refs_2_, ...), custom_call_target="tpu_custom_call", output_to_operand_aliasing={{}: (9, {})} | custom-call | flops 6979321856 | bytes 19529728 | tf_op jit(solution)/shard_map/weight_grad/pallas_call | solution.py:40
  211.2 3.2 %finish.4 = (bf16[128,6656]{1,0:T(8,128)(2,1)}, bf16[128,6656]{1,0:T(8,128)(2,1)}) custom-call(bf16[128,6656]{1,0:T(8,128)(2,1)} %refs_0_.9, bf16[128,6656]{1,0:T(8,128)(2,1)} %refs_1_.19, f32[4,1664,128]{2,1,0:T(8,128)} %get-tuple-element.118.refs_10_.refs_0_.refs_2_, bf16[4,1664,128]{2,1,0:T(8,128)(2,1)} %collective-permute-done.17.refs_1_.refs_3_, ...), custom_call_target="tpu_custom_call" | custom-call | bytes 9797632 | tf_op jit(solution)/shard_map/finish/pallas_call | solution.py:40
  214.4 3.2 %finish.5 = (bf16[128,6656]{1,0:T(8,128)(2,1)}, bf16[128,6656]{1,0:T(8,128)(2,1)}) custom-call(bf16[128,6656]{1,0:T(8,128)(2,1)} %refs_0_.9, bf16[128,6656]{1,0:T(8,128)(2,1)} %refs_1_.19, f32[4,1664,128]{2,1,0:T(8,128)} %get-tuple-element.123.refs_0_.refs_2_, ...), custom_call_target="tpu_custom_call", output_to_operand_aliasing={{0}: (6, {}), {1}: (7, {})} | custom-call | bytes 9797632 | tf_op jit(solution)/shard_map/finish/pallas_call | solution.py:40
  217.6 3.2 %finish.6 = (bf16[128,6656]{1,0:T(8,128)(2,1)}, bf16[128,6656]{1,0:T(8,128)(2,1)}) custom-call(bf16[128,6656]{1,0:T(8,128)(2,1)} %refs_0_.9, bf16[128,6656]{1,0:T(8,128)(2,1)} %refs_1_.19, f32[4,1664,128]{2,1,0:T(8,128)} %get-tuple-element.121.refs_2_.refs_0_, ...), custom_call_target="tpu_custom_call", output_to_operand_aliasing={{0}: (6, {}), {1}: (7, {})} | custom-call | bytes 9797632 | tf_op jit(solution)/shard_map/finish/pallas_call | solution.py:40
  220.8 0.7 copy-done.2
  221.6 3.2 %finish.7 = (bf16[128,6656]{1,0:T(8,128)(2,1)}, bf16[128,6656]{1,0:T(8,128)(2,1)}) custom-call(bf16[128,6656]{1,0:T(8,128)(2,1)} %refs_0_.9, bf16[128,6656]{1,0:T(8,128)(2,1)} %refs_1_.19, f32[4,1664,128]{2,1,0:T(8,128)} %get-tuple-element.119.refs_0_.refs_2_, ...), custom_call_target="tpu_custom_call", output_to_operand_aliasing={{0}: (6, {}), {1}: (7, {})} | custom-call | bytes 9797632 | tf_op jit(solution)/shard_map/finish/pallas_call | solution.py:40
  (39 shorter events, 4.2 us)
Async XLA Ops:
  5.0 41.3 %collective-permute-start.6 = (bf16[6656,128]{1,0:T(8,128)(2,1)}, bf16[6656,128]{1,0:T(8,128)(2,1)}, u32[]{:S(2)}, u32[]{:S(2)}) collective-permute-start(bf16[6656,128]{1,0:T(8,128)(2,1)} %hidden.1.refs_3_.refs_11_.refs_0_), channel_id=1, source_target_pairs={{0,4},{4,0},{8,12},{12,8},{16,20},{20,16},{24,28},{28,24},{1,5},{5... | collective-permute-start | bytes 5111816 | tf_op jit(solution)/shard_map/ppermute | solution.py:232
  5.0 59.6 %collective-permute-start.5 = (bf16[6656,128]{1,0:T(8,128)(2,1)}, bf16[6656,128]{1,0:T(8,128)(2,1)}, u32[]{:S(2)}, u32[]{:S(2)}) collective-permute-start(bf16[6656,128]{1,0:T(8,128)(2,1)} %hidden.1.refs_3_.refs_11_.refs_0_), channel_id=1, source_target_pairs={{0,16},{4,20},{8,24},{12,28},{16,0},{20,4},{24,8},{28,12},{1,17},{... | collective-permute-start | bytes 5111816 | tf_op jit(solution)/shard_map/ppermute | solution.py:232
  6.6 58.1 %collective-permute-start.4 = (bf16[6656,128]{1,0:T(8,128)(2,1)}, bf16[6656,128]{1,0:T(8,128)(2,1)}, u32[]{:S(2)}, u32[]{:S(2)}) collective-permute-start(bf16[6656,128]{1,0:T(8,128)(2,1)} %hidden.1.refs_3_.refs_11_.refs_0_), channel_id=1, source_target_pairs={{0,8},{4,12},{8,0},{12,4},{16,24},{20,28},{24,16},{28,20},{1,9},{5... | collective-permute-start | bytes 5111816 | tf_op jit(solution)/shard_map/ppermute | solution.py:232
  8.1 27.2 %collective-permute-start = (bf16[256,2048]{1,0:T(8,128)(2,1)}, bf16[256,2048]{1,0:T(8,128)(2,1)}, u32[]{:S(2)}, u32[]{:S(2)}) collective-permute-start(bf16[256,2048]{1,0:T(8,128)(2,1)} %refs_2_.1), channel_id=1, source_target_pairs={{0,1},{1,2},{2,3},{4,5},{5,6},{6,7},{8,9},{9,10},{10,11},{12,13},{... | collective-permute-start | bytes 3145736 | tf_op jit(solution)/shard_map/ppermute | solution.py:245
  11.5 26.9 %collective-permute-start.1 = (bf16[256,2048]{1,0:T(8,128)(2,1)}, bf16[256,2048]{1,0:T(8,128)(2,1)}, u32[]{:S(2)}, u32[]{:S(2)}) collective-permute-start(bf16[256,2048]{1,0:T(8,128)(2,1)} %refs_2_.1), channel_id=1, source_target_pairs={{1,0},{2,1},{3,2},{5,4},{6,5},{7,6},{9,8},{10,9},{11,10},{13,12},{... | collective-permute-start | bytes 3145736 | tf_op jit(solution)/shard_map/ppermute | solution.py:246
  38.5 31.0 %collective-permute-start.2 = (bf16[256,2048]{1,0:T(8,128)(2,1)}, bf16[256,2048]{1,0:T(8,128)(2,1)}, u32[]{:S(2)}, u32[]{:S(2)}) collective-permute-start(bf16[256,2048]{1,0:T(8,128)(2,1)} %collective-permute-done.refs_3_), channel_id=1, source_target_pairs={{1,2},{2,3},{5,6},{6,7},{9,10},{10,11},{13,14},{14,15},{17,18},{18... | collective-permute-start | bytes 3145736 | tf_op jit(solution)/shard_map/ppermute | solution.py:245
  40.4 29.1 %collective-permute-start.3 = (bf16[256,2048]{1,0:T(8,128)(2,1)}, bf16[256,2048]{1,0:T(8,128)(2,1)}, u32[]{:S(2)}, u32[]{:S(2)}) collective-permute-start(bf16[256,2048]{1,0:T(8,128)(2,1)} %collective-permute-done.1.refs_2_), channel_id=1, source_target_pairs={{1,0},{2,1},{5,4},{6,5},{9,8},{10,9},{13,12},{14,13},{17,16},{18,1... | collective-permute-start | bytes 3145736 | tf_op jit(solution)/shard_map/ppermute | solution.py:246
  69.5 30.2 %collective-permute-start.9 = (bf16[13312,128]{1,0:T(8,128)(2,1)}, bf16[13312,128]{1,0:T(8,128)(2,1)}, u32[]{:S(2)}, u32[]{:S(2)}) collective-permute-start(bf16[13312,128]{1,0:T(8,128)(2,1)} %pad_maximum_fusion), channel_id=1, source_target_pairs={{0,4},{4,0},{8,12},{12,8},{16,20},{20,16},{24,28},{28,24},{1,5},{5... | collective-permute-start | bytes 10223624 | tf_op jit(solution)/shard_map/ppermute | solution.py:232
  69.6 28.3 %collective-permute-start.8 = (bf16[256,2048]{1,0:T(8,128)(2,1)}, bf16[256,2048]{1,0:T(8,128)(2,1)}, u32[]{:S(2)}, u32[]{:S(2)}) collective-permute-start(bf16[256,2048]{1,0:T(8,128)(2,1)} %collective-permute-done.3.refs_3_.refs_2_), channel_id=1, source_target_pairs={{1,0},{5,4},{9,8},{13,12},{17,16},{21,20},{25,24},{29,28}} | collective-permute-start | bytes 3145736 | tf_op jit(solution)/shard_map/ppermute | solution.py:246
  71.2 26.7 %collective-permute-start.7 = (bf16[256,2048]{1,0:T(8,128)(2,1)}, bf16[256,2048]{1,0:T(8,128)(2,1)}, u32[]{:S(2)}, u32[]{:S(2)}) collective-permute-start(bf16[256,2048]{1,0:T(8,128)(2,1)} %collective-permute-done.2.refs_4_), channel_id=1, source_target_pairs={{2,3},{6,7},{10,11},{14,15},{18,19},{22,23},{26,27},{30,31}} | collective-permute-start | bytes 3145736 | tf_op jit(solution)/shard_map/ppermute | solution.py:245
  77.8 21.5 %collective-permute-start.11 = (bf16[3328,128]{1,0:T(8,128)(2,1)}, bf16[3328,128]{1,0:T(8,128)(2,1)S(1)}, u32[]{:S(2)}, u32[]{:S(2)}) collective-permute-start(bf16[3328,128]{1,0:T(8,128)(2,1)} %slice.7), channel_id=1, source_target_pairs={{0,8},{4,12},{8,0},{12,4},{16,24},{20,28},{24,16},{28,20},{1,9},{5... | collective-permute-start | bytes 2555912 | tf_op jit(solution)/shard_map/ppermute | solution.py:232
  78.3 21.4 %collective-permute-start.10 = (bf16[3328,128]{1,0:T(8,128)(2,1)}, bf16[3328,128]{1,0:T(8,128)(2,1)}, u32[]{:S(2)}, u32[]{:S(2)}) collective-permute-start(bf16[3328,128]{1,0:T(8,128)(2,1)} %slice.6), channel_id=1, source_target_pairs={{0,16},{4,20},{8,24},{12,28},{16,0},{20,4},{24,8},{28,12},{1,17},{... | collective-permute-start | bytes 2555912 | tf_op jit(solution)/shard_map/ppermute | solution.py:232
  99.3 1.5 copy-start
  99.7 12.8 %collective-permute-start.12 = (bf16[3328,128]{1,0:T(8,128)(2,1)}, bf16[3328,128]{1,0:T(8,128)(2,1)}, u32[]{:S(2)}, u32[]{:S(2)}) collective-permute-start(bf16[3328,128]{1,0:T(8,128)(2,1)} %collective-permute-done.10.refs_17_.refs_6_), channel_id=1, source_target_pairs={{0,4},{4,0},{8,12},{12,8},{16,20},{20,16},{24,28},{28,24},{1,5},{5... | collective-permute-start | bytes 2555912 | tf_op jit(solution)/shard_map/ppermute | solution.py:232
  99.7 12.8 %collective-permute-start.13 = (bf16[3328,128]{1,0:T(8,128)(2,1)S(1)}, bf16[3328,128]{1,0:T(8,128)(2,1)}, u32[]{:S(2)}, u32[]{:S(2)}) collective-permute-start(bf16[3328,128]{1,0:T(8,128)(2,1)S(1)} %collective-permute-done.11.refs_18_.refs_6_), channel_id=1, source_target_pairs={{0,4},{4,0},{8,12},{12,8},{16,20},{20,16},{24,28},{28,24},{1,5},{5... | collective-permute-start | bytes 2555912 | tf_op jit(solution)/shard_map/ppermute | solution.py:232
  111.9 17.2 %collective-permute-start.16 = (bf16[4,1664,128]{2,1,0:T(8,128)(2,1)}, bf16[4,1664,128]{2,1,0:T(8,128)(2,1)}, u32[]{:S(2)}, u32[]{:S(2)}) collective-permute-start(bf16[4,1664,128]{2,1,0:T(8,128)(2,1)} %get-tuple-element.124), channel_id=1, source_target_pairs={{0,4},{4,0},{8,12},{12,8},{16,20},{20,16},{24,28},{28,24},{1,5},{5... | collective-permute-start | bytes 5111816 | tf_op jit(solution)/shard_map/ppermute | solution.py:232
  112.0 12.0 %collective-permute-start.17 = (bf16[4,1664,128]{2,1,0:T(8,128)(2,1)}, bf16[4,1664,128]{2,1,0:T(8,128)(2,1)}, u32[]{:S(2)}, u32[]{:S(2)}) collective-permute-start(bf16[4,1664,128]{2,1,0:T(8,128)(2,1)} %get-tuple-element.125), channel_id=1, source_target_pairs={{0,4},{4,0},{8,12},{12,8},{16,20},{20,16},{24,28},{28,24},{1,5},{5... | collective-permute-start | bytes 5111816 | tf_op jit(solution)/shard_map/ppermute | solution.py:232
  123.4 9.9 %collective-permute-start.15 = (bf16[4,1664,128]{2,1,0:T(8,128)(2,1)}, bf16[4,1664,128]{2,1,0:T(8,128)(2,1)}, u32[]{:S(2)}, u32[]{:S(2)}) collective-permute-start(bf16[4,1664,128]{2,1,0:T(8,128)(2,1)} %get-tuple-element.122), channel_id=1, source_target_pairs={{0,4},{4,0},{8,12},{12,8},{16,20},{20,16},{24,28},{28,24},{1,5},{5... | collective-permute-start | bytes 5111816 | tf_op jit(solution)/shard_map/ppermute | solution.py:232
  123.5 13.9 %collective-permute-start.14 = (bf16[4,1664,128]{2,1,0:T(8,128)(2,1)}, bf16[4,1664,128]{2,1,0:T(8,128)(2,1)}, u32[]{:S(2)}, u32[]{:S(2)}) collective-permute-start(bf16[4,1664,128]{2,1,0:T(8,128)(2,1)} %get-tuple-element.120), channel_id=1, source_target_pairs={{0,4},{4,0},{8,12},{12,8},{16,20},{20,16},{24,28},{28,24},{1,5},{5... | collective-permute-start | bytes 5111816 | tf_op jit(solution)/shard_map/ppermute | solution.py:232
  127.6 27.4 %collective-permute-start.21 = (bf16[2,1664,128]{2,1,0:T(8,128)(2,1)}, bf16[2,1664,128]{2,1,0:T(8,128)(2,1)}, u32[]{:S(2)}, u32[]{:S(2)}) collective-permute-start(bf16[2,1664,128]{2,1,0:T(8,128)(2,1)} %stage_sum.8.refs_2_), channel_id=1, source_target_pairs={{0,8},{4,12},{8,0},{12,4},{16,24},{20,28},{24,16},{28,20},{1,9},{5... | collective-permute-start | bytes 2555912 | tf_op jit(solution)/shard_map/ppermute | solution.py:232
  132.7 26.3 %collective-permute-start.20 = (bf16[2,1664,128]{2,1,0:T(8,128)(2,1)}, bf16[2,1664,128]{2,1,0:T(8,128)(2,1)}, u32[]{:S(2)}, u32[]{:S(2)}) collective-permute-start(bf16[2,1664,128]{2,1,0:T(8,128)(2,1)} %stage_sum.9.refs_2_), channel_id=1, source_target_pairs={{0,16},{4,20},{8,24},{12,28},{16,0},{20,4},{24,8},{28,12},{1,17},{... | collective-permute-start | bytes 2555912 | tf_op jit(solution)/shard_map/ppermute | solution.py:232
  136.9 52.0 %collective-permute-start.19 = (bf16[2,1664,128]{2,1,0:T(8,128)(2,1)}, bf16[2,1664,128]{2,1,0:T(8,128)(2,1)}, u32[]{:S(2)}, u32[]{:S(2)}) collective-permute-start(bf16[2,1664,128]{2,1,0:T(8,128)(2,1)} %stage_sum.10.refs_2_), channel_id=1, source_target_pairs={{0,8},{4,12},{8,0},{12,4},{16,24},{20,28},{24,16},{28,20},{1,9},{5... | collective-permute-start | bytes 2555912 | tf_op jit(solution)/shard_map/ppermute | solution.py:232
  141.0 52.8 %collective-permute-start.18 = (bf16[2,1664,128]{2,1,0:T(8,128)(2,1)}, bf16[2,1664,128]{2,1,0:T(8,128)(2,1)S(1)}, u32[]{:S(2)}, u32[]{:S(2)}) collective-permute-start(bf16[2,1664,128]{2,1,0:T(8,128)(2,1)} %stage_sum.11.refs_9_), channel_id=1, source_target_pairs={{0,16},{4,20},{8,24},{12,28},{16,0},{20,4},{24,8},{28,12},{1,17},{... | collective-permute-start | bytes 2555912 | tf_op jit(solution)/shard_map/ppermute | solution.py:232
  158.4 52.8 %collective-permute-start.25 = (bf16[1,1664,128]{2,1,0:T(8,128)(2,1)}, bf16[1,1664,128]{2,1,0:T(8,128)(2,1)}, u32[]{:S(2)}, u32[]{:S(2)}) collective-permute-start(bf16[1,1664,128]{2,1,0:T(8,128)(2,1)} %stage_sum.12.refs_3_), channel_id=1, source_target_pairs={{0,16},{4,20},{8,24},{12,28},{16,0},{20,4},{24,8},{28,12},{1,17},{... | collective-permute-start | bytes 1277960 | tf_op jit(solution)/shard_map/ppermute | solution.py:232
  162.4 52.0 %collective-permute-start.24 = (bf16[1,1664,128]{2,1,0:T(8,128)(2,1)}, bf16[1,1664,128]{2,1,0:T(8,128)(2,1)}, u32[]{:S(2)}, u32[]{:S(2)}) collective-permute-start(bf16[1,1664,128]{2,1,0:T(8,128)(2,1)} %stage_sum.13.refs_10_), channel_id=1, source_target_pairs={{0,8},{4,12},{8,0},{12,4},{16,24},{20,28},{24,16},{28,20},{1,9},{5... | collective-permute-start | bytes 1277960 | tf_op jit(solution)/shard_map/ppermute | solution.py:232
  192.4 25.3 %collective-permute-start.23 = (bf16[1,1664,128]{2,1,0:T(8,128)(2,1)}, bf16[1,1664,128]{2,1,0:T(8,128)(2,1)}, u32[]{:S(2)}, u32[]{:S(2)}) collective-permute-start(bf16[1,1664,128]{2,1,0:T(8,128)(2,1)} %stage_sum.14.refs_3_), channel_id=1, source_target_pairs={{0,16},{4,20},{8,24},{12,28},{16,0},{20,4},{24,8},{28,12},{1,17},{... | collective-permute-start | bytes 1277960 | tf_op jit(solution)/shard_map/ppermute | solution.py:232
  193.8 0.9 copy-start.1
  198.2 22.6 %collective-permute-start.22 = (bf16[1,1664,128]{2,1,0:T(8,128)(2,1)}, bf16[1,1664,128]{2,1,0:T(8,128)(2,1)S(1)}, u32[]{:S(2)}, u32[]{:S(2)}) collective-permute-start(bf16[1,1664,128]{2,1,0:T(8,128)(2,1)} %stage_sum.15.refs_10_), channel_id=1, source_target_pairs={{0,8},{4,12},{8,0},{12,4},{16,24},{20,28},{24,16},{28,20},{1,9},{5... | collective-permute-start | bytes 1277960 | tf_op jit(solution)/shard_map/ppermute | solution.py:232
  220.8 0.8 copy-start.2

commit v5 on v4

--- a/solution.py
+++ b/solution.py
@@ -49,7 +49,9 @@
         out_shape=[jax.ShapeDtypeStruct(o[0], o[1]) for o in outs],
         input_output_aliases={lead + len(ins) + k: n for k, (n, _) in enumerate(held)},
         compiler_params=pltpu.CompilerParams(vmem_limit_bytes=VMEM_LIMIT),
-        cost_estimate=pl.CostEstimate(flops=flops, bytes_accessed=moved, transcendentals=exps),
+        cost_estimate=pl.CostEstimate(
+            flops=flops, bytes_accessed=moved, transcendentals=exps
+        ),
         name=name,
     )(*([] if at is None else [at]), *arrays)
 
@@ -57,7 +59,7 @@
 def hidden_kernel(gate_ref, up_ref, out_ref):
     gate = gate_ref[...].astype(F32)
     hidden = gate * jax.nn.sigmoid(gate) * up_ref[...].astype(F32)
-    out_ref[...] = jnp.transpose(hidden).astype(BF16)
+    out_ref[...] = jnp.transpose(hidden.astype(BF16))
 
 
 def hidden_transposed(gate, up):
@@ -100,16 +102,24 @@
         if ordering:
             to_order.start()
 
-    part = lax.dot_general(
-        weight_ref[...], dy_ref[...], (((1,), (1,)), ((), ())), preferred_element_type=F32
-    )
+    half = weight_ref.shape[0] // 2
+    parts = [
+        lax.dot_general(
+            weight_ref[pl.ds(n * half, half)],
+            dy_ref[...],
+            (((1,), (1,)), ((), ())),
+            preferred_element_type=F32,
+        )
+        for n in range(2)
+    ]
     first = 0
     for q, count in enumerate(counts):
 
         @pl.when((step >= first) & (step < first + count))
         def _():
-            outs[2 * q][...] = part[:, :block][None]
-            outs[2 * q + 1][...] = part[:, block:].astype(BF16)[None]
+            for n, part in enumerate(parts):
+                outs[2 * q][0, pl.ds(n * half, half)] = part[:, :block]
+                outs[2 * q + 1][0, pl.ds(n * half, half)] = part[:, block:].astype(BF16)
 
         first += count
 
@@ -122,7 +132,7 @@
 
 def hidden_grad_terms(at, sources, weight, first, widths, held, ordered, total, deps):
     block, depth = sources[0].shape[0] // 2, sources[0].shape[1]
-    tall = divisor(math.gcd(first, *widths), 832, 16)
+    tall = divisor(math.gcd(first, *widths), 832, 32)
     counts = [w // tall for w in widths]
     ins = [(weight, pl.BlockSpec((tall, depth), lambda i, at: (first // tall + i, 0)))]
     ins += [(x, pl.BlockSpec(memory_space=pl.ANY)) for x in sources]
@@ -145,19 +155,9 @@
         pltpu.SemaphoreType.DMA,
     ]
     flops = 4 * block * depth * sum(widths)
-    return run(kernel, "hidden_grad_terms", (start,), ins, outs, deps, at, scratch, flops)
-
-
-def stage_kernel(*refs):
-    refs[-1][...] = sum(ref[...].astype(F32) for ref in refs[:-1]).astype(BF16)
-
-
-def stage_sum(terms, rows, deps):
-    width, block = terms[0].shape[1:]
-    tall = divisor(width, 416, 16)
-    ins = [(t, pl.BlockSpec((rows, tall, block), lambda i: (1, i, 0))) for t in terms]
-    out = ((rows, width, block), BF16, pl.BlockSpec((rows, tall, block), lambda i: (0, i, 0)), None)
-    return run(stage_kernel, "stage_sum", (width // tall,), ins, [out], deps)[0]
+    return run(
+        kernel, "hidden_grad_terms", (start,), ins, outs, deps, at, scratch, flops
+    )
 
 
 def finish_kernel(gate_ref, up_ref, *refs):
@@ -185,16 +185,18 @@
 def weight_grad(pieces, dy, whole, total, start, rows, deps):
     block = pieces[0][0].shape[1]
     tokens, depth = dy.shape
-    wide = divisor(depth, 256, 128)
+    tall, wide = divisor(rows, 832, 16), divisor(depth, 512, 128)
 
     def spec(base):
-        return pl.BlockSpec((rows, block), lambda i: ((start - base) // rows, 0))
+        return pl.BlockSpec((tall, block), lambda i, j: ((start - base) // tall + i, 0))
 
     ins = [(x, spec(base)) for x, base in pieces]
-    ins.append((dy, pl.BlockSpec((tokens, wide), lambda i: (0, i))))
-    out = ((total, depth), BF16, pl.BlockSpec((rows, wide), lambda i: (start // rows, i)), whole)
+    ins.append((dy, pl.BlockSpec((tokens, wide), lambda i, j: (0, j))))
+    place = pl.BlockSpec((tall, wide), lambda i, j: (start // tall + i, j))
+    out = ((total, depth), BF16, place, whole)
+    grid = (rows // tall, depth // wide)
     flops = 2 * rows * tokens * depth
-    return run(weight_grad_kernel, "weight_grad", (depth // wide,), ins, [out], deps, flops=flops)[0]
+    return run(weight_grad_kernel, "weight_grad", grid, ins, [out], deps, flops=flops)[0]
 
 
 def arrivals(z, count):
@@ -335,7 +337,12 @@
         if kind == "S":
             bit = streams[n % 2][stages[n]]
             stages[n] += 1
-            send = stage_sum(sums[n], (row_count // 2) >> stages[n], [last])
+            rows = (row_count // 2) >> stages[n]
+            is_whole = last is grad_down
+            sums[n], last = lax.optimization_barrier((sums[n], last))
+            if is_whole:
+                grad_down = last
+            send = sum(t[rows : 2 * rows].astype(F32) for t in sums[n]).astype(BF16)
             sums[n] = sums[n] + [swap(send, bit)]
             return send
         if kind == "F":

time: 227 us -> 217 us (0.956)
  Pallas kernels: 172 us -> 147 us
  other arithmetic: 4.87 us -> 20 us
    pallas_call x22 -> x14, Pallas kernels: 172 us -> 147 us  [run(): pl.pallas_call(body, grid_spec=pltpu.PrefetchScalarGridSpec(num_scalar_pr...]
    convert_element_type x0 -> x8, other arithmetic: none -> 15.1 us  [step(): send = sum((t[rows:2 * rows].astype(F32) for t in sums[n])).astype(BF16)]
  transfers between devices with their start and end apart: 26 -> 26, of which waited for: 4 -> 5; matrix products, arithmetic and copies ran while one was open for 5% -> 12% of each run, Pallas kernels for 73% -> 65%
where the time goes in v5:
time: 217 us; the launch traced here: 215 us
  Pallas kernels  147 us (68%)
  starting transfers between devices  31.3 us (14%)
  other arithmetic  20 us (9%)
  local copies, waits for them, and re-layouts  8.62 us (4%)
  waiting for transfers between devices  6.76 us (3%)
    pallas_call x14, Pallas kernels, run(): pl.pallas_call(body, grid_spec=pltpu.PrefetchScalarGridSpec(num_scalar_pr...  147 us
    convert_element_type x8, other arithmetic, step(): send = sum((t[rows:2 * rows].astype(F32) for t in sums[n])).astype(BF16)  15.1 us
    ppermute x20, starting transfers between devices, swap(): return jax.tree.map(lambda x: lax.ppermute(x, 'row', pairs), x)  13.8 us
    ppermute x3, starting transfers between devices, forward(): lax.ppermute(down[-1], 'col', [(i, i - 1) for i in range(1, col_count - s...  9.89 us
    ppermute x3, starting transfers between devices, forward(): lax.ppermute(up[-1], 'col', [(i, i + 1) for i in range(s - 1, col_count -...  7.65 us
    concatenate x1, other arithmetic, program(): both = [jnp.concatenate(held[a] + held[b])]  4.87 us
  transfers between devices with their start and end apart: 26, of which 5 were waited for; matrix products, arithmetic and copies ran while one was open for 12% of the time, Pallas kernels for 65%

profile of v5, /device:TPU:16, one launch (start us, length us, event | category | flops | bytes accessed | tf_op | source)
XLA Modules:
  0.0 215.0 jit_solution(11067936001037072136)
XLA Ops:
  0.6 4.4 %hidden.1.refs_3_.refs_11_.refs_0_ = bf16[6656,128]{1,0:T(8,128)(2,1)} custom-call(bf16[128,6656]{1,0:T(8,128)(2,1)} %refs_0_.9, bf16[128,6656]{1,0:T(8,128)(2,1)} %refs_1_.19), custom_call_target="tpu_custom_call" | custom-call | bytes 3407872 | tf_op jit(solution)/shard_map/hidden/pallas_call | solution.py:40
  5.1 1.5 collective-permute-start.5
  6.6 1.5 collective-permute-start.4
  8.1 3.5 %collective-permute-start = (bf16[256,2048]{1,0:T(8,128)(2,1)}, bf16[256,2048]{1,0:T(8,128)(2,1)}, u32[]{:S(2)}, u32[]{:S(2)}) collective-permute-start(bf16[256,2048]{1,0:T(8,128)(2,1)} %refs_2_.1), channel_id=1, source_target_pairs={{0,1},{1,2},{2,3},{4,5},{5,6},{6,7},{8,9},{9,10},{10,11},{12,13},{... | collective-permute-start | bytes 3145736 | tf_op jit(solution)/shard_map/ppermute | solution.py:247
  11.5 2.4 %collective-permute-start.1 = (bf16[256,2048]{1,0:T(8,128)(2,1)}, bf16[256,2048]{1,0:T(8,128)(2,1)}, u32[]{:S(2)}, u32[]{:S(2)}) collective-permute-start(bf16[256,2048]{1,0:T(8,128)(2,1)} %refs_2_.1), channel_id=1, source_target_pairs={{1,0},{2,1},{3,2},{5,4},{6,5},{7,6},{9,8},{10,9},{11,10},{13,12},{... | collective-permute-start | bytes 3145736 | tf_op jit(solution)/shard_map/ppermute | solution.py:248
  14.0 0.7 stack.91.refs_0_
  14.7 0.6 stack.86.refs_0_
  15.3 18.3 %hidden_grad_terms.5 = (f32[4,1664,128]{2,1,0:T(8,128)}, bf16[4,1664,128]{2,1,0:T(8,128)(2,1)}, f32[4,1664,128]{2,1,0:T(8,128)}, bf16[4,1664,128]{2,1,0:T(8,128)...) custom-call(s32[6]{0:T(128)} %stack.86.refs_0_, ...), custom_call_target="tpu_custom_call" | custom-call | flops 6979321856 | bytes 28311552 | tf_op jit(solution)/shard_map/hidden_grad_terms/pallas_call | solution.py:40
  33.5 1.7 collective-permute-done.refs_3_
  35.3 3.2 %collective-permute-done.1.refs_2_ = bf16[256,2048]{1,0:T(8,128)(2,1)} collective-permute-done((bf16[256,2048]{1,0:T(8,128)(2,1)}, bf16[256,2048]{1,0:T(8,128)(2,1)}, u32[]{:S(2)}, u32[]{:S(2)}) %collective-permute-start.1) | collective-permute-done | bytes 1048608 | tf_op jit(solution)/shard_map/ppermute | solution.py:248
  38.5 1.9 collective-permute-start.2
  40.4 5.9 %collective-permute-start.3 = (bf16[256,2048]{1,0:T(8,128)(2,1)}, bf16[256,2048]{1,0:T(8,128)(2,1)}, u32[]{:S(2)}, u32[]{:S(2)}) collective-permute-start(bf16[256,2048]{1,0:T(8,128)(2,1)} %collective-permute-done.1.refs_2_), channel_id=1, source_target_pairs={{1,0},{2,1},{5,4},{6,5},{9,8},{10,9},{13,12},{14,13},{17,16},{18,1... | collective-permute-start | bytes 3145736 | tf_op jit(solution)/shard_map/ppermute | solution.py:248
  46.3 18.3 %hidden_grad_terms.6 = (f32[4,1664,128]{2,1,0:T(8,128)}, bf16[4,1664,128]{2,1,0:T(8,128)(2,1)}, f32[4,1664,128]{2,1,0:T(8,128)}, bf16[4,1664,128]{2,1,0:T(8,128)...) custom-call(s32[6]{0:T(128)} %stack.91.refs_0_, ...), custom_call_target="tpu_custom_call", output_to_operand_aliasing={{0}: (4, {}), {1}: (5, {}), {2}: (6, {}), {3}: (7, {}), {4}... | custom-call | flops 6979321856 | bytes 29360128 | tf_op jit(solution)/shard_map/hidden_grad_terms/pallas_call | solution.py:40
  64.6 4.9 %pad_maximum_fusion = bf16[13312,128]{1,0:T(8,128)(2,1)} fusion(bf16[6656,128]{1,0:T(8,128)(2,1)} %collective-permute-done.5.refs_15_.refs_4_, bf16[6656,128]{1,0:T(8,128)(2,1)} %collective-permute-done.4.refs_13_.refs_2_), kind=kLoop, calls=%fused_computation | loop fusion | flops 6815744 | bytes 6815744 | tf_op jit(solution)/shard_map/concatenate | solution.py:301
  69.6 1.6 collective-permute-start.8
  71.2 2.3 %collective-permute-start.7 = (bf16[256,2048]{1,0:T(8,128)(2,1)}, bf16[256,2048]{1,0:T(8,128)(2,1)}, u32[]{:S(2)}, u32[]{:S(2)}) collective-permute-start(bf16[256,2048]{1,0:T(8,128)(2,1)} %collective-permute-done.2.refs_4_), channel_id=1, source_target_pairs={{2,3},{6,7},{10,11},{14,15},{18,19},{22,23},{26,27},{30,31}} | collective-permute-start | bytes 3145736 | tf_op jit(solution)/shard_map/ppermute | solution.py:247
  73.5 2.1 slice.66
  75.6 2.1 slice.67
  78.7 0.7 stack.82.refs_0_
  79.4 0.7 stack.96.refs_0_
  80.0 18.3 %hidden_grad_terms.7 = (f32[4,1664,128]{2,1,0:T(8,128)}, bf16[4,1664,128]{2,1,0:T(8,128)(2,1)}, f32[4,1664,128]{2,1,0:T(8,128)}, bf16[4,1664,128]{2,1,0:T(8,128)...) custom-call(s32[6]{0:T(128)} %stack.96.refs_0_, ...), custom_call_target="tpu_custom_call", output_to_operand_aliasing={{0}: (5, {}), {1}: (6, {}), {2}: (7, {}), {3}: (8, {}), {4}... | custom-call | flops 6979321856 | bytes 30408704 | tf_op jit(solution)/shard_map/hidden_grad_terms/pallas_call | solution.py:40
  98.4 0.8 collective-permute-done.11.refs_18_.refs_6_
  100.1 11.0 %hidden_grad_terms.8 = (f32[4,1664,128]{2,1,0:T(8,128)}, bf16[4,1664,128]{2,1,0:T(8,128)(2,1)}, f32[4,1664,128]{2,1,0:T(8,128)}, bf16[4,1664,128]{2,1,0:T(8,128)(2,1)}, bf16[1024,2048]{1,0:T(8,128)(2,1)}) custom-call(s32[6]{0:T(128)} %stack.82.refs_0_, ...), custom_call_target="tpu_custom_call", output_to_operand_aliasing={{0}: (6, {}), {1}: (7, {}), {2}: (8, {}), {3}: (9, {}), {4}... | custom-call | flops 3489660928 | bytes 31457280 | tf_op jit(solution)/shard_map/hidden_grad_terms/pallas_call | solution.py:40
  111.7 10.9 %hidden_grad_terms.9 = (f32[4,1664,128]{2,1,0:T(8,128)}, bf16[4,1664,128]{2,1,0:T(8,128)(2,1)}, f32[4,1664,128]{2,1,0:T(8,128)}, bf16[4,1664,128]{2,1,0:T(8,128)(2,1)}) custom-call(s32[6]{0:T(128)} %stack.82.refs_0_, bf16[6656,2048]{1,0:T(8,128)(2,1)} %refs_1_.15, ...), custom_call_target="tpu_custom_call", output_to_operand_aliasing={{0}: (6, {}), {1}: (7, {}), {2}: (8, {}), {3}: (9, {})} | custom-call | flops 3489660928 | bytes 31457280 | tf_op jit(solution)/shard_map/hidden_grad_terms/pallas_call | solution.py:40
  123.2 2.9 %add_convert_fusion.3 = bf16[2,1664,128]{2,1,0:T(8,128)(2,1)} fusion(f32[4,1664,128]{2,1,0:T(8,128)} %get-tuple-element.158.refs_10_.refs_2_, bf16[4,1664,128]{2,1,0:T(8,128)(2,1)} %collective-permute-done.17.refs_3_), kind=kLoop, calls=%fused_computation.4 | loop fusion | flops 1277952 | bytes 3407872 | tf_op jit(solution)/shard_map/convert_element_type | solution.py:345
  126.2 1.5 collective-permute-start.20
  127.6 2.4 %add_convert_fusion.2 = bf16[2,1664,128]{2,1,0:T(8,128)(2,1)} fusion(f32[4,1664,128]{2,1,0:T(8,128)S(1)} %copy-done, bf16[4,1664,128]{2,1,0:T(8,128)(2,1)} %collective-permute-done.16.refs_3_), kind=kLoop, calls=%fused_computation.3 | loop fusion | flops 1277952 | bytes 3407872 | tf_op jit(solution)/shard_map/convert_element_type | solution.py:345
  130.1 0.8 collective-permute-start.21
  130.9 1.1 add_convert_fusion.1
  132.7 0.9 copy-done.4
  133.6 1.4 collective-permute-start.18
  135.1 13.3 %weight_grad.4.refs_9_ = bf16[6656,2048]{1,0:T(8,128)(2,1)} custom-call(bf16[6656,128]{1,0:T(8,128)(2,1)} %hidden.1.refs_3_.refs_11_.refs_0_, bf16[6656,128]{1,0:T(8,128)(2,1)} %collective-permute-done.6.refs_13_.refs_12_.refs_1_, bf16[6656,128]{1,0:T(8,128)(2,1)} %collective-permute-done.4.refs_13_.refs_2_, ...), custom_call_target="tpu_custom_call" | custom-call | flops 6979321856 | bytes 19529728 | tf_op jit(solution)/shard_map/weight_grad/pallas_call | solution.py:40
  148.4 2.3 %add_convert_fusion.7 = bf16[1,1664,128]{2,1,0:T(8,128)(2,1)} fusion(f32[4,1664,128]{2,1,0:T(8,128)} %get-tuple-element.158.refs_10_.refs_2_, bf16[2,1664,128]{2,1,0:T(8,128)(2,1)} %collective-permute-done.20.refs_4_, bf16[4,1664,128]{2,1,0:T(8,128)(2,1)} %collective-permute-done.17.refs_3_), kind=kLoop, calls=%fused_computation.8 | loop fusion | flops 1064960 | bytes 2129920 | tf_op jit(solution)/shard_map/convert_element_type | solution.py:345
  150.7 0.9 collective-permute-start.25
  152.2 2.3 %add_convert_fusion.6.refs_10_ = bf16[1,1664,128]{2,1,0:T(8,128)(2,1)} fusion(f32[4,1664,128]{2,1,0:T(8,128)} %get-tuple-element.161.refs_2_, bf16[2,1664,128]{2,1,0:T(8,128)(2,1)} %collective-permute-done.21.refs_4_, bf16[4,1664,128]{2,1,0:T(8,128)(2,1)} %collective-permute-done.16.refs_3_), kind=kLoop, calls=%fused_computation.7 | loop fusion | flops 1064960 | bytes 2129920 | tf_op jit(solution)/shard_map/convert_element_type | solution.py:345
  154.6 0.9 collective-permute-start.24
  155.5 13.3 %weight_grad.5.refs_9_ = bf16[6656,2048]{1,0:T(8,128)(2,1)} custom-call(bf16[6656,128]{1,0:T(8,128)(2,1)} %hidden.1.refs_3_.refs_11_.refs_0_, bf16[6656,128]{1,0:T(8,128)(2,1)} %collective-permute-done.6.refs_13_.refs_12_.refs_1_, bf16[6656,128]{1,0:T(8,128)(2,1)} %collective-permute-done.4.refs_13_.refs_2_, ...), custom_call_target="tpu_custom_call", output_to_operand_aliasing={{}: (9, {})} | custom-call | flops 6979321856 | bytes 19529728 | tf_op jit(solution)/shard_map/weight_grad/pallas_call | solution.py:40
  168.8 13.4 %weight_grad.6.refs_9_ = bf16[6656,2048]{1,0:T(8,128)(2,1)} custom-call(bf16[6656,128]{1,0:T(8,128)(2,1)} %hidden.1.refs_3_.refs_11_.refs_0_, bf16[6656,128]{1,0:T(8,128)(2,1)} %collective-permute-done.6.refs_13_.refs_12_.refs_1_, bf16[6656,128]{1,0:T(8,128)(2,1)} %collective-permute-done.4.refs_13_.refs_2_, ...), custom_call_target="tpu_custom_call", output_to_operand_aliasing={{}: (9, {})} | custom-call | flops 6979321856 | bytes 19529728 | tf_op jit(solution)/shard_map/weight_grad/pallas_call | solution.py:40
  182.2 2.3 %add_convert_fusion.5 = bf16[1,1664,128]{2,1,0:T(8,128)(2,1)} fusion(f32[4,1664,128]{2,1,0:T(8,128)} %get-tuple-element.164.refs_2_, bf16[2,1664,128]{2,1,0:T(8,128)(2,1)} %collective-permute-done.19.refs_4_, bf16[4,1664,128]{2,1,0:T(8,128)(2,1)} %copy-done.5), kind=kLoop, calls=%fused_computation.6 | loop fusion | flops 1064960 | bytes 2129920 | tf_op jit(solution)/shard_map/convert_element_type | solution.py:345
  184.5 1.1 collective-permute-start.23
  185.6 1.5 add_convert_fusion.4.refs_10_
  187.1 0.9 collective-permute-start.22
  188.0 13.4 %weight_grad.7.refs_6_ = bf16[6656,2048]{1,0:T(8,128)(2,1)} custom-call(bf16[6656,128]{1,0:T(8,128)(2,1)} %hidden.1.refs_3_.refs_11_.refs_0_, bf16[6656,128]{1,0:T(8,128)(2,1)} %collective-permute-done.6.refs_13_.refs_12_.refs_1_, bf16[6656,128]{1,0:T(8,128)(2,1)} %collective-permute-done.4.refs_13_.refs_2_, ...), custom_call_target="tpu_custom_call", output_to_operand_aliasing={{}: (9, {})} | custom-call | flops 6979321856 | bytes 19529728 | tf_op jit(solution)/shard_map/weight_grad/pallas_call | solution.py:40
  201.4 3.2 %finish.4 = (bf16[128,6656]{1,0:T(8,128)(2,1)}, bf16[128,6656]{1,0:T(8,128)(2,1)}) custom-call(bf16[128,6656]{1,0:T(8,128)(2,1)} %refs_0_.9, bf16[128,6656]{1,0:T(8,128)(2,1)} %refs_1_.19, f32[4,1664,128]{2,1,0:T(8,128)} %get-tuple-element.158.refs_10_.refs_2_, bf16[4,1664,128]{2,1,0:T(8,128)(2,1)} %collective-permute-done.17.refs_3_, ...), custom_call_target="tpu_custom_call" | custom-call | bytes 9797632 | tf_op jit(solution)/shard_map/finish/pallas_call | solution.py:40
  204.6 3.2 %finish.5 = (bf16[128,6656]{1,0:T(8,128)(2,1)}, bf16[128,6656]{1,0:T(8,128)(2,1)}) custom-call(bf16[128,6656]{1,0:T(8,128)(2,1)} %refs_0_.9, bf16[128,6656]{1,0:T(8,128)(2,1)} %refs_1_.19, f32[4,1664,128]{2,1,0:T(8,128)} %get-tuple-element.161.refs_2_, ...), custom_call_target="tpu_custom_call", output_to_operand_aliasing={{0}: (6, {}), {1}: (7, {})} | custom-call | bytes 9797632 | tf_op jit(solution)/shard_map/finish/pallas_call | solution.py:40
  207.8 3.2 %finish.6 = (bf16[128,6656]{1,0:T(8,128)(2,1)}, bf16[128,6656]{1,0:T(8,128)(2,1)}) custom-call(bf16[128,6656]{1,0:T(8,128)(2,1)} %refs_0_.9, bf16[128,6656]{1,0:T(8,128)(2,1)} %refs_1_.19, f32[4,1664,128]{2,1,0:T(8,128)} %get-tuple-element.164.refs_2_, bf16[4,1664,128]{2,1,0:T(8,128)(2,1)} %copy-done.5, ...), custom_call_target="tpu_custom_call", output_to_operand_aliasing={{0}: (6, {}), {1}: (7, {})} | custom-call | bytes 9797632 | tf_op jit(solution)/shard_map/finish/pallas_call | solution.py:40
  211.1 0.8 copy-done.8
  211.8 3.2 %finish.7 = (bf16[128,6656]{1,0:T(8,128)(2,1)}, bf16[128,6656]{1,0:T(8,128)(2,1)}) custom-call(bf16[128,6656]{1,0:T(8,128)(2,1)} %refs_0_.9, bf16[128,6656]{1,0:T(8,128)(2,1)} %refs_1_.19, f32[4,1664,128]{2,1,0:T(8,128)} %get-tuple-element.167.refs_2_, bf16[4,1664,128]{2,1,0:T(8,128)(2,1)} %copy-done.4, ...), custom_call_target="tpu_custom_call", output_to_operand_aliasing={{0}: (6, {}), {1}: (7, {})} | custom-call | bytes 9797632 | tf_op jit(solution)/shard_map/finish/pallas_call | solution.py:40
  (51 shorter events, 4.5 us)
Async XLA Ops:
  5.0 41.3 %collective-permute-start.6 = (bf16[6656,128]{1,0:T(8,128)(2,1)}, bf16[6656,128]{1,0:T(8,128)(2,1)}, u32[]{:S(2)}, u32[]{:S(2)}) collective-permute-start(bf16[6656,128]{1,0:T(8,128)(2,1)} %hidden.1.refs_3_.refs_11_.refs_0_), channel_id=1, source_target_pairs={{0,4},{4,0},{8,12},{12,8},{16,20},{20,16},{24,28},{28,24},{1,5},{5... | collective-permute-start | bytes 5111816 | tf_op jit(solution)/shard_map/ppermute | solution.py:234
  5.1 59.5 %collective-permute-start.5 = (bf16[6656,128]{1,0:T(8,128)(2,1)}, bf16[6656,128]{1,0:T(8,128)(2,1)}, u32[]{:S(2)}, u32[]{:S(2)}) collective-permute-start(bf16[6656,128]{1,0:T(8,128)(2,1)} %hidden.1.refs_3_.refs_11_.refs_0_), channel_id=1, source_target_pairs={{0,16},{4,20},{8,24},{12,28},{16,0},{20,4},{24,8},{28,12},{1,17},{... | collective-permute-start | bytes 5111816 | tf_op jit(solution)/shard_map/ppermute | solution.py:234
  6.6 58.0 %collective-permute-start.4 = (bf16[6656,128]{1,0:T(8,128)(2,1)}, bf16[6656,128]{1,0:T(8,128)(2,1)}, u32[]{:S(2)}, u32[]{:S(2)}) collective-permute-start(bf16[6656,128]{1,0:T(8,128)(2,1)} %hidden.1.refs_3_.refs_11_.refs_0_), channel_id=1, source_target_pairs={{0,8},{4,12},{8,0},{12,4},{16,24},{20,28},{24,16},{28,20},{1,9},{5... | collective-permute-start | bytes 5111816 | tf_op jit(solution)/shard_map/ppermute | solution.py:234
  8.1 27.2 %collective-permute-start = (bf16[256,2048]{1,0:T(8,128)(2,1)}, bf16[256,2048]{1,0:T(8,128)(2,1)}, u32[]{:S(2)}, u32[]{:S(2)}) collective-permute-start(bf16[256,2048]{1,0:T(8,128)(2,1)} %refs_2_.1), channel_id=1, source_target_pairs={{0,1},{1,2},{2,3},{4,5},{5,6},{6,7},{8,9},{9,10},{10,11},{12,13},{... | collective-permute-start | bytes 3145736 | tf_op jit(solution)/shard_map/ppermute | solution.py:247
  11.5 26.9 %collective-permute-start.1 = (bf16[256,2048]{1,0:T(8,128)(2,1)}, bf16[256,2048]{1,0:T(8,128)(2,1)}, u32[]{:S(2)}, u32[]{:S(2)}) collective-permute-start(bf16[256,2048]{1,0:T(8,128)(2,1)} %refs_2_.1), channel_id=1, source_target_pairs={{1,0},{2,1},{3,2},{5,4},{6,5},{7,6},{9,8},{10,9},{11,10},{13,12},{... | collective-permute-start | bytes 3145736 | tf_op jit(solution)/shard_map/ppermute | solution.py:248
  38.5 31.0 %collective-permute-start.2 = (bf16[256,2048]{1,0:T(8,128)(2,1)}, bf16[256,2048]{1,0:T(8,128)(2,1)}, u32[]{:S(2)}, u32[]{:S(2)}) collective-permute-start(bf16[256,2048]{1,0:T(8,128)(2,1)} %collective-permute-done.refs_3_), channel_id=1, source_target_pairs={{1,2},{2,3},{5,6},{6,7},{9,10},{10,11},{13,14},{14,15},{17,18},{18... | collective-permute-start | bytes 3145736 | tf_op jit(solution)/shard_map/ppermute | solution.py:247
  40.4 29.1 %collective-permute-start.3 = (bf16[256,2048]{1,0:T(8,128)(2,1)}, bf16[256,2048]{1,0:T(8,128)(2,1)}, u32[]{:S(2)}, u32[]{:S(2)}) collective-permute-start(bf16[256,2048]{1,0:T(8,128)(2,1)} %collective-permute-done.1.refs_2_), channel_id=1, source_target_pairs={{1,0},{2,1},{5,4},{6,5},{9,8},{10,9},{13,12},{14,13},{17,16},{18,1... | collective-permute-start | bytes 3145736 | tf_op jit(solution)/shard_map/ppermute | solution.py:248
  69.5 30.1 %collective-permute-start.9 = (bf16[13312,128]{1,0:T(8,128)(2,1)}, bf16[13312,128]{1,0:T(8,128)(2,1)}, u32[]{:S(2)}, u32[]{:S(2)}) collective-permute-start(bf16[13312,128]{1,0:T(8,128)(2,1)} %pad_maximum_fusion), channel_id=1, source_target_pairs={{0,4},{4,0},{8,12},{12,8},{16,20},{20,16},{24,28},{28,24},{1,5},{5... | collective-permute-start | bytes 10223624 | tf_op jit(solution)/shard_map/ppermute | solution.py:234
  69.6 28.8 %collective-permute-start.8 = (bf16[256,2048]{1,0:T(8,128)(2,1)}, bf16[256,2048]{1,0:T(8,128)(2,1)}, u32[]{:S(2)}, u32[]{:S(2)}) collective-permute-start(bf16[256,2048]{1,0:T(8,128)(2,1)} %collective-permute-done.3.refs_3_.refs_2_), channel_id=1, source_target_pairs={{1,0},{5,4},{9,8},{13,12},{17,16},{21,20},{25,24},{29,28}} | collective-permute-start | bytes 3145736 | tf_op jit(solution)/shard_map/ppermute | solution.py:248
  71.2 27.2 %collective-permute-start.7 = (bf16[256,2048]{1,0:T(8,128)(2,1)}, bf16[256,2048]{1,0:T(8,128)(2,1)}, u32[]{:S(2)}, u32[]{:S(2)}) collective-permute-start(bf16[256,2048]{1,0:T(8,128)(2,1)} %collective-permute-done.2.refs_4_), channel_id=1, source_target_pairs={{2,3},{6,7},{10,11},{14,15},{18,19},{22,23},{26,27},{30,31}} | collective-permute-start | bytes 3145736 | tf_op jit(solution)/shard_map/ppermute | solution.py:247
  77.7 21.5 %collective-permute-start.11 = (bf16[3328,128]{1,0:T(8,128)(2,1)}, bf16[3328,128]{1,0:T(8,128)(2,1)S(1)}, u32[]{:S(2)}, u32[]{:S(2)}) collective-permute-start(bf16[3328,128]{1,0:T(8,128)(2,1)} %slice.67), channel_id=1, source_target_pairs={{0,8},{4,12},{8,0},{12,4},{16,24},{20,28},{24,16},{28,20},{1,9},{5... | collective-permute-start | bytes 2555912 | tf_op jit(solution)/shard_map/ppermute | solution.py:234
  78.2 21.4 %collective-permute-start.10 = (bf16[3328,128]{1,0:T(8,128)(2,1)}, bf16[3328,128]{1,0:T(8,128)(2,1)}, u32[]{:S(2)}, u32[]{:S(2)}) collective-permute-start(bf16[3328,128]{1,0:T(8,128)(2,1)} %slice.66), channel_id=1, source_target_pairs={{0,16},{4,20},{8,24},{12,28},{16,0},{20,4},{24,8},{28,12},{1,17},{... | collective-permute-start | bytes 2555912 | tf_op jit(solution)/shard_map/ppermute | solution.py:234
  99.2 0.9 copy-start.3
  99.6 12.1 %collective-permute-start.12 = (bf16[3328,128]{1,0:T(8,128)(2,1)}, bf16[3328,128]{1,0:T(8,128)(2,1)}, u32[]{:S(2)}, u32[]{:S(2)}) collective-permute-start(bf16[3328,128]{1,0:T(8,128)(2,1)} %collective-permute-done.10.refs_17_.refs_6_), channel_id=1, source_target_pairs={{0,4},{4,0},{8,12},{12,8},{16,20},{20,16},{24,28},{28,24},{1,5},{5... | collective-permute-start | bytes 2555912 | tf_op jit(solution)/shard_map/ppermute | solution.py:234
  99.6 12.1 %collective-permute-start.13 = (bf16[3328,128]{1,0:T(8,128)(2,1)S(1)}, bf16[3328,128]{1,0:T(8,128)(2,1)}, u32[]{:S(2)}, u32[]{:S(2)}) collective-permute-start(bf16[3328,128]{1,0:T(8,128)(2,1)S(1)} %collective-permute-done.11.refs_18_.refs_6_), channel_id=1, source_target_pairs={{0,4},{4,0},{8,12},{12,8},{16,20},{20,16},{24,28},{28,24},{1,5},{5... | collective-permute-start | bytes 2555912 | tf_op jit(solution)/shard_map/ppermute | solution.py:234
  111.1 12.1 %collective-permute-start.17 = (bf16[4,1664,128]{2,1,0:T(8,128)(2,1)}, bf16[4,1664,128]{2,1,0:T(8,128)(2,1)}, u32[]{:S(2)}, u32[]{:S(2)}) collective-permute-start(bf16[4,1664,128]{2,1,0:T(8,128)(2,1)} %get-tuple-element.147), channel_id=1, source_target_pairs={{0,4},{4,0},{8,12},{12,8},{16,20},{20,16},{24,28},{28,24},{1,5},{5... | collective-permute-start | bytes 5111816 | tf_op jit(solution)/shard_map/ppermute | solution.py:234
  111.2 16.4 %collective-permute-start.16 = (bf16[4,1664,128]{2,1,0:T(8,128)(2,1)}, bf16[4,1664,128]{2,1,0:T(8,128)(2,1)}, u32[]{:S(2)}, u32[]{:S(2)}) collective-permute-start(bf16[4,1664,128]{2,1,0:T(8,128)(2,1)} %get-tuple-element.146), channel_id=1, source_target_pairs={{0,4},{4,0},{8,12},{12,8},{16,20},{20,16},{24,28},{28,24},{1,5},{5... | collective-permute-start | bytes 5111816 | tf_op jit(solution)/shard_map/ppermute | solution.py:234
  122.6 8.3 %collective-permute-start.15 = (bf16[4,1664,128]{2,1,0:T(8,128)(2,1)}, bf16[4,1664,128]{2,1,0:T(8,128)(2,1)S(1)}, u32[]{:S(2)}, u32[]{:S(2)}) collective-permute-start(bf16[4,1664,128]{2,1,0:T(8,128)(2,1)} %get-tuple-element.144), channel_id=1, source_target_pairs={{0,4},{4,0},{8,12},{12,8},{16,20},{20,16},{24,28},{28,24},{1,5},{5... | collective-permute-start | bytes 5111816 | tf_op jit(solution)/shard_map/ppermute | solution.py:234
  122.8 9.7 %collective-permute-start.14 = (bf16[4,1664,128]{2,1,0:T(8,128)(2,1)}, bf16[4,1664,128]{2,1,0:T(8,128)(2,1)S(1)}, u32[]{:S(2)}, u32[]{:S(2)}) collective-permute-start(bf16[4,1664,128]{2,1,0:T(8,128)(2,1)} %get-tuple-element.142), channel_id=1, source_target_pairs={{0,4},{4,0},{8,12},{12,8},{16,20},{20,16},{24,28},{28,24},{1,5},{5... | collective-permute-start | bytes 5111816 | tf_op jit(solution)/shard_map/ppermute | solution.py:234
  123.2 4.4 %copy-start = (f32[4,1664,128]{2,1,0:T(8,128)S(1)}, f32[4,1664,128]{2,1,0:T(8,128)}, u32[]{:S(2)}) copy-start(f32[4,1664,128]{2,1,0:T(8,128)} %get-tuple-element.161.refs_2_) | copy-start | bytes 10223620
  126.2 22.3 %collective-permute-start.20 = (bf16[2,1664,128]{2,1,0:T(8,128)(2,1)}, bf16[2,1664,128]{2,1,0:T(8,128)(2,1)}, u32[]{:S(2)}, u32[]{:S(2)}) collective-permute-start(bf16[2,1664,128]{2,1,0:T(8,128)(2,1)} %add_convert_fusion.3), channel_id=1, source_target_pairs={{0,8},{4,12},{8,0},{12,4},{16,24},{20,28},{24,16},{28,20},{1,9},{5... | collective-permute-start | bytes 2555912 | tf_op jit(solution)/shard_map/ppermute | solution.py:234
  127.6 3.3 %copy-start.1 = (f32[4,1664,128]{2,1,0:T(8,128)S(1)}, f32[4,1664,128]{2,1,0:T(8,128)}, u32[]{:S(2)}) copy-start(f32[4,1664,128]{2,1,0:T(8,128)} %get-tuple-element.164.refs_2_) | copy-start | bytes 10223620
  130.1 2.5 %copy-start.2 = (f32[4,1664,128]{2,1,0:T(8,128)S(1)}, f32[4,1664,128]{2,1,0:T(8,128)}, u32[]{:S(2)}) copy-start(f32[4,1664,128]{2,1,0:T(8,128)} %get-tuple-element.167.refs_2_) | copy-start | bytes 10223620
  130.1 22.2 %collective-permute-start.21 = (bf16[2,1664,128]{2,1,0:T(8,128)(2,1)}, bf16[2,1664,128]{2,1,0:T(8,128)(2,1)}, u32[]{:S(2)}, u32[]{:S(2)}) collective-permute-start(bf16[2,1664,128]{2,1,0:T(8,128)(2,1)} %add_convert_fusion.2), channel_id=1, source_target_pairs={{0,16},{4,20},{8,24},{12,28},{16,0},{20,4},{24,8},{28,12},{1,17},{... | collective-permute-start | bytes 2555912 | tf_op jit(solution)/shard_map/ppermute | solution.py:234
  130.9 1.6 copy-start.5
  132.0 50.2 %collective-permute-start.19 = (bf16[2,1664,128]{2,1,0:T(8,128)(2,1)}, bf16[2,1664,128]{2,1,0:T(8,128)(2,1)}, u32[]{:S(2)}, u32[]{:S(2)}) collective-permute-start(bf16[2,1664,128]{2,1,0:T(8,128)(2,1)} %add_convert_fusion.1), channel_id=1, source_target_pairs={{0,8},{4,12},{8,0},{12,4},{16,24},{20,28},{24,16},{28,20},{1,9},{5... | collective-permute-start | bytes 2555912 | tf_op jit(solution)/shard_map/ppermute | solution.py:234
  132.5 1.2 copy-start.4
  133.6 1.4 copy-start.6
  133.6 51.9 %collective-permute-start.18 = (bf16[2,1664,128]{2,1,0:T(8,128)(2,1)S(1)}, bf16[2,1664,128]{2,1,0:T(8,128)(2,1)}, u32[]{:S(2)}, u32[]{:S(2)}) collective-permute-start(bf16[2,1664,128]{2,1,0:T(8,128)(2,1)S(1)} %add_convert_fusion.refs_9_), channel_id=1, source_target_pairs={{0,16},{4,20},{8,24},{12,28},{16,0},{20,4},{24,8},{28,12},{1,17},{... | collective-permute-start | bytes 2555912 | tf_op jit(solution)/shard_map/ppermute | solution.py:234
  150.7 50.7 %collective-permute-start.25 = (bf16[1,1664,128]{2,1,0:T(8,128)(2,1)}, bf16[1,1664,128]{2,1,0:T(8,128)(2,1)}, u32[]{:S(2)}, u32[]{:S(2)}) collective-permute-start(bf16[1,1664,128]{2,1,0:T(8,128)(2,1)} %add_convert_fusion.7), channel_id=1, source_target_pairs={{0,16},{4,20},{8,24},{12,28},{16,0},{20,4},{24,8},{28,12},{1,17},{... | collective-permute-start | bytes 1277960 | tf_op jit(solution)/shard_map/ppermute | solution.py:234
  154.6 50.0 %collective-permute-start.24 = (bf16[1,1664,128]{2,1,0:T(8,128)(2,1)}, bf16[1,1664,128]{2,1,0:T(8,128)(2,1)}, u32[]{:S(2)}, u32[]{:S(2)}) collective-permute-start(bf16[1,1664,128]{2,1,0:T(8,128)(2,1)} %add_convert_fusion.6.refs_10_), channel_id=1, source_target_pairs={{0,8},{4,12},{8,0},{12,4},{16,24},{20,28},{24,16},{28,20},{1,9},{5... | collective-permute-start | bytes 1277960 | tf_op jit(solution)/shard_map/ppermute | solution.py:234
  184.5 23.4 %collective-permute-start.23 = (bf16[1,1664,128]{2,1,0:T(8,128)(2,1)}, bf16[1,1664,128]{2,1,0:T(8,128)(2,1)}, u32[]{:S(2)}, u32[]{:S(2)}) collective-permute-start(bf16[1,1664,128]{2,1,0:T(8,128)(2,1)} %add_convert_fusion.5), channel_id=1, source_target_pairs={{0,16},{4,20},{8,24},{12,28},{16,0},{20,4},{24,8},{28,12},{1,17},{... | collective-permute-start | bytes 1277960 | tf_op jit(solution)/shard_map/ppermute | solution.py:234
  187.1 0.9 copy-start.7
  187.1 23.9 %collective-permute-start.22 = (bf16[1,1664,128]{2,1,0:T(8,128)(2,1)S(1)}, bf16[1,1664,128]{2,1,0:T(8,128)(2,1)S(1)}, u32[]{:S(2)}, u32[]{:S(2)}) collective-permute-start(bf16[1,1664,128]{2,1,0:T(8,128)(2,1)S(1)} %add_convert_fusion.4.refs_10_), channel_id=1, source_target_pairs={{0,8},{4,12},{8,0},{12,4},{16,24},{20,28},{24,16},{28,20},{1,9},{5... | collective-permute-start | bytes 1277960 | tf_op jit(solution)/shard_map/ppermute | solution.py:234
  211.0 0.8 copy-start.8

commit v6 on v5

--- a/solution.py
+++ b/solution.py
@@ -71,8 +71,8 @@
 
 
 def product_kernel(choices, counts, ordering, at_ref, weight_ref, *refs):
-    sources, outs = refs[:choices], refs[choices:-3]
-    dy_ref, sems, out_sem = refs[-3:]
+    sources, outs = refs[:choices], refs[choices:-4]
+    dy_ref, turned_ref, sems, out_sem = refs[-4:]
     step = pl.program_id(0)
     block = dy_ref.shape[0] // 2
     to_order = None
@@ -101,25 +101,16 @@
 
         if ordering:
             to_order.start()
-
-    half = weight_ref.shape[0] // 2
-    parts = [
-        lax.dot_general(
-            weight_ref[pl.ds(n * half, half)],
-            dy_ref[...],
-            (((1,), (1,)), ((), ())),
-            preferred_element_type=F32,
-        )
-        for n in range(2)
-    ]
+        turned_ref[...] = jnp.transpose(dy_ref[...])
+
+    part = jnp.dot(weight_ref[...], turned_ref[...], preferred_element_type=F32)
     first = 0
     for q, count in enumerate(counts):
 
         @pl.when((step >= first) & (step < first + count))
         def _():
-            for n, part in enumerate(parts):
-                outs[2 * q][0, pl.ds(n * half, half)] = part[:, :block]
-                outs[2 * q + 1][0, pl.ds(n * half, half)] = part[:, block:].astype(BF16)
+            outs[2 * q][...] = part[:, :block][None]
+            outs[2 * q + 1][...] = part[:, block:].astype(BF16)[None]
 
         first += count
 
@@ -132,7 +123,7 @@
 
 def hidden_grad_terms(at, sources, weight, first, widths, held, ordered, total, deps):
     block, depth = sources[0].shape[0] // 2, sources[0].shape[1]
-    tall = divisor(math.gcd(first, *widths), 832, 32)
+    tall = divisor(math.gcd(first, *widths), 832, 16)
     counts = [w // tall for w in widths]
     ins = [(weight, pl.BlockSpec((tall, depth), lambda i, at: (first // tall + i, 0)))]
     ins += [(x, pl.BlockSpec(memory_space=pl.ANY)) for x in sources]
@@ -151,6 +142,7 @@
     kernel = functools.partial(product_kernel, len(sources), counts, ordered is not None)
     scratch = [
         pltpu.VMEM((2 * block, depth), BF16),
+        pltpu.VMEM((depth, 2 * block), BF16),
         pltpu.SemaphoreType.DMA((2,)),
         pltpu.SemaphoreType.DMA,
     ]
@@ -185,7 +177,7 @@
 def weight_grad(pieces, dy, whole, total, start, rows, deps):
     block = pieces[0][0].shape[1]
     tokens, depth = dy.shape
-    tall, wide = divisor(rows, 832, 16), divisor(depth, 512, 128)
+    tall, wide = divisor(rows, 832, 16), divisor(depth, 1024, 128)
 
     def spec(base):
         return pl.BlockSpec((tall, block), lambda i, j: ((start - base) // tall + i, 0))

time: 217 us -> 213 us (0.982)
  Pallas kernels: 147 us -> 144 us
    pallas_call x14, Pallas kernels: 147 us -> 144 us  [run(): pl.pallas_call(body, grid_spec=pltpu.PrefetchScalarGridSpec(num_scalar_pr...]
  transfers between devices with their start and end apart: 26 -> 26, of which waited for: 5 -> 6; matrix products, arithmetic and copies ran while one was open for 12% -> 13% of each run, Pallas kernels for 65% -> 64%
where the time goes in v6:
time: 213 us; the launch traced here: 212 us
  Pallas kernels  144 us (68%)
  starting transfers between devices  31.4 us (15%)
  other arithmetic  20 us (9%)
  local copies, waits for them, and re-layouts  8.62 us (4%)
  waiting for transfers between devices  7.71 us (4%)
    pallas_call x14, Pallas kernels, run(): pl.pallas_call(body, grid_spec=pltpu.PrefetchScalarGridSpec(num_scalar_pr...  144 us
    convert_element_type x8, other arithmetic, step(): send = sum((t[rows:2 * rows].astype(F32) for t in sums[n])).astype(BF16)  15.1 us
    ppermute x20, starting transfers between devices, swap(): return jax.tree.map(lambda x: lax.ppermute(x, 'row', pairs), x)  13.9 us
    ppermute x3, starting transfers between devices, forward(): lax.ppermute(down[-1], 'col', [(i, i - 1) for i in range(1, col_count - s...  9.89 us
    ppermute x3, starting transfers between devices, forward(): lax.ppermute(up[-1], 'col', [(i, i + 1) for i in range(s - 1, col_count -...  7.65 us
    concatenate x1, other arithmetic, program(): both = [jnp.concatenate(held[a] + held[b])]  4.87 us
  transfers between devices with their start and end apart: 26, of which 6 were waited for; matrix products, arithmetic and copies ran while one was open for 13% of the time, Pallas kernels for 64%

profile of v6, /device:TPU:16, one launch (start us, length us, event | category | flops | bytes accessed | tf_op | source)
XLA Modules:
  0.0 212.1 jit_solution(17840264004287393641)
XLA Ops:
  0.6 4.4 %hidden.1.refs_3_.refs_11_.refs_0_ = bf16[6656,128]{1,0:T(8,128)(2,1)} custom-call(bf16[128,6656]{1,0:T(8,128)(2,1)} %refs_0_.9, bf16[128,6656]{1,0:T(8,128)(2,1)} %refs_1_.19), custom_call_target="tpu_custom_call" | custom-call | bytes 3407872 | tf_op jit(solution)/shard_map/hidden/pallas_call | solution.py:40
  5.1 1.5 collective-permute-start.5
  6.6 1.5 collective-permute-start.4
  8.1 3.5 %collective-permute-start = (bf16[256,2048]{1,0:T(8,128)(2,1)}, bf16[256,2048]{1,0:T(8,128)(2,1)}, u32[]{:S(2)}, u32[]{:S(2)}) collective-permute-start(bf16[256,2048]{1,0:T(8,128)(2,1)} %refs_2_.1), channel_id=1, source_target_pairs={{0,1},{1,2},{2,3},{4,5},{5,6},{6,7},{8,9},{9,10},{10,11},{12,13},{... | collective-permute-start | bytes 3145736 | tf_op jit(solution)/shard_map/ppermute | solution.py:239
  11.5 2.4 %collective-permute-start.1 = (bf16[256,2048]{1,0:T(8,128)(2,1)}, bf16[256,2048]{1,0:T(8,128)(2,1)}, u32[]{:S(2)}, u32[]{:S(2)}) collective-permute-start(bf16[256,2048]{1,0:T(8,128)(2,1)} %refs_2_.1), channel_id=1, source_target_pairs={{1,0},{2,1},{3,2},{5,4},{6,5},{7,6},{9,8},{10,9},{11,10},{13,12},{... | collective-permute-start | bytes 3145736 | tf_op jit(solution)/shard_map/ppermute | solution.py:240
  14.0 0.7 stack.91.refs_0_
  15.3 18.5 %hidden_grad_terms.5 = (f32[4,1664,128]{2,1,0:T(8,128)}, bf16[4,1664,128]{2,1,0:T(8,128)(2,1)}, f32[4,1664,128]{2,1,0:T(8,128)}, bf16[4,1664,128]{2,1,0:T(8,128)...) custom-call(s32[6]{0:T(128)} %stack.86.refs_0_, ...), custom_call_target="tpu_custom_call" | custom-call | flops 6979321856 | bytes 28311552 | tf_op jit(solution)/shard_map/hidden_grad_terms/pallas_call | solution.py:40
  33.7 1.5 collective-permute-done.refs_3_
  35.3 3.2 %collective-permute-done.1.refs_2_ = bf16[256,2048]{1,0:T(8,128)(2,1)} collective-permute-done((bf16[256,2048]{1,0:T(8,128)(2,1)}, bf16[256,2048]{1,0:T(8,128)(2,1)}, u32[]{:S(2)}, u32[]{:S(2)}) %collective-permute-start.1) | collective-permute-done | bytes 1048608 | tf_op jit(solution)/shard_map/ppermute | solution.py:240
  38.5 1.9 collective-permute-start.2
  40.4 5.9 %collective-permute-start.3 = (bf16[256,2048]{1,0:T(8,128)(2,1)}, bf16[256,2048]{1,0:T(8,128)(2,1)}, u32[]{:S(2)}, u32[]{:S(2)}) collective-permute-start(bf16[256,2048]{1,0:T(8,128)(2,1)} %collective-permute-done.1.refs_2_), channel_id=1, source_target_pairs={{1,0},{2,1},{5,4},{6,5},{9,8},{10,9},{13,12},{14,13},{17,16},{18,1... | collective-permute-start | bytes 3145736 | tf_op jit(solution)/shard_map/ppermute | solution.py:240
  46.3 18.5 %hidden_grad_terms.6 = (f32[4,1664,128]{2,1,0:T(8,128)}, bf16[4,1664,128]{2,1,0:T(8,128)(2,1)}, f32[4,1664,128]{2,1,0:T(8,128)}, bf16[4,1664,128]{2,1,0:T(8,128)...) custom-call(s32[6]{0:T(128)} %stack.91.refs_0_, ...), custom_call_target="tpu_custom_call", output_to_operand_aliasing={{0}: (4, {}), {1}: (5, {}), {2}: (6, {}), {3}: (7, {}), {4}... | custom-call | flops 6979321856 | bytes 29360128 | tf_op jit(solution)/shard_map/hidden_grad_terms/pallas_call | solution.py:40
  64.8 4.9 %pad_maximum_fusion = bf16[13312,128]{1,0:T(8,128)(2,1)} fusion(bf16[6656,128]{1,0:T(8,128)(2,1)} %collective-permute-done.5.refs_15_.refs_4_, bf16[6656,128]{1,0:T(8,128)(2,1)} %collective-permute-done.4.refs_13_.refs_2_), kind=kLoop, calls=%fused_computation | loop fusion | flops 6815744 | bytes 6815744 | tf_op jit(solution)/shard_map/concatenate | solution.py:293
  69.8 1.6 collective-permute-start.8
  71.4 2.3 %collective-permute-start.7 = (bf16[256,2048]{1,0:T(8,128)(2,1)}, bf16[256,2048]{1,0:T(8,128)(2,1)}, u32[]{:S(2)}, u32[]{:S(2)}) collective-permute-start(bf16[256,2048]{1,0:T(8,128)(2,1)} %collective-permute-done.2.refs_4_), channel_id=1, source_target_pairs={{2,3},{6,7},{10,11},{14,15},{18,19},{22,23},{26,27},{30,31}} | collective-permute-start | bytes 3145736 | tf_op jit(solution)/shard_map/ppermute | solution.py:239
  73.7 2.1 slice.66
  75.8 2.1 %slice.67 = bf16[3328,128]{1,0:T(8,128)(2,1)} slice(bf16[6656,128]{1,0:T(8,128)(2,1)} %collective-permute-done.5.refs_15_.refs_4_), slice={[3328:6656], [0:128]} | slice | bytes 1703936 | tf_op jit(solution)/shard_map/slice | solution.py:302
  78.9 0.7 stack.82.refs_0_
  80.2 18.5 %hidden_grad_terms.7 = (f32[4,1664,128]{2,1,0:T(8,128)}, bf16[4,1664,128]{2,1,0:T(8,128)(2,1)}, f32[4,1664,128]{2,1,0:T(8,128)}, bf16[4,1664,128]{2,1,0:T(8,128)...) custom-call(s32[6]{0:T(128)} %stack.96.refs_0_, ...), custom_call_target="tpu_custom_call", output_to_operand_aliasing={{0}: (5, {}), {1}: (6, {}), {2}: (7, {}), {3}: (8, {}), {4}... | custom-call | flops 6979321856 | bytes 30408704 | tf_op jit(solution)/shard_map/hidden_grad_terms/pallas_call | solution.py:40
  98.7 0.7 collective-permute-done.11.refs_18_.refs_6_
  100.3 11.1 %hidden_grad_terms.8 = (f32[4,1664,128]{2,1,0:T(8,128)}, bf16[4,1664,128]{2,1,0:T(8,128)(2,1)}, f32[4,1664,128]{2,1,0:T(8,128)}, bf16[4,1664,128]{2,1,0:T(8,128)(2,1)}, bf16[1024,2048]{1,0:T(8,128)(2,1)}) custom-call(s32[6]{0:T(128)} %stack.82.refs_0_, ...), custom_call_target="tpu_custom_call", output_to_operand_aliasing={{0}: (6, {}), {1}: (7, {}), {2}: (8, {}), {3}: (9, {}), {4}... | custom-call | flops 3489660928 | bytes 31457280 | tf_op jit(solution)/shard_map/hidden_grad_terms/pallas_call | solution.py:40
  112.0 11.2 %hidden_grad_terms.9 = (f32[4,1664,128]{2,1,0:T(8,128)}, bf16[4,1664,128]{2,1,0:T(8,128)(2,1)}, f32[4,1664,128]{2,1,0:T(8,128)}, bf16[4,1664,128]{2,1,0:T(8,128)(2,1)}) custom-call(s32[6]{0:T(128)} %stack.82.refs_0_, bf16[6656,2048]{1,0:T(8,128)(2,1)} %refs_1_.15, ...), custom_call_target="tpu_custom_call", output_to_operand_aliasing={{0}: (6, {}), {1}: (7, {}), {2}: (8, {}), {3}: (9, {})} | custom-call | flops 3489660928 | bytes 31457280 | tf_op jit(solution)/shard_map/hidden_grad_terms/pallas_call | solution.py:40
  123.8 2.9 %add_convert_fusion.3 = bf16[2,1664,128]{2,1,0:T(8,128)(2,1)} fusion(f32[4,1664,128]{2,1,0:T(8,128)} %get-tuple-element.158.refs_10_.refs_2_, bf16[4,1664,128]{2,1,0:T(8,128)(2,1)} %collective-permute-done.17.refs_3_), kind=kLoop, calls=%fused_computation.4 | loop fusion | flops 1277952 | bytes 3407872 | tf_op jit(solution)/shard_map/convert_element_type | solution.py:337
  126.8 1.5 collective-permute-start.20
  128.2 2.4 %add_convert_fusion.2 = bf16[2,1664,128]{2,1,0:T(8,128)(2,1)} fusion(f32[4,1664,128]{2,1,0:T(8,128)S(1)} %copy-done, bf16[4,1664,128]{2,1,0:T(8,128)(2,1)} %collective-permute-done.16.refs_3_), kind=kLoop, calls=%fused_computation.3 | loop fusion | flops 1277952 | bytes 3407872 | tf_op jit(solution)/shard_map/convert_element_type | solution.py:337
  130.7 0.9 collective-permute-start.21
  131.6 1.1 add_convert_fusion.1
  133.4 1.0 copy-done.4
  134.4 1.3 collective-permute-start.18
  135.7 12.1 %weight_grad.4.refs_9_ = bf16[6656,2048]{1,0:T(8,128)(2,1)} custom-call(bf16[6656,128]{1,0:T(8,128)(2,1)} %hidden.1.refs_3_.refs_11_.refs_0_, bf16[6656,128]{1,0:T(8,128)(2,1)} %collective-permute-done.6.refs_13_.refs_12_.refs_1_, bf16[6656,128]{1,0:T(8,128)(2,1)} %collective-permute-done.4.refs_13_.refs_2_, ...), custom_call_target="tpu_custom_call" | custom-call | flops 6979321856 | bytes 19529728 | tf_op jit(solution)/shard_map/weight_grad/pallas_call | solution.py:40
  147.8 1.1 collective-permute-done.20.refs_4_
  148.9 2.3 %add_convert_fusion.7 = bf16[1,1664,128]{2,1,0:T(8,128)(2,1)} fusion(f32[4,1664,128]{2,1,0:T(8,128)} %get-tuple-element.158.refs_10_.refs_2_, bf16[2,1664,128]{2,1,0:T(8,128)(2,1)} %collective-permute-done.20.refs_4_, bf16[4,1664,128]{2,1,0:T(8,128)(2,1)} %collective-permute-done.17.refs_3_), kind=kLoop, calls=%fused_computation.8 | loop fusion | flops 1064960 | bytes 2129920 | tf_op jit(solution)/shard_map/convert_element_type | solution.py:337
  151.2 0.9 collective-permute-start.25
  152.1 0.8 collective-permute-done.21.refs_4_
  152.8 2.3 %add_convert_fusion.6.refs_10_ = bf16[1,1664,128]{2,1,0:T(8,128)(2,1)} fusion(f32[4,1664,128]{2,1,0:T(8,128)} %get-tuple-element.161.refs_2_, bf16[2,1664,128]{2,1,0:T(8,128)(2,1)} %collective-permute-done.21.refs_4_, bf16[4,1664,128]{2,1,0:T(8,128)(2,1)} %collective-permute-done.16.refs_3_), kind=kLoop, calls=%fused_computation.7 | loop fusion | flops 1064960 | bytes 2129920 | tf_op jit(solution)/shard_map/convert_element_type | solution.py:337
  155.2 0.8 collective-permute-start.24
  155.9 12.1 %weight_grad.5.refs_9_ = bf16[6656,2048]{1,0:T(8,128)(2,1)} custom-call(bf16[6656,128]{1,0:T(8,128)(2,1)} %hidden.1.refs_3_.refs_11_.refs_0_, bf16[6656,128]{1,0:T(8,128)(2,1)} %collective-permute-done.6.refs_13_.refs_12_.refs_1_, bf16[6656,128]{1,0:T(8,128)(2,1)} %collective-permute-done.4.refs_13_.refs_2_, ...), custom_call_target="tpu_custom_call", output_to_operand_aliasing={{}: (9, {})} | custom-call | flops 6979321856 | bytes 19529728 | tf_op jit(solution)/shard_map/weight_grad/pallas_call | solution.py:40
  168.0 12.2 %weight_grad.6.refs_9_ = bf16[6656,2048]{1,0:T(8,128)(2,1)} custom-call(bf16[6656,128]{1,0:T(8,128)(2,1)} %hidden.1.refs_3_.refs_11_.refs_0_, bf16[6656,128]{1,0:T(8,128)(2,1)} %collective-permute-done.6.refs_13_.refs_12_.refs_1_, bf16[6656,128]{1,0:T(8,128)(2,1)} %collective-permute-done.4.refs_13_.refs_2_, ...), custom_call_target="tpu_custom_call", output_to_operand_aliasing={{}: (9, {})} | custom-call | flops 6979321856 | bytes 19529728 | tf_op jit(solution)/shard_map/weight_grad/pallas_call | solution.py:40
  180.2 2.3 %add_convert_fusion.5 = bf16[1,1664,128]{2,1,0:T(8,128)(2,1)} fusion(f32[4,1664,128]{2,1,0:T(8,128)} %get-tuple-element.164.refs_2_, bf16[2,1664,128]{2,1,0:T(8,128)(2,1)} %collective-permute-done.19.refs_4_, bf16[4,1664,128]{2,1,0:T(8,128)(2,1)} %copy-done.5), kind=kLoop, calls=%fused_computation.6 | loop fusion | flops 1064960 | bytes 2129920 | tf_op jit(solution)/shard_map/convert_element_type | solution.py:337
  182.5 1.1 collective-permute-start.23
  183.6 1.5 add_convert_fusion.4.refs_10_
  185.1 1.2 collective-permute-start.22
  186.3 12.2 %weight_grad.7.refs_6_ = bf16[6656,2048]{1,0:T(8,128)(2,1)} custom-call(bf16[6656,128]{1,0:T(8,128)(2,1)} %hidden.1.refs_3_.refs_11_.refs_0_, bf16[6656,128]{1,0:T(8,128)(2,1)} %collective-permute-done.6.refs_13_.refs_12_.refs_1_, bf16[6656,128]{1,0:T(8,128)(2,1)} %collective-permute-done.4.refs_13_.refs_2_, ...), custom_call_target="tpu_custom_call", output_to_operand_aliasing={{}: (9, {})} | custom-call | flops 6979321856 | bytes 19529728 | tf_op jit(solution)/shard_map/weight_grad/pallas_call | solution.py:40
  198.5 3.2 %finish.4 = (bf16[128,6656]{1,0:T(8,128)(2,1)}, bf16[128,6656]{1,0:T(8,128)(2,1)}) custom-call(bf16[128,6656]{1,0:T(8,128)(2,1)} %refs_0_.9, bf16[128,6656]{1,0:T(8,128)(2,1)} %refs_1_.19, f32[4,1664,128]{2,1,0:T(8,128)} %get-tuple-element.158.refs_10_.refs_2_, bf16[4,1664,128]{2,1,0:T(8,128)(2,1)} %collective-permute-done.17.refs_3_, ...), custom_call_target="tpu_custom_call" | custom-call | bytes 9797632 | tf_op jit(solution)/shard_map/finish/pallas_call | solution.py:40
  201.7 3.2 %finish.5 = (bf16[128,6656]{1,0:T(8,128)(2,1)}, bf16[128,6656]{1,0:T(8,128)(2,1)}) custom-call(bf16[128,6656]{1,0:T(8,128)(2,1)} %refs_0_.9, bf16[128,6656]{1,0:T(8,128)(2,1)} %refs_1_.19, f32[4,1664,128]{2,1,0:T(8,128)} %get-tuple-element.161.refs_2_, ...), custom_call_target="tpu_custom_call", output_to_operand_aliasing={{0}: (6, {}), {1}: (7, {})} | custom-call | bytes 9797632 | tf_op jit(solution)/shard_map/finish/pallas_call | solution.py:40
  204.9 3.2 %finish.6 = (bf16[128,6656]{1,0:T(8,128)(2,1)}, bf16[128,6656]{1,0:T(8,128)(2,1)}) custom-call(bf16[128,6656]{1,0:T(8,128)(2,1)} %refs_0_.9, bf16[128,6656]{1,0:T(8,128)(2,1)} %refs_1_.19, f32[4,1664,128]{2,1,0:T(8,128)} %get-tuple-element.164.refs_2_, bf16[4,1664,128]{2,1,0:T(8,128)(2,1)} %copy-done.5, ...), custom_call_target="tpu_custom_call", output_to_operand_aliasing={{0}: (6, {}), {1}: (7, {})} | custom-call | bytes 9797632 | tf_op jit(solution)/shard_map/finish/pallas_call | solution.py:40
  208.2 0.8 copy-done.8
  208.9 3.2 %finish.7 = (bf16[128,6656]{1,0:T(8,128)(2,1)}, bf16[128,6656]{1,0:T(8,128)(2,1)}) custom-call(bf16[128,6656]{1,0:T(8,128)(2,1)} %refs_0_.9, bf16[128,6656]{1,0:T(8,128)(2,1)} %refs_1_.19, f32[4,1664,128]{2,1,0:T(8,128)} %get-tuple-element.167.refs_2_, bf16[4,1664,128]{2,1,0:T(8,128)(2,1)} %copy-done.4, ...), custom_call_target="tpu_custom_call", output_to_operand_aliasing={{0}: (6, {}), {1}: (7, {})} | custom-call | bytes 9797632 | tf_op jit(solution)/shard_map/finish/pallas_call | solution.py:40
  (51 shorter events, 5.1 us)
Async XLA Ops:
  5.0 41.3 %collective-permute-start.6 = (bf16[6656,128]{1,0:T(8,128)(2,1)}, bf16[6656,128]{1,0:T(8,128)(2,1)}, u32[]{:S(2)}, u32[]{:S(2)}) collective-permute-start(bf16[6656,128]{1,0:T(8,128)(2,1)} %hidden.1.refs_3_.refs_11_.refs_0_), channel_id=1, source_target_pairs={{0,4},{4,0},{8,12},{12,8},{16,20},{20,16},{24,28},{28,24},{1,5},{5... | collective-permute-start | bytes 5111816 | tf_op jit(solution)/shard_map/ppermute | solution.py:226
  5.1 59.7 %collective-permute-start.5 = (bf16[6656,128]{1,0:T(8,128)(2,1)}, bf16[6656,128]{1,0:T(8,128)(2,1)}, u32[]{:S(2)}, u32[]{:S(2)}) collective-permute-start(bf16[6656,128]{1,0:T(8,128)(2,1)} %hidden.1.refs_3_.refs_11_.refs_0_), channel_id=1, source_target_pairs={{0,16},{4,20},{8,24},{12,28},{16,0},{20,4},{24,8},{28,12},{1,17},{... | collective-permute-start | bytes 5111816 | tf_op jit(solution)/shard_map/ppermute | solution.py:226
  6.6 58.2 %collective-permute-start.4 = (bf16[6656,128]{1,0:T(8,128)(2,1)}, bf16[6656,128]{1,0:T(8,128)(2,1)}, u32[]{:S(2)}, u32[]{:S(2)}) collective-permute-start(bf16[6656,128]{1,0:T(8,128)(2,1)} %hidden.1.refs_3_.refs_11_.refs_0_), channel_id=1, source_target_pairs={{0,8},{4,12},{8,0},{12,4},{16,24},{20,28},{24,16},{28,20},{1,9},{5... | collective-permute-start | bytes 5111816 | tf_op jit(solution)/shard_map/ppermute | solution.py:226
  8.1 27.2 %collective-permute-start = (bf16[256,2048]{1,0:T(8,128)(2,1)}, bf16[256,2048]{1,0:T(8,128)(2,1)}, u32[]{:S(2)}, u32[]{:S(2)}) collective-permute-start(bf16[256,2048]{1,0:T(8,128)(2,1)} %refs_2_.1), channel_id=1, source_target_pairs={{0,1},{1,2},{2,3},{4,5},{5,6},{6,7},{8,9},{9,10},{10,11},{12,13},{... | collective-permute-start | bytes 3145736 | tf_op jit(solution)/shard_map/ppermute | solution.py:239
  11.5 26.9 %collective-permute-start.1 = (bf16[256,2048]{1,0:T(8,128)(2,1)}, bf16[256,2048]{1,0:T(8,128)(2,1)}, u32[]{:S(2)}, u32[]{:S(2)}) collective-permute-start(bf16[256,2048]{1,0:T(8,128)(2,1)} %refs_2_.1), channel_id=1, source_target_pairs={{1,0},{2,1},{3,2},{5,4},{6,5},{7,6},{9,8},{10,9},{11,10},{13,12},{... | collective-permute-start | bytes 3145736 | tf_op jit(solution)/shard_map/ppermute | solution.py:240
  38.5 31.2 %collective-permute-start.2 = (bf16[256,2048]{1,0:T(8,128)(2,1)}, bf16[256,2048]{1,0:T(8,128)(2,1)}, u32[]{:S(2)}, u32[]{:S(2)}) collective-permute-start(bf16[256,2048]{1,0:T(8,128)(2,1)} %collective-permute-done.refs_3_), channel_id=1, source_target_pairs={{1,2},{2,3},{5,6},{6,7},{9,10},{10,11},{13,14},{14,15},{17,18},{18... | collective-permute-start | bytes 3145736 | tf_op jit(solution)/shard_map/ppermute | solution.py:239
  40.4 29.3 %collective-permute-start.3 = (bf16[256,2048]{1,0:T(8,128)(2,1)}, bf16[256,2048]{1,0:T(8,128)(2,1)}, u32[]{:S(2)}, u32[]{:S(2)}) collective-permute-start(bf16[256,2048]{1,0:T(8,128)(2,1)} %collective-permute-done.1.refs_2_), channel_id=1, source_target_pairs={{1,0},{2,1},{5,4},{6,5},{9,8},{10,9},{13,12},{14,13},{17,16},{18,1... | collective-permute-start | bytes 3145736 | tf_op jit(solution)/shard_map/ppermute | solution.py:240
  69.7 30.1 %collective-permute-start.9 = (bf16[13312,128]{1,0:T(8,128)(2,1)}, bf16[13312,128]{1,0:T(8,128)(2,1)}, u32[]{:S(2)}, u32[]{:S(2)}) collective-permute-start(bf16[13312,128]{1,0:T(8,128)(2,1)} %pad_maximum_fusion), channel_id=1, source_target_pairs={{0,4},{4,0},{8,12},{12,8},{16,20},{20,16},{24,28},{28,24},{1,5},{5... | collective-permute-start | bytes 10223624 | tf_op jit(solution)/shard_map/ppermute | solution.py:226
  69.8 29.0 %collective-permute-start.8 = (bf16[256,2048]{1,0:T(8,128)(2,1)}, bf16[256,2048]{1,0:T(8,128)(2,1)}, u32[]{:S(2)}, u32[]{:S(2)}) collective-permute-start(bf16[256,2048]{1,0:T(8,128)(2,1)} %collective-permute-done.3.refs_3_.refs_2_), channel_id=1, source_target_pairs={{1,0},{5,4},{9,8},{13,12},{17,16},{21,20},{25,24},{29,28}} | collective-permute-start | bytes 3145736 | tf_op jit(solution)/shard_map/ppermute | solution.py:240
  71.4 27.3 %collective-permute-start.7 = (bf16[256,2048]{1,0:T(8,128)(2,1)}, bf16[256,2048]{1,0:T(8,128)(2,1)}, u32[]{:S(2)}, u32[]{:S(2)}) collective-permute-start(bf16[256,2048]{1,0:T(8,128)(2,1)} %collective-permute-done.2.refs_4_), channel_id=1, source_target_pairs={{2,3},{6,7},{10,11},{14,15},{18,19},{22,23},{26,27},{30,31}} | collective-permute-start | bytes 3145736 | tf_op jit(solution)/shard_map/ppermute | solution.py:239
  77.9 21.5 %collective-permute-start.11 = (bf16[3328,128]{1,0:T(8,128)(2,1)}, bf16[3328,128]{1,0:T(8,128)(2,1)S(1)}, u32[]{:S(2)}, u32[]{:S(2)}) collective-permute-start(bf16[3328,128]{1,0:T(8,128)(2,1)} %slice.67), channel_id=1, source_target_pairs={{0,8},{4,12},{8,0},{12,4},{16,24},{20,28},{24,16},{28,20},{1,9},{5... | collective-permute-start | bytes 2555912 | tf_op jit(solution)/shard_map/ppermute | solution.py:226
  78.4 21.4 %collective-permute-start.10 = (bf16[3328,128]{1,0:T(8,128)(2,1)}, bf16[3328,128]{1,0:T(8,128)(2,1)}, u32[]{:S(2)}, u32[]{:S(2)}) collective-permute-start(bf16[3328,128]{1,0:T(8,128)(2,1)} %slice.66), channel_id=1, source_target_pairs={{0,16},{4,20},{8,24},{12,28},{16,0},{20,4},{24,8},{28,12},{1,17},{... | collective-permute-start | bytes 2555912 | tf_op jit(solution)/shard_map/ppermute | solution.py:226
  99.4 0.9 copy-start.3
  99.8 12.3 %collective-permute-start.12 = (bf16[3328,128]{1,0:T(8,128)(2,1)}, bf16[3328,128]{1,0:T(8,128)(2,1)}, u32[]{:S(2)}, u32[]{:S(2)}) collective-permute-start(bf16[3328,128]{1,0:T(8,128)(2,1)} %collective-permute-done.10.refs_17_.refs_6_), channel_id=1, source_target_pairs={{0,4},{4,0},{8,12},{12,8},{16,20},{20,16},{24,28},{28,24},{1,5},{5... | collective-permute-start | bytes 2555912 | tf_op jit(solution)/shard_map/ppermute | solution.py:226
  99.8 12.3 %collective-permute-start.13 = (bf16[3328,128]{1,0:T(8,128)(2,1)S(1)}, bf16[3328,128]{1,0:T(8,128)(2,1)}, u32[]{:S(2)}, u32[]{:S(2)}) collective-permute-start(bf16[3328,128]{1,0:T(8,128)(2,1)S(1)} %collective-permute-done.11.refs_18_.refs_6_), channel_id=1, source_target_pairs={{0,4},{4,0},{8,12},{12,8},{16,20},{20,16},{24,28},{28,24},{1,5},{5... | collective-permute-start | bytes 2555912 | tf_op jit(solution)/shard_map/ppermute | solution.py:226
  111.5 12.3 %collective-permute-start.17 = (bf16[4,1664,128]{2,1,0:T(8,128)(2,1)}, bf16[4,1664,128]{2,1,0:T(8,128)(2,1)}, u32[]{:S(2)}, u32[]{:S(2)}) collective-permute-start(bf16[4,1664,128]{2,1,0:T(8,128)(2,1)} %get-tuple-element.147), channel_id=1, source_target_pairs={{0,4},{4,0},{8,12},{12,8},{16,20},{20,16},{24,28},{28,24},{1,5},{5... | collective-permute-start | bytes 5111816 | tf_op jit(solution)/shard_map/ppermute | solution.py:226
  111.5 16.7 %collective-permute-start.16 = (bf16[4,1664,128]{2,1,0:T(8,128)(2,1)}, bf16[4,1664,128]{2,1,0:T(8,128)(2,1)}, u32[]{:S(2)}, u32[]{:S(2)}) collective-permute-start(bf16[4,1664,128]{2,1,0:T(8,128)(2,1)} %get-tuple-element.146), channel_id=1, source_target_pairs={{0,4},{4,0},{8,12},{12,8},{16,20},{20,16},{24,28},{28,24},{1,5},{5... | collective-permute-start | bytes 5111816 | tf_op jit(solution)/shard_map/ppermute | solution.py:226
  123.2 8.4 %collective-permute-start.15 = (bf16[4,1664,128]{2,1,0:T(8,128)(2,1)}, bf16[4,1664,128]{2,1,0:T(8,128)(2,1)S(1)}, u32[]{:S(2)}, u32[]{:S(2)}) collective-permute-start(bf16[4,1664,128]{2,1,0:T(8,128)(2,1)} %get-tuple-element.144), channel_id=1, source_target_pairs={{0,4},{4,0},{8,12},{12,8},{16,20},{20,16},{24,28},{28,24},{1,5},{5... | collective-permute-start | bytes 5111816 | tf_op jit(solution)/shard_map/ppermute | solution.py:226
  123.4 9.8 %collective-permute-start.14 = (bf16[4,1664,128]{2,1,0:T(8,128)(2,1)}, bf16[4,1664,128]{2,1,0:T(8,128)(2,1)S(1)}, u32[]{:S(2)}, u32[]{:S(2)}) collective-permute-start(bf16[4,1664,128]{2,1,0:T(8,128)(2,1)} %get-tuple-element.142), channel_id=1, source_target_pairs={{0,4},{4,0},{8,12},{12,8},{16,20},{20,16},{24,28},{28,24},{1,5},{5... | collective-permute-start | bytes 5111816 | tf_op jit(solution)/shard_map/ppermute | solution.py:226
  123.8 4.4 %copy-start = (f32[4,1664,128]{2,1,0:T(8,128)S(1)}, f32[4,1664,128]{2,1,0:T(8,128)}, u32[]{:S(2)}) copy-start(f32[4,1664,128]{2,1,0:T(8,128)} %get-tuple-element.161.refs_2_) | copy-start | bytes 10223620
  126.8 22.1 %collective-permute-start.20 = (bf16[2,1664,128]{2,1,0:T(8,128)(2,1)}, bf16[2,1664,128]{2,1,0:T(8,128)(2,1)}, u32[]{:S(2)}, u32[]{:S(2)}) collective-permute-start(bf16[2,1664,128]{2,1,0:T(8,128)(2,1)} %add_convert_fusion.3), channel_id=1, source_target_pairs={{0,8},{4,12},{8,0},{12,4},{16,24},{20,28},{24,16},{28,20},{1,9},{5... | collective-permute-start | bytes 2555912 | tf_op jit(solution)/shard_map/ppermute | solution.py:226
  128.2 3.4 %copy-start.1 = (f32[4,1664,128]{2,1,0:T(8,128)S(1)}, f32[4,1664,128]{2,1,0:T(8,128)}, u32[]{:S(2)}) copy-start(f32[4,1664,128]{2,1,0:T(8,128)} %get-tuple-element.164.refs_2_) | copy-start | bytes 10223620
  130.7 2.5 %copy-start.2 = (f32[4,1664,128]{2,1,0:T(8,128)S(1)}, f32[4,1664,128]{2,1,0:T(8,128)}, u32[]{:S(2)}) copy-start(f32[4,1664,128]{2,1,0:T(8,128)} %get-tuple-element.167.refs_2_) | copy-start | bytes 10223620
  130.7 22.2 %collective-permute-start.21 = (bf16[2,1664,128]{2,1,0:T(8,128)(2,1)}, bf16[2,1664,128]{2,1,0:T(8,128)(2,1)}, u32[]{:S(2)}, u32[]{:S(2)}) collective-permute-start(bf16[2,1664,128]{2,1,0:T(8,128)(2,1)} %add_convert_fusion.2), channel_id=1, source_target_pairs={{0,16},{4,20},{8,24},{12,28},{16,0},{20,4},{24,8},{28,12},{1,17},{... | collective-permute-start | bytes 2555912 | tf_op jit(solution)/shard_map/ppermute | solution.py:226
  131.6 1.6 copy-start.5
  132.7 47.5 %collective-permute-start.19 = (bf16[2,1664,128]{2,1,0:T(8,128)(2,1)}, bf16[2,1664,128]{2,1,0:T(8,128)(2,1)}, u32[]{:S(2)}, u32[]{:S(2)}) collective-permute-start(bf16[2,1664,128]{2,1,0:T(8,128)(2,1)} %add_convert_fusion.1), channel_id=1, source_target_pairs={{0,8},{4,12},{8,0},{12,4},{16,24},{20,28},{24,16},{28,20},{1,9},{5... | collective-permute-start | bytes 2555912 | tf_op jit(solution)/shard_map/ppermute | solution.py:226
  133.2 1.2 copy-start.4
  134.4 1.3 copy-start.6
  134.4 49.2 %collective-permute-start.18 = (bf16[2,1664,128]{2,1,0:T(8,128)(2,1)S(1)}, bf16[2,1664,128]{2,1,0:T(8,128)(2,1)}, u32[]{:S(2)}, u32[]{:S(2)}) collective-permute-start(bf16[2,1664,128]{2,1,0:T(8,128)(2,1)S(1)} %add_convert_fusion.refs_9_), channel_id=1, source_target_pairs={{0,16},{4,20},{8,24},{12,28},{16,0},{20,4},{24,8},{28,12},{1,17},{... | collective-permute-start | bytes 2555912 | tf_op jit(solution)/shard_map/ppermute | solution.py:226
  151.2 47.3 %collective-permute-start.25 = (bf16[1,1664,128]{2,1,0:T(8,128)(2,1)}, bf16[1,1664,128]{2,1,0:T(8,128)(2,1)}, u32[]{:S(2)}, u32[]{:S(2)}) collective-permute-start(bf16[1,1664,128]{2,1,0:T(8,128)(2,1)} %add_convert_fusion.7), channel_id=1, source_target_pairs={{0,16},{4,20},{8,24},{12,28},{16,0},{20,4},{24,8},{28,12},{1,17},{... | collective-permute-start | bytes 1277960 | tf_op jit(solution)/shard_map/ppermute | solution.py:226
  155.2 46.6 %collective-permute-start.24 = (bf16[1,1664,128]{2,1,0:T(8,128)(2,1)}, bf16[1,1664,128]{2,1,0:T(8,128)(2,1)}, u32[]{:S(2)}, u32[]{:S(2)}) collective-permute-start(bf16[1,1664,128]{2,1,0:T(8,128)(2,1)} %add_convert_fusion.6.refs_10_), channel_id=1, source_target_pairs={{0,8},{4,12},{8,0},{12,4},{16,24},{20,28},{24,16},{28,20},{1,9},{5... | collective-permute-start | bytes 1277960 | tf_op jit(solution)/shard_map/ppermute | solution.py:226
  182.5 22.4 %collective-permute-start.23 = (bf16[1,1664,128]{2,1,0:T(8,128)(2,1)}, bf16[1,1664,128]{2,1,0:T(8,128)(2,1)}, u32[]{:S(2)}, u32[]{:S(2)}) collective-permute-start(bf16[1,1664,128]{2,1,0:T(8,128)(2,1)} %add_convert_fusion.5), channel_id=1, source_target_pairs={{0,16},{4,20},{8,24},{12,28},{16,0},{20,4},{24,8},{28,12},{1,17},{... | collective-permute-start | bytes 1277960 | tf_op jit(solution)/shard_map/ppermute | solution.py:226
  185.1 1.2 copy-start.7
  185.1 23.0 %collective-permute-start.22 = (bf16[1,1664,128]{2,1,0:T(8,128)(2,1)S(1)}, bf16[1,1664,128]{2,1,0:T(8,128)(2,1)S(1)}, u32[]{:S(2)}, u32[]{:S(2)}) collective-permute-start(bf16[1,1664,128]{2,1,0:T(8,128)(2,1)S(1)} %add_convert_fusion.4.refs_10_), channel_id=1, source_target_pairs={{0,8},{4,12},{8,0},{12,4},{16,24},{20,28},{24,16},{28,20},{1,9},{5... | collective-permute-start | bytes 1277960 | tf_op jit(solution)/shard_map/ppermute | solution.py:226
  208.1 0.8 copy-start.8

commit v7 on v6

--- a/solution.py
+++ b/solution.py
@@ -12,9 +12,10 @@
 VMEM_LIMIT = 63 * 1024 * 1024
 CHUNKS = 4
 GROUPS = 2
-PARTS = 4
+PARTS = [(0, 2), (2, 3), (3, 4)]
+SPLIT = 4
 LANES = 128
-PLAN = ["P0 P1 S0 S1", "S2 S3 W0 S0", "S1 W1 W2 S2", "S3 W3 F0 F1", "F2 F3"]
+PLAN = ["P0 P1 S0 S1", "S2 S3 W0 S0", "S1 W1 S2 S3", "W2 F0 F1 F2", "F3"]
 
 
 def divisor(extent, most, step):
@@ -70,7 +71,8 @@
     return run(hidden_kernel, "hidden", (width // step,), [(gate, spec), (up, spec)], [out])[0]
 
 
-def product_kernel(choices, counts, ordering, at_ref, weight_ref, *refs):
+def product_kernel(choices, counts, ordering, at_ref, *refs):
+    weights, refs = refs[:SPLIT], refs[SPLIT:]
     sources, outs = refs[:choices], refs[choices:-4]
     dy_ref, turned_ref, sems, out_sem = refs[-4:]
     step = pl.program_id(0)
@@ -103,14 +105,17 @@
             to_order.start()
         turned_ref[...] = jnp.transpose(dy_ref[...])
 
-    part = jnp.dot(weight_ref[...], turned_ref[...], preferred_element_type=F32)
+    turned = turned_ref[...]
+    parts = [jnp.dot(ref[...], turned, preferred_element_type=F32) for ref in weights]
+    rows = weights[0].shape[0]
     first = 0
     for q, count in enumerate(counts):
 
         @pl.when((step >= first) & (step < first + count))
         def _():
-            outs[2 * q][...] = part[:, :block][None]
-            outs[2 * q + 1][...] = part[:, block:].astype(BF16)[None]
+            for n, part in enumerate(parts):
+                outs[2 * q][0, pl.ds(n * rows, rows)] = part[:, :block]
+                outs[2 * q + 1][0, pl.ds(n * rows, rows)] = part[:, block:].astype(BF16)
 
         first += count
 
@@ -123,9 +128,14 @@
 
 def hidden_grad_terms(at, sources, weight, first, widths, held, ordered, total, deps):
     block, depth = sources[0].shape[0] // 2, sources[0].shape[1]
-    tall = divisor(math.gcd(first, *widths), 832, 16)
+    tall = divisor(math.gcd(first, *widths), 832, 16 * SPLIT)
     counts = [w // tall for w in widths]
-    ins = [(weight, pl.BlockSpec((tall, depth), lambda i, at: (first // tall + i, 0)))]
+
+    def weight_spec(n):
+        start = first // tall
+        return pl.BlockSpec((tall // SPLIT, depth), lambda i, at: ((start + i) * SPLIT + n, 0))
+
+    ins = [(weight, weight_spec(n)) for n in range(SPLIT)]
     ins += [(x, pl.BlockSpec(memory_space=pl.ANY)) for x in sources]
     outs, start = [], 0
     for q, (w, count) in enumerate(zip(widths, counts)):
@@ -170,25 +180,42 @@
 
 
 def weight_grad_kernel(*refs):
-    hidden = jnp.concatenate([ref[...] for ref in refs[:-2]], axis=1)
-    refs[-1][...] = jnp.dot(hidden, refs[-2][...], preferred_element_type=F32).astype(BF16)
+    pieces, (source, out_ref, dy_ref, sems) = refs[:-4], refs[-4:]
+
+    @pl.when(pl.program_id(0) == 0)
+    def _():
+        count = sems.shape[0]
+        rows = dy_ref.shape[0] // count
+        copies = []
+        for n in range(count):
+            cut = pl.ds(n * rows, rows)
+            copies.append(pltpu.make_async_copy(source.at[cut], dy_ref.at[cut], sems.at[n]))
+        for copy in copies:
+            copy.start()
+        for copy in copies:
+            copy.wait()
+
+    hidden = jnp.concatenate([ref[...] for ref in pieces], axis=1)
+    out_ref[...] = jnp.dot(hidden, dy_ref[...], preferred_element_type=F32).astype(BF16)
 
 
 def weight_grad(pieces, dy, whole, total, start, rows, deps):
     block = pieces[0][0].shape[1]
     tokens, depth = dy.shape
-    tall, wide = divisor(rows, 832, 16), divisor(depth, 1024, 128)
+    tall = divisor(rows, 416, 16)
 
     def spec(base):
-        return pl.BlockSpec((tall, block), lambda i, j: ((start - base) // tall + i, 0))
+        return pl.BlockSpec((tall, block), lambda i: ((start - base) // tall + i, 0))
 
     ins = [(x, spec(base)) for x, base in pieces]
-    ins.append((dy, pl.BlockSpec((tokens, wide), lambda i, j: (0, j))))
-    place = pl.BlockSpec((tall, wide), lambda i, j: (start // tall + i, j))
+    ins.append((dy, pl.BlockSpec(memory_space=pl.ANY)))
+    place = pl.BlockSpec((tall, depth), lambda i: (start // tall + i, 0))
     out = ((total, depth), BF16, place, whole)
-    grid = (rows // tall, depth // wide)
+    scratch = [pltpu.VMEM((tokens, depth), BF16), pltpu.SemaphoreType.DMA((8,))]
     flops = 2 * rows * tokens * depth
-    return run(weight_grad_kernel, "weight_grad", grid, ins, [out], deps, flops=flops)[0]
+    return run(
+        weight_grad_kernel, "weight_grad", (rows // tall,), ins, [out], deps, None, scratch, flops
+    )[0]
 
 
 def arrivals(z, count):
@@ -315,7 +342,6 @@
 
     grad_gate = grad_up = grad_down = None
     sums, stages = [None] * CHUNKS, [0] * CHUNKS
-    part = width // PARTS
 
     def step(kind, n, last):
         nonlocal grad_gate, grad_up, grad_down
@@ -342,11 +368,10 @@
                 gate_act, up_act, sums[n], edges[n], widths[n], (grad_gate, grad_up), [last]
             )
             return grad_up
-        pieces = []
-        for f in range(row_count):
-            side = -1 if n * part >= half else 0
-            pieces.append((held[f][side], base[f][side]))
-        grad_down = weight_grad(pieces, ordered, grad_down, width, n * part, part, [last])
+        start, stop = (width * x // 4 for x in PARTS[n])
+        side = -1 if start >= half else 0
+        pieces = [(held[f][side], base[f][side]) for f in range(row_count)]
+        grad_down = weight_grad(pieces, ordered, grad_down, width, start, stop - start, [last])
         return grad_down
 
     for item in " ".join(PLAN).split():

time: 213 us -> 209 us (0.981)
  Pallas kernels: 144 us -> 141 us
    pallas_call x14 -> x13, Pallas kernels: 144 us -> 141 us  [run(): pl.pallas_call(body, grid_spec=pltpu.PrefetchScalarGridSpec(num_scalar_pr...]
  transfers between devices with their start and end apart: 26 -> 26, of which waited for: 6 -> 4; matrix products, arithmetic and copies ran while one was open for 13% -> 14% of each run, Pallas kernels for 64% -> 64%
where the time goes in v7:
time: 209 us; the launch traced here: 208 us
  Pallas kernels  141 us (67%)
  starting transfers between devices  31.6 us (15%)
  other arithmetic  22 us (11%)
  local copies, waits for them, and re-layouts  7.05 us (3%)
  waiting for transfers between devices  5.77 us (3%)
    pallas_call x13, Pallas kernels, run(): pl.pallas_call(body, grid_spec=pltpu.PrefetchScalarGridSpec(num_scalar_pr...  141 us
    convert_element_type x8, other arithmetic, step(): send = sum((t[rows:2 * rows].astype(F32) for t in sums[n])).astype(BF16)  17.1 us
    ppermute x20, starting transfers between devices, swap(): return jax.tree.map(lambda x: lax.ppermute(x, 'row', pairs), x)  14 us
    ppermute x3, starting transfers between devices, forward(): lax.ppermute(down[-1], 'col', [(i, i - 1) for i in range(1, col_count - s...  9.89 us
    ppermute x3, starting transfers between devices, forward(): lax.ppermute(up[-1], 'col', [(i, i + 1) for i in range(s - 1, col_count -...  7.64 us
    concatenate x1, other arithmetic, program(): both = [jnp.concatenate(held[a] + held[b])]  4.87 us
    slice x2, local copies, waits for them, and re-layouts, program(): held[a | b] = [swap(held[a][0][:half], b), swap(held[b][0][half:], a)]  4.22 us
  transfers between devices with their start and end apart: 26, of which 4 were waited for; matrix products, arithmetic and copies ran while one was open for 14% of the time, Pallas kernels for 64%

profile of v7, /device:TPU:16, one launch (start us, length us, event | category | flops | bytes accessed | tf_op | source)
XLA Modules:
  0.0 208.2 jit_solution(16631414614512829526)
XLA Ops:
  0.6 4.4 %hidden.1.refs_6_.refs_14_.refs_0_ = bf16[6656,128]{1,0:T(8,128)(2,1)} custom-call(bf16[128,6656]{1,0:T(8,128)(2,1)} %refs_0_.9, bf16[128,6656]{1,0:T(8,128)(2,1)} %refs_1_.19), custom_call_target="tpu_custom_call" | custom-call | bytes 3407872 | tf_op jit(solution)/shard_map/hidden/pallas_call | solution.py:41
  5.1 1.5 collective-permute-start.5
  6.6 1.5 collective-permute-start.4
  8.1 3.5 %collective-permute-start = (bf16[256,2048]{1,0:T(8,128)(2,1)}, bf16[256,2048]{1,0:T(8,128)(2,1)}, u32[]{:S(2)}, u32[]{:S(2)}) collective-permute-start(bf16[256,2048]{1,0:T(8,128)(2,1)} %refs_5_.1), channel_id=1, source_target_pairs={{0,1},{1,2},{2,3},{4,5},{5,6},{6,7},{8,9},{9,10},{10,11},{12,13},{... | collective-permute-start | bytes 3145736 | tf_op jit(solution)/shard_map/ppermute | solution.py:266
  11.5 2.4 %collective-permute-start.1 = (bf16[256,2048]{1,0:T(8,128)(2,1)}, bf16[256,2048]{1,0:T(8,128)(2,1)}, u32[]{:S(2)}, u32[]{:S(2)}) collective-permute-start(bf16[256,2048]{1,0:T(8,128)(2,1)} %refs_5_.1), channel_id=1, source_target_pairs={{1,0},{2,1},{3,2},{5,4},{6,5},{7,6},{9,8},{10,9},{11,10},{13,12},{... | collective-permute-start | bytes 3145736 | tf_op jit(solution)/shard_map/ppermute | solution.py:267
  14.0 0.7 stack.91.refs_0_
  14.7 0.6 stack.86.refs_0_
  15.3 18.5 %hidden_grad_terms.5 = (f32[4,1664,128]{2,1,0:T(8,128)}, bf16[4,1664,128]{2,1,0:T(8,128)(2,1)}, f32[4,1664,128]{2,1,0:T(8,128)}, bf16[4,1664,128]{2,1,0:T(8,128)...) custom-call(s32[6]{0:T(128)} %stack.86.refs_0_, ...), custom_call_target="tpu_custom_call" | custom-call | flops 6979321856 | bytes 110100480 | tf_op jit(solution)/shard_map/hidden_grad_terms/pallas_call | solution.py:41
  33.8 1.5 collective-permute-done.refs_6_
  35.3 3.2 %collective-permute-done.1.refs_5_ = bf16[256,2048]{1,0:T(8,128)(2,1)} collective-permute-done((bf16[256,2048]{1,0:T(8,128)(2,1)}, bf16[256,2048]{1,0:T(8,128)(2,1)}, u32[]{:S(2)}, u32[]{:S(2)}) %collective-permute-start.1) | collective-permute-done | bytes 1048608 | tf_op jit(solution)/shard_map/ppermute | solution.py:267
  38.5 1.9 collective-permute-start.2
  40.4 5.9 %collective-permute-start.3 = (bf16[256,2048]{1,0:T(8,128)(2,1)}, bf16[256,2048]{1,0:T(8,128)(2,1)}, u32[]{:S(2)}, u32[]{:S(2)}) collective-permute-start(bf16[256,2048]{1,0:T(8,128)(2,1)} %collective-permute-done.1.refs_5_), channel_id=1, source_target_pairs={{1,0},{2,1},{5,4},{6,5},{9,8},{10,9},{13,12},{14,13},{17,16},{18,1... | collective-permute-start | bytes 3145736 | tf_op jit(solution)/shard_map/ppermute | solution.py:267
  46.3 18.5 %hidden_grad_terms.6 = (f32[4,1664,128]{2,1,0:T(8,128)}, bf16[4,1664,128]{2,1,0:T(8,128)(2,1)}, f32[4,1664,128]{2,1,0:T(8,128)}, bf16[4,1664,128]{2,1,0:T(8,128)...) custom-call(s32[6]{0:T(128)} %stack.91.refs_0_, ...), custom_call_target="tpu_custom_call", output_to_operand_aliasing={{0}: (7, {}), {1}: (8, {}), {2}: (9, {}), {3}: (10, {}), {4... | custom-call | flops 6979321856 | bytes 111149056 | tf_op jit(solution)/shard_map/hidden_grad_terms/pallas_call | solution.py:41
  64.8 4.9 %pad_maximum_fusion = bf16[13312,128]{1,0:T(8,128)(2,1)} fusion(bf16[6656,128]{1,0:T(8,128)(2,1)} %collective-permute-done.5.refs_18_.refs_4_, bf16[6656,128]{1,0:T(8,128)(2,1)} %collective-permute-done.4.refs_16_.refs_2_), kind=kLoop, calls=%fused_computation | loop fusion | flops 6815744 | bytes 6815744 | tf_op jit(solution)/shard_map/concatenate | solution.py:320
  69.8 1.6 collective-permute-start.8
  71.4 2.3 %collective-permute-start.7 = (bf16[256,2048]{1,0:T(8,128)(2,1)}, bf16[256,2048]{1,0:T(8,128)(2,1)}, u32[]{:S(2)}, u32[]{:S(2)}) collective-permute-start(bf16[256,2048]{1,0:T(8,128)(2,1)} %collective-permute-done.2.refs_7_), channel_id=1, source_target_pairs={{2,3},{6,7},{10,11},{14,15},{18,19},{22,23},{26,27},{30,31}} | collective-permute-start | bytes 3145736 | tf_op jit(solution)/shard_map/ppermute | solution.py:266
  73.7 2.1 %slice.66 = bf16[3328,128]{1,0:T(8,128)(2,1)} slice(bf16[6656,128]{1,0:T(8,128)(2,1)} %collective-permute-done.4.refs_16_.refs_2_), slice={[0:3328], [0:128]} | slice | bytes 1703936 | tf_op jit(solution)/shard_map/slice | solution.py:329
  75.8 2.1 %slice.67 = bf16[3328,128]{1,0:T(8,128)(2,1)} slice(bf16[6656,128]{1,0:T(8,128)(2,1)} %collective-permute-done.5.refs_18_.refs_4_), slice={[3328:6656], [0:128]} | slice | bytes 1703936 | tf_op jit(solution)/shard_map/slice | solution.py:329
  77.9 0.5 collective-permute-start.11
  79.0 0.6 stack.82.refs_0_
  79.6 0.7 stack.96.refs_0_
  80.3 18.5 %hidden_grad_terms.7 = (f32[4,1664,128]{2,1,0:T(8,128)}, bf16[4,1664,128]{2,1,0:T(8,128)(2,1)}, f32[4,1664,128]{2,1,0:T(8,128)}, bf16[4,1664,128]{2,1,0:T(8,128)...) custom-call(s32[6]{0:T(128)} %stack.96.refs_0_, ...), custom_call_target="tpu_custom_call", output_to_operand_aliasing={{0}: (8, {}), {1}: (9, {}), {2}: (10, {}), {3}: (11, {}), {... | custom-call | flops 6979321856 | bytes 112197632 | tf_op jit(solution)/shard_map/hidden_grad_terms/pallas_call | solution.py:41
  98.8 0.7 collective-permute-done.11.refs_21_.refs_6_
  100.4 11.2 %hidden_grad_terms.8 = (f32[4,1664,128]{2,1,0:T(8,128)}, bf16[4,1664,128]{2,1,0:T(8,128)(2,1)}, f32[4,1664,128]{2,1,0:T(8,128)}, bf16[4,1664,128]{2,1,0:T(8,128)(2,1)}, bf16[1024,2048]{1,0:T(8,128)(2,1)}) custom-call(s32[6]{0:T(128)} %stack.82.refs_0_, ...), custom_call_target="tpu_custom_call", output_to_operand_aliasing={{0}: (9, {}), {1}: (10, {}), {2}: (11, {}), {3}: (12, {}), ... | custom-call | flops 3489660928 | bytes 113246208 | tf_op jit(solution)/shard_map/hidden_grad_terms/pallas_call | solution.py:41
  112.1 11.2 %hidden_grad_terms.9 = (f32[4,1664,128]{2,1,0:T(8,128)}, bf16[4,1664,128]{2,1,0:T(8,128)(2,1)}, f32[4,1664,128]{2,1,0:T(8,128)}, bf16[4,1664,128]{2,1,0:T(8,128)(2,1)}) custom-call(s32[6]{0:T(128)} %stack.82.refs_0_, bf16[6656,2048]{1,0:T(8,128)(2,1)} %refs_4_.9, ...), custom_call_target="tpu_custom_call", output_to_operand_aliasing={{0}: (9, {}), {1}: (10, {}), {2}: (11, {}), {3}: (12, {})} | custom-call | flops 3489660928 | bytes 113246208 | tf_op jit(solution)/shard_map/hidden_grad_terms/pallas_call | solution.py:41
  123.9 2.9 %add_convert_fusion.3 = bf16[2,1664,128]{2,1,0:T(8,128)(2,1)} fusion(f32[4,1664,128]{2,1,0:T(8,128)} %get-tuple-element.158.refs_13_.refs_2_, bf16[4,1664,128]{2,1,0:T(8,128)(2,1)} %collective-permute-done.17.refs_3_), kind=kLoop, calls=%fused_computation.4 | loop fusion | flops 1277952 | bytes 3407872 | tf_op jit(solution)/shard_map/convert_element_type | solution.py:363
  126.9 1.4 collective-permute-start.20
  128.3 2.5 %add_convert_fusion.2 = bf16[2,1664,128]{2,1,0:T(8,128)(2,1)} fusion(f32[4,1664,128]{2,1,0:T(8,128)S(1)} %copy-done, bf16[4,1664,128]{2,1,0:T(8,128)(2,1)} %collective-permute-done.16.refs_3_), kind=kLoop, calls=%fused_computation.3 | loop fusion | flops 1277952 | bytes 3407872 | tf_op jit(solution)/shard_map/convert_element_type | solution.py:363
  130.8 0.9 collective-permute-start.21
  131.7 1.1 add_convert_fusion.1
  132.8 0.6 collective-permute-start.19
  133.4 1.2 add_convert_fusion.refs_9_
  134.8 1.3 collective-permute-start.18
  136.1 20.5 %weight_grad.3.refs_9_ = bf16[6656,2048]{1,0:T(8,128)(2,1)} custom-call(bf16[6656,128]{1,0:T(8,128)(2,1)} %hidden.1.refs_6_.refs_14_.refs_0_, bf16[6656,128]{1,0:T(8,128)(2,1)} %collective-permute-done.6.refs_16_.refs_15_.refs_1_, bf16[6656,128]{1,0:T(8,128)(2,1)} %collective-permute-done.4.refs_16_.refs_2_, ...), custom_call_target="tpu_custom_call" | custom-call | flops 13958643712 | bytes 19529728 | tf_op jit(solution)/shard_map/weight_grad/pallas_call | solution.py:41
  156.6 2.3 %add_convert_fusion.7 = bf16[1,1664,128]{2,1,0:T(8,128)(2,1)} fusion(f32[4,1664,128]{2,1,0:T(8,128)} %get-tuple-element.158.refs_13_.refs_2_, bf16[2,1664,128]{2,1,0:T(8,128)(2,1)} %collective-permute-done.20.refs_4_, bf16[4,1664,128]{2,1,0:T(8,128)(2,1)} %collective-permute-done.17.refs_3_), kind=kLoop, calls=%fused_computation.8 | loop fusion | flops 1064960 | bytes 2129920 | tf_op jit(solution)/shard_map/convert_element_type | solution.py:363
  158.9 0.8 collective-permute-start.25
  159.7 2.3 %add_convert_fusion.6.refs_10_ = bf16[1,1664,128]{2,1,0:T(8,128)(2,1)} fusion(f32[4,1664,128]{2,1,0:T(8,128)} %get-tuple-element.161.refs_2_, bf16[2,1664,128]{2,1,0:T(8,128)(2,1)} %collective-permute-done.21.refs_4_, bf16[4,1664,128]{2,1,0:T(8,128)(2,1)} %collective-permute-done.16.refs_3_), kind=kLoop, calls=%fused_computation.7 | loop fusion | flops 1064960 | bytes 2129920 | tf_op jit(solution)/shard_map/convert_element_type | solution.py:363
  162.0 1.5 collective-permute-start.24
  163.5 12.6 %weight_grad.4.refs_9_ = bf16[6656,2048]{1,0:T(8,128)(2,1)} custom-call(bf16[6656,128]{1,0:T(8,128)(2,1)} %hidden.1.refs_6_.refs_14_.refs_0_, bf16[6656,128]{1,0:T(8,128)(2,1)} %collective-permute-done.6.refs_16_.refs_15_.refs_1_, bf16[6656,128]{1,0:T(8,128)(2,1)} %collective-permute-done.4.refs_16_.refs_2_, ...), custom_call_target="tpu_custom_call", output_to_operand_aliasing={{}: (9, {})} | custom-call | flops 6979321856 | bytes 19529728 | tf_op jit(solution)/shard_map/weight_grad/pallas_call | solution.py:41
  176.1 2.3 %add_convert_fusion.5 = bf16[1,1664,128]{2,1,0:T(8,128)(2,1)} fusion(f32[4,1664,128]{2,1,0:T(8,128)} %get-tuple-element.164.refs_2_, bf16[2,1664,128]{2,1,0:T(8,128)(2,1)} %collective-permute-done.19.refs_4_, bf16[4,1664,128]{2,1,0:T(8,128)(2,1)} %copy-done.5), kind=kLoop, calls=%fused_computation.6 | loop fusion | flops 1064960 | bytes 2129920 | tf_op jit(solution)/shard_map/convert_element_type | solution.py:363
  178.5 1.2 collective-permute-start.23
  179.7 2.5 %add_convert_fusion.4.refs_10_ = bf16[1,1664,128]{2,1,0:T(8,128)(2,1)} fusion(f32[4,1664,128]{2,1,0:T(8,128)} %get-tuple-element.167.refs_2_, bf16[2,1664,128]{2,1,0:T(8,128)(2,1)S(1)} %collective-permute-done.18.refs_4_, bf16[4,1664,128]{2,1,0:T(8,128)(2,1)} %copy-done.4), kind=kLoop, calls=%fused_computation.5 | loop fusion | flops 1064960 | bytes 2129920 | tf_op jit(solution)/shard_map/convert_element_type | solution.py:363
  182.2 0.6 collective-permute-start.22
  182.7 12.6 %weight_grad.5.refs_6_ = bf16[6656,2048]{1,0:T(8,128)(2,1)} custom-call(bf16[6656,128]{1,0:T(8,128)(2,1)} %hidden.1.refs_6_.refs_14_.refs_0_, bf16[6656,128]{1,0:T(8,128)(2,1)} %collective-permute-done.6.refs_16_.refs_15_.refs_1_, bf16[6656,128]{1,0:T(8,128)(2,1)} %collective-permute-done.4.refs_16_.refs_2_, ...), custom_call_target="tpu_custom_call", output_to_operand_aliasing={{}: (9, {})} | custom-call | flops 6979321856 | bytes 19529728 | tf_op jit(solution)/shard_map/weight_grad/pallas_call | solution.py:41
  195.4 3.2 %finish.4 = (bf16[128,6656]{1,0:T(8,128)(2,1)}, bf16[128,6656]{1,0:T(8,128)(2,1)}) custom-call(bf16[128,6656]{1,0:T(8,128)(2,1)} %refs_0_.9, bf16[128,6656]{1,0:T(8,128)(2,1)} %refs_1_.19, f32[4,1664,128]{2,1,0:T(8,128)} %get-tuple-element.158.refs_13_.refs_2_, bf16[4,1664,128]{2,1,0:T(8,128)(2,1)} %collective-permute-done.17.refs_3_, ...), custom_call_target="tpu_custom_call" | custom-call | bytes 9797632 | tf_op jit(solution)/shard_map/finish/pallas_call | solution.py:41
  198.6 3.2 %finish.5 = (bf16[128,6656]{1,0:T(8,128)(2,1)}, bf16[128,6656]{1,0:T(8,128)(2,1)}) custom-call(bf16[128,6656]{1,0:T(8,128)(2,1)} %refs_0_.9, bf16[128,6656]{1,0:T(8,128)(2,1)} %refs_1_.19, f32[4,1664,128]{2,1,0:T(8,128)} %get-tuple-element.161.refs_2_, ...), custom_call_target="tpu_custom_call", output_to_operand_aliasing={{0}: (6, {}), {1}: (7, {})} | custom-call | bytes 9797632 | tf_op jit(solution)/shard_map/finish/pallas_call | solution.py:41
  201.8 3.2 %finish.6 = (bf16[128,6656]{1,0:T(8,128)(2,1)}, bf16[128,6656]{1,0:T(8,128)(2,1)}) custom-call(bf16[128,6656]{1,0:T(8,128)(2,1)} %refs_0_.9, bf16[128,6656]{1,0:T(8,128)(2,1)} %refs_1_.19, f32[4,1664,128]{2,1,0:T(8,128)} %get-tuple-element.164.refs_2_, bf16[4,1664,128]{2,1,0:T(8,128)(2,1)} %copy-done.5, ...), custom_call_target="tpu_custom_call", output_to_operand_aliasing={{0}: (6, {}), {1}: (7, {})} | custom-call | bytes 9797632 | tf_op jit(solution)/shard_map/finish/pallas_call | solution.py:41
  205.0 3.2 %finish.7 = (bf16[128,6656]{1,0:T(8,128)(2,1)}, bf16[128,6656]{1,0:T(8,128)(2,1)}) custom-call(bf16[128,6656]{1,0:T(8,128)(2,1)} %refs_0_.9, bf16[128,6656]{1,0:T(8,128)(2,1)} %refs_1_.19, f32[4,1664,128]{2,1,0:T(8,128)} %get-tuple-element.167.refs_2_, bf16[4,1664,128]{2,1,0:T(8,128)(2,1)} %copy-done.4, ...), custom_call_target="tpu_custom_call", output_to_operand_aliasing={{0}: (6, {}), {1}: (7, {})} | custom-call | bytes 9797632 | tf_op jit(solution)/shard_map/finish/pallas_call | solution.py:41
  (46 shorter events, 3.0 us)
Async XLA Ops:
  5.0 41.3 %collective-permute-start.6 = (bf16[6656,128]{1,0:T(8,128)(2,1)}, bf16[6656,128]{1,0:T(8,128)(2,1)}, u32[]{:S(2)}, u32[]{:S(2)}) collective-permute-start(bf16[6656,128]{1,0:T(8,128)(2,1)} %hidden.1.refs_6_.refs_14_.refs_0_), channel_id=1, source_target_pairs={{0,4},{4,0},{8,12},{12,8},{16,20},{20,16},{24,28},{28,24},{1,5},{5... | collective-permute-start | bytes 5111816 | tf_op jit(solution)/shard_map/ppermute | solution.py:253
  5.1 59.8 %collective-permute-start.5 = (bf16[6656,128]{1,0:T(8,128)(2,1)}, bf16[6656,128]{1,0:T(8,128)(2,1)}, u32[]{:S(2)}, u32[]{:S(2)}) collective-permute-start(bf16[6656,128]{1,0:T(8,128)(2,1)} %hidden.1.refs_6_.refs_14_.refs_0_), channel_id=1, source_target_pairs={{0,16},{4,20},{8,24},{12,28},{16,0},{20,4},{24,8},{28,12},{1,17},{... | collective-permute-start | bytes 5111816 | tf_op jit(solution)/shard_map/ppermute | solution.py:253
  6.6 58.3 %collective-permute-start.4 = (bf16[6656,128]{1,0:T(8,128)(2,1)}, bf16[6656,128]{1,0:T(8,128)(2,1)}, u32[]{:S(2)}, u32[]{:S(2)}) collective-permute-start(bf16[6656,128]{1,0:T(8,128)(2,1)} %hidden.1.refs_6_.refs_14_.refs_0_), channel_id=1, source_target_pairs={{0,8},{4,12},{8,0},{12,4},{16,24},{20,28},{24,16},{28,20},{1,9},{5... | collective-permute-start | bytes 5111816 | tf_op jit(solution)/shard_map/ppermute | solution.py:253
  8.1 27.2 %collective-permute-start = (bf16[256,2048]{1,0:T(8,128)(2,1)}, bf16[256,2048]{1,0:T(8,128)(2,1)}, u32[]{:S(2)}, u32[]{:S(2)}) collective-permute-start(bf16[256,2048]{1,0:T(8,128)(2,1)} %refs_5_.1), channel_id=1, source_target_pairs={{0,1},{1,2},{2,3},{4,5},{5,6},{6,7},{8,9},{9,10},{10,11},{12,13},{... | collective-permute-start | bytes 3145736 | tf_op jit(solution)/shard_map/ppermute | solution.py:266
  11.5 26.9 %collective-permute-start.1 = (bf16[256,2048]{1,0:T(8,128)(2,1)}, bf16[256,2048]{1,0:T(8,128)(2,1)}, u32[]{:S(2)}, u32[]{:S(2)}) collective-permute-start(bf16[256,2048]{1,0:T(8,128)(2,1)} %refs_5_.1), channel_id=1, source_target_pairs={{1,0},{2,1},{3,2},{5,4},{6,5},{7,6},{9,8},{10,9},{11,10},{13,12},{... | collective-permute-start | bytes 3145736 | tf_op jit(solution)/shard_map/ppermute | solution.py:267
  38.5 31.2 %collective-permute-start.2 = (bf16[256,2048]{1,0:T(8,128)(2,1)}, bf16[256,2048]{1,0:T(8,128)(2,1)}, u32[]{:S(2)}, u32[]{:S(2)}) collective-permute-start(bf16[256,2048]{1,0:T(8,128)(2,1)} %collective-permute-done.refs_6_), channel_id=1, source_target_pairs={{1,2},{2,3},{5,6},{6,7},{9,10},{10,11},{13,14},{14,15},{17,18},{18... | collective-permute-start | bytes 3145736 | tf_op jit(solution)/shard_map/ppermute | solution.py:266
  40.4 29.3 %collective-permute-start.3 = (bf16[256,2048]{1,0:T(8,128)(2,1)}, bf16[256,2048]{1,0:T(8,128)(2,1)}, u32[]{:S(2)}, u32[]{:S(2)}) collective-permute-start(bf16[256,2048]{1,0:T(8,128)(2,1)} %collective-permute-done.1.refs_5_), channel_id=1, source_target_pairs={{1,0},{2,1},{5,4},{6,5},{9,8},{10,9},{13,12},{14,13},{17,16},{18,1... | collective-permute-start | bytes 3145736 | tf_op jit(solution)/shard_map/ppermute | solution.py:267
  69.7 30.1 %collective-permute-start.9 = (bf16[13312,128]{1,0:T(8,128)(2,1)}, bf16[13312,128]{1,0:T(8,128)(2,1)}, u32[]{:S(2)}, u32[]{:S(2)}) collective-permute-start(bf16[13312,128]{1,0:T(8,128)(2,1)} %pad_maximum_fusion), channel_id=1, source_target_pairs={{0,4},{4,0},{8,12},{12,8},{16,20},{20,16},{24,28},{28,24},{1,5},{5... | collective-permute-start | bytes 10223624 | tf_op jit(solution)/shard_map/ppermute | solution.py:253
  69.8 29.0 %collective-permute-start.8 = (bf16[256,2048]{1,0:T(8,128)(2,1)}, bf16[256,2048]{1,0:T(8,128)(2,1)}, u32[]{:S(2)}, u32[]{:S(2)}) collective-permute-start(bf16[256,2048]{1,0:T(8,128)(2,1)} %collective-permute-done.3.refs_6_.refs_5_), channel_id=1, source_target_pairs={{1,0},{5,4},{9,8},{13,12},{17,16},{21,20},{25,24},{29,28}} | collective-permute-start | bytes 3145736 | tf_op jit(solution)/shard_map/ppermute | solution.py:267
  71.4 27.3 %collective-permute-start.7 = (bf16[256,2048]{1,0:T(8,128)(2,1)}, bf16[256,2048]{1,0:T(8,128)(2,1)}, u32[]{:S(2)}, u32[]{:S(2)}) collective-permute-start(bf16[256,2048]{1,0:T(8,128)(2,1)} %collective-permute-done.2.refs_7_), channel_id=1, source_target_pairs={{2,3},{6,7},{10,11},{14,15},{18,19},{22,23},{26,27},{30,31}} | collective-permute-start | bytes 3145736 | tf_op jit(solution)/shard_map/ppermute | solution.py:266
  77.9 21.5 %collective-permute-start.11 = (bf16[3328,128]{1,0:T(8,128)(2,1)}, bf16[3328,128]{1,0:T(8,128)(2,1)S(1)}, u32[]{:S(2)}, u32[]{:S(2)}) collective-permute-start(bf16[3328,128]{1,0:T(8,128)(2,1)} %slice.67), channel_id=1, source_target_pairs={{0,8},{4,12},{8,0},{12,4},{16,24},{20,28},{24,16},{28,20},{1,9},{5... | collective-permute-start | bytes 2555912 | tf_op jit(solution)/shard_map/ppermute | solution.py:253
  78.4 21.4 %collective-permute-start.10 = (bf16[3328,128]{1,0:T(8,128)(2,1)}, bf16[3328,128]{1,0:T(8,128)(2,1)}, u32[]{:S(2)}, u32[]{:S(2)}) collective-permute-start(bf16[3328,128]{1,0:T(8,128)(2,1)} %slice.66), channel_id=1, source_target_pairs={{0,16},{4,20},{8,24},{12,28},{16,0},{20,4},{24,8},{28,12},{1,17},{... | collective-permute-start | bytes 2555912 | tf_op jit(solution)/shard_map/ppermute | solution.py:253
  99.4 0.9 copy-start.3
  99.8 12.3 %collective-permute-start.12 = (bf16[3328,128]{1,0:T(8,128)(2,1)}, bf16[3328,128]{1,0:T(8,128)(2,1)}, u32[]{:S(2)}, u32[]{:S(2)}) collective-permute-start(bf16[3328,128]{1,0:T(8,128)(2,1)} %collective-permute-done.10.refs_20_.refs_6_), channel_id=1, source_target_pairs={{0,4},{4,0},{8,12},{12,8},{16,20},{20,16},{24,28},{28,24},{1,5},{5... | collective-permute-start | bytes 2555912 | tf_op jit(solution)/shard_map/ppermute | solution.py:253
  99.8 12.3 %collective-permute-start.13 = (bf16[3328,128]{1,0:T(8,128)(2,1)S(1)}, bf16[3328,128]{1,0:T(8,128)(2,1)}, u32[]{:S(2)}, u32[]{:S(2)}) collective-permute-start(bf16[3328,128]{1,0:T(8,128)(2,1)S(1)} %collective-permute-done.11.refs_21_.refs_6_), channel_id=1, source_target_pairs={{0,4},{4,0},{8,12},{12,8},{16,20},{20,16},{24,28},{28,24},{1,5},{5... | collective-permute-start | bytes 2555912 | tf_op jit(solution)/shard_map/ppermute | solution.py:253
  111.5 12.4 %collective-permute-start.17 = (bf16[4,1664,128]{2,1,0:T(8,128)(2,1)}, bf16[4,1664,128]{2,1,0:T(8,128)(2,1)}, u32[]{:S(2)}, u32[]{:S(2)}) collective-permute-start(bf16[4,1664,128]{2,1,0:T(8,128)(2,1)} %get-tuple-element.147), channel_id=1, source_target_pairs={{0,4},{4,0},{8,12},{12,8},{16,20},{20,16},{24,28},{28,24},{1,5},{5... | collective-permute-start | bytes 5111816 | tf_op jit(solution)/shard_map/ppermute | solution.py:253
  111.6 16.7 %collective-permute-start.16 = (bf16[4,1664,128]{2,1,0:T(8,128)(2,1)}, bf16[4,1664,128]{2,1,0:T(8,128)(2,1)}, u32[]{:S(2)}, u32[]{:S(2)}) collective-permute-start(bf16[4,1664,128]{2,1,0:T(8,128)(2,1)} %get-tuple-element.146), channel_id=1, source_target_pairs={{0,4},{4,0},{8,12},{12,8},{16,20},{20,16},{24,28},{28,24},{1,5},{5... | collective-permute-start | bytes 5111816 | tf_op jit(solution)/shard_map/ppermute | solution.py:253
  123.3 8.4 %collective-permute-start.15 = (bf16[4,1664,128]{2,1,0:T(8,128)(2,1)}, bf16[4,1664,128]{2,1,0:T(8,128)(2,1)S(1)}, u32[]{:S(2)}, u32[]{:S(2)}) collective-permute-start(bf16[4,1664,128]{2,1,0:T(8,128)(2,1)} %get-tuple-element.144), channel_id=1, source_target_pairs={{0,4},{4,0},{8,12},{12,8},{16,20},{20,16},{24,28},{28,24},{1,5},{5... | collective-permute-start | bytes 5111816 | tf_op jit(solution)/shard_map/ppermute | solution.py:253
  123.5 9.9 %collective-permute-start.14 = (bf16[4,1664,128]{2,1,0:T(8,128)(2,1)}, bf16[4,1664,128]{2,1,0:T(8,128)(2,1)S(1)}, u32[]{:S(2)}, u32[]{:S(2)}) collective-permute-start(bf16[4,1664,128]{2,1,0:T(8,128)(2,1)} %get-tuple-element.142), channel_id=1, source_target_pairs={{0,4},{4,0},{8,12},{12,8},{16,20},{20,16},{24,28},{28,24},{1,5},{5... | collective-permute-start | bytes 5111816 | tf_op jit(solution)/shard_map/ppermute | solution.py:253
  123.9 4.4 %copy-start = (f32[4,1664,128]{2,1,0:T(8,128)S(1)}, f32[4,1664,128]{2,1,0:T(8,128)}, u32[]{:S(2)}) copy-start(f32[4,1664,128]{2,1,0:T(8,128)} %get-tuple-element.161.refs_2_) | copy-start | bytes 10223620
  126.9 29.8 %collective-permute-start.20 = (bf16[2,1664,128]{2,1,0:T(8,128)(2,1)}, bf16[2,1664,128]{2,1,0:T(8,128)(2,1)}, u32[]{:S(2)}, u32[]{:S(2)}) collective-permute-start(bf16[2,1664,128]{2,1,0:T(8,128)(2,1)} %add_convert_fusion.3), channel_id=1, source_target_pairs={{0,8},{4,12},{8,0},{12,4},{16,24},{20,28},{24,16},{28,20},{1,9},{5... | collective-permute-start | bytes 2555912 | tf_op jit(solution)/shard_map/ppermute | solution.py:253
  128.3 3.4 %copy-start.1 = (f32[4,1664,128]{2,1,0:T(8,128)S(1)}, f32[4,1664,128]{2,1,0:T(8,128)}, u32[]{:S(2)}) copy-start(f32[4,1664,128]{2,1,0:T(8,128)} %get-tuple-element.164.refs_2_) | copy-start | bytes 10223620
  130.8 2.6 %copy-start.2 = (f32[4,1664,128]{2,1,0:T(8,128)S(1)}, f32[4,1664,128]{2,1,0:T(8,128)}, u32[]{:S(2)}) copy-start(f32[4,1664,128]{2,1,0:T(8,128)} %get-tuple-element.167.refs_2_) | copy-start | bytes 10223620
  130.8 28.9 %collective-permute-start.21 = (bf16[2,1664,128]{2,1,0:T(8,128)(2,1)}, bf16[2,1664,128]{2,1,0:T(8,128)(2,1)}, u32[]{:S(2)}, u32[]{:S(2)}) collective-permute-start(bf16[2,1664,128]{2,1,0:T(8,128)(2,1)} %add_convert_fusion.2), channel_id=1, source_target_pairs={{0,16},{4,20},{8,24},{12,28},{16,0},{20,4},{24,8},{28,12},{1,17},{... | collective-permute-start | bytes 2555912 | tf_op jit(solution)/shard_map/ppermute | solution.py:253
  131.7 1.6 copy-start.5
  132.8 43.3 %collective-permute-start.19 = (bf16[2,1664,128]{2,1,0:T(8,128)(2,1)}, bf16[2,1664,128]{2,1,0:T(8,128)(2,1)}, u32[]{:S(2)}, u32[]{:S(2)}) collective-permute-start(bf16[2,1664,128]{2,1,0:T(8,128)(2,1)} %add_convert_fusion.1), channel_id=1, source_target_pairs={{0,8},{4,12},{8,0},{12,4},{16,24},{20,28},{24,16},{28,20},{1,9},{5... | collective-permute-start | bytes 2555912 | tf_op jit(solution)/shard_map/ppermute | solution.py:253
  133.4 1.5 copy-start.4
  134.8 44.9 %collective-permute-start.18 = (bf16[2,1664,128]{2,1,0:T(8,128)(2,1)}, bf16[2,1664,128]{2,1,0:T(8,128)(2,1)S(1)}, u32[]{:S(2)}, u32[]{:S(2)}) collective-permute-start(bf16[2,1664,128]{2,1,0:T(8,128)(2,1)} %add_convert_fusion.refs_9_), channel_id=1, source_target_pairs={{0,16},{4,20},{8,24},{12,28},{16,0},{20,4},{24,8},{28,12},{1,17},{... | collective-permute-start | bytes 2555912 | tf_op jit(solution)/shard_map/ppermute | solution.py:253
  158.9 36.4 %collective-permute-start.25 = (bf16[1,1664,128]{2,1,0:T(8,128)(2,1)}, bf16[1,1664,128]{2,1,0:T(8,128)(2,1)}, u32[]{:S(2)}, u32[]{:S(2)}) collective-permute-start(bf16[1,1664,128]{2,1,0:T(8,128)(2,1)} %add_convert_fusion.7), channel_id=1, source_target_pairs={{0,16},{4,20},{8,24},{12,28},{16,0},{20,4},{24,8},{28,12},{1,17},{... | collective-permute-start | bytes 1277960 | tf_op jit(solution)/shard_map/ppermute | solution.py:253
  162.0 36.6 %collective-permute-start.24 = (bf16[1,1664,128]{2,1,0:T(8,128)(2,1)}, bf16[1,1664,128]{2,1,0:T(8,128)(2,1)}, u32[]{:S(2)}, u32[]{:S(2)}) collective-permute-start(bf16[1,1664,128]{2,1,0:T(8,128)(2,1)} %add_convert_fusion.6.refs_10_), channel_id=1, source_target_pairs={{0,8},{4,12},{8,0},{12,4},{16,24},{20,28},{24,16},{28,20},{1,9},{5... | collective-permute-start | bytes 1277960 | tf_op jit(solution)/shard_map/ppermute | solution.py:253
  178.5 23.3 %collective-permute-start.23 = (bf16[1,1664,128]{2,1,0:T(8,128)(2,1)}, bf16[1,1664,128]{2,1,0:T(8,128)(2,1)}, u32[]{:S(2)}, u32[]{:S(2)}) collective-permute-start(bf16[1,1664,128]{2,1,0:T(8,128)(2,1)} %add_convert_fusion.5), channel_id=1, source_target_pairs={{0,16},{4,20},{8,24},{12,28},{16,0},{20,4},{24,8},{28,12},{1,17},{... | collective-permute-start | bytes 1277960 | tf_op jit(solution)/shard_map/ppermute | solution.py:253
  179.7 15.7 %copy-start.6 = (bf16[2,1664,128]{2,1,0:T(8,128)(2,1)}, bf16[2,1664,128]{2,1,0:T(8,128)(2,1)S(1)}, u32[]{:S(2)}) copy-start(bf16[2,1664,128]{2,1,0:T(8,128)(2,1)S(1)} %collective-permute-done.18.refs_4_) | copy-start | bytes 2555908
  182.2 22.9 %collective-permute-start.22 = (bf16[1,1664,128]{2,1,0:T(8,128)(2,1)}, bf16[1,1664,128]{2,1,0:T(8,128)(2,1)}, u32[]{:S(2)}, u32[]{:S(2)}) collective-permute-start(bf16[1,1664,128]{2,1,0:T(8,128)(2,1)} %add_convert_fusion.4.refs_10_), channel_id=1, source_target_pairs={{0,8},{4,12},{8,0},{12,4},{16,24},{20,28},{24,16},{28,20},{1,9},{5... | collective-permute-start | bytes 1277960 | tf_op jit(solution)/shard_map/ppermute | solution.py:253

commit v8 on v7

--- a/solution.py
+++ b/solution.py
@@ -12,10 +12,10 @@
 VMEM_LIMIT = 63 * 1024 * 1024
 CHUNKS = 4
 GROUPS = 2
-PARTS = [(0, 2), (2, 3), (3, 4)]
+PARTS = [(0, 3), (3, 4)]
 SPLIT = 4
 LANES = 128
-PLAN = ["P0 P1 S0 S1", "S2 S3 W0 S0", "S1 W1 S2 S3", "W2 F0 F1 F2", "F3"]
+PLAN = ["P0 P1 S0 S1", "S2 S3 W0 S0", "S1 S2 S3 W1", "F0 F1 F2 F3"]
 
 
 def divisor(extent, most, step):
@@ -179,8 +179,8 @@
     return run(finish_kernel, "finish", (1,), ins, outs, deps, exps=tokens * width)
 
 
-def weight_grad_kernel(*refs):
-    pieces, (source, out_ref, dy_ref, sems) = refs[:-4], refs[-4:]
+def weight_grad_kernel(switch, shared, *refs):
+    pieces, (source, out_ref, dy_ref, sems) = list(refs[:-4]), refs[-4:]
 
     @pl.when(pl.program_id(0) == 0)
     def _():
@@ -195,27 +195,42 @@
         for copy in copies:
             copy.wait()
 
-    hidden = jnp.concatenate([ref[...] for ref in pieces], axis=1)
+    blocks = []
+    for count in shared:
+        block = pieces.pop(0)[...]
+        if count == 2:
+            block = jnp.where(pl.program_id(0) < switch, block, pieces.pop(0)[...])
+        blocks.append(block)
+    hidden = jnp.concatenate(blocks, axis=1)
     out_ref[...] = jnp.dot(hidden, dy_ref[...], preferred_element_type=F32).astype(BF16)
 
 
 def weight_grad(pieces, dy, whole, total, start, rows, deps):
-    block = pieces[0][0].shape[1]
+    block = pieces[0][0][0].shape[1]
     tokens, depth = dy.shape
-    tall = divisor(rows, 416, 16)
-
-    def spec(base):
-        return pl.BlockSpec((tall, block), lambda i: ((start - base) // tall + i, 0))
-
-    ins = [(x, spec(base)) for x, base in pieces]
+    middle = total // 2
+    if start < middle < start + rows:
+        tall = divisor(math.gcd(rows, middle - start), 416, 16)
+        switch = (middle - start) // tall
+    else:
+        tall = divisor(rows, 416, 16)
+        switch = 0
+        pieces = [p if len(p) == 1 else [p[start >= middle]] for p in pieces]
+
+    def spec(x, base):
+        last = x.shape[0] // tall - 1
+        return pl.BlockSpec(
+            (tall, block), lambda i: (jnp.clip((start - base) // tall + i, 0, last), 0)
+        )
+
+    ins = [(x, spec(x, base)) for p in pieces for x, base in p]
     ins.append((dy, pl.BlockSpec(memory_space=pl.ANY)))
     place = pl.BlockSpec((tall, depth), lambda i: (start // tall + i, 0))
     out = ((total, depth), BF16, place, whole)
     scratch = [pltpu.VMEM((tokens, depth), BF16), pltpu.SemaphoreType.DMA((8,))]
     flops = 2 * rows * tokens * depth
-    return run(
-        weight_grad_kernel, "weight_grad", (rows // tall,), ins, [out], deps, None, scratch, flops
-    )[0]
+    kernel = functools.partial(weight_grad_kernel, switch, [len(p) for p in pieces])
+    return run(kernel, "weight_grad", (rows // tall,), ins, [out], deps, None, scratch, flops)[0]
 
 
 def arrivals(z, count):
@@ -369,8 +384,7 @@
             )
             return grad_up
         start, stop = (width * x // 4 for x in PARTS[n])
-        side = -1 if start >= half else 0
-        pieces = [(held[f][side], base[f][side]) for f in range(row_count)]
+        pieces = [list(zip(held[f], base[f])) for f in range(row_count)]
         grad_down = weight_grad(pieces, ordered, grad_down, width, start, stop - start, [last])
         return grad_down
 

time: 209 us -> 206 us (0.986)
  Pallas kernels: 141 us -> 137 us
    pallas_call x13 -> x12, Pallas kernels: 141 us -> 137 us  [run(): pl.pallas_call(body, grid_spec=pltpu.PrefetchScalarGridSpec(num_scalar_pr...]
  transfers between devices with their start and end apart: 26 -> 26, of which waited for: 4 -> 4; matrix products, arithmetic and copies ran while one was open for 14% -> 14% of each run, Pallas kernels for 64% -> 63%
where the time goes in v8:
time: 206 us; the launch traced here: 205 us
  Pallas kernels  137 us (67%)
  starting transfers between devices  31.6 us (15%)
  other arithmetic  22 us (11%)
  local copies, waits for them, and re-layouts  7.05 us (3%)
  waiting for transfers between devices  5.77 us (3%)
    pallas_call x12, Pallas kernels, run(): pl.pallas_call(body, grid_spec=pltpu.PrefetchScalarGridSpec(num_scalar_pr...  137 us
    convert_element_type x8, other arithmetic, step(): send = sum((t[rows:2 * rows].astype(F32) for t in sums[n])).astype(BF16)  17.1 us
    ppermute x20, starting transfers between devices, swap(): return jax.tree.map(lambda x: lax.ppermute(x, 'row', pairs), x)  14 us
    ppermute x3, starting transfers between devices, forward(): lax.ppermute(down[-1], 'col', [(i, i - 1) for i in range(1, col_count - s...  9.89 us
    ppermute x3, starting transfers between devices, forward(): lax.ppermute(up[-1], 'col', [(i, i + 1) for i in range(s - 1, col_count -...  7.64 us
    concatenate x1, other arithmetic, program(): both = [jnp.concatenate(held[a] + held[b])]  4.87 us
    slice x2, local copies, waits for them, and re-layouts, program(): held[a | b] = [swap(held[a][0][:half], b), swap(held[b][0][half:], a)]  4.22 us
  transfers between devices with their start and end apart: 26, of which 4 were waited for; matrix products, arithmetic and copies ran while one was open for 14% of the time, Pallas kernels for 63%

profile of v8, /device:TPU:16, one launch (start us, length us, event | category | flops | bytes accessed | tf_op | source)
XLA Modules:
  0.0 204.5 jit_solution(18303635683675125941)
XLA Ops:
  0.6 4.4 %hidden.1.refs_6_.refs_14_.refs_0_ = bf16[6656,128]{1,0:T(8,128)(2,1)} custom-call(bf16[128,6656]{1,0:T(8,128)(2,1)} %refs_0_.9, bf16[128,6656]{1,0:T(8,128)(2,1)} %refs_1_.19), custom_call_target="tpu_custom_call" | custom-call | bytes 3407872 | tf_op jit(solution)/shard_map/hidden/pallas_call | solution.py:41
  5.1 1.5 collective-permute-start.5
  6.6 1.5 collective-permute-start.4
  8.1 3.5 %collective-permute-start = (bf16[256,2048]{1,0:T(8,128)(2,1)}, bf16[256,2048]{1,0:T(8,128)(2,1)}, u32[]{:S(2)}, u32[]{:S(2)}) collective-permute-start(bf16[256,2048]{1,0:T(8,128)(2,1)} %refs_5_.1), channel_id=1, source_target_pairs={{0,1},{1,2},{2,3},{4,5},{5,6},{6,7},{8,9},{9,10},{10,11},{12,13},{... | collective-permute-start | bytes 3145736 | tf_op jit(solution)/shard_map/ppermute | solution.py:281
  11.5 2.4 %collective-permute-start.1 = (bf16[256,2048]{1,0:T(8,128)(2,1)}, bf16[256,2048]{1,0:T(8,128)(2,1)}, u32[]{:S(2)}, u32[]{:S(2)}) collective-permute-start(bf16[256,2048]{1,0:T(8,128)(2,1)} %refs_5_.1), channel_id=1, source_target_pairs={{1,0},{2,1},{3,2},{5,4},{6,5},{7,6},{9,8},{10,9},{11,10},{13,12},{... | collective-permute-start | bytes 3145736 | tf_op jit(solution)/shard_map/ppermute | solution.py:282
  14.0 0.7 stack.91.refs_0_
  14.7 0.6 stack.86.refs_0_
  15.3 18.5 %hidden_grad_terms.5 = (f32[4,1664,128]{2,1,0:T(8,128)}, bf16[4,1664,128]{2,1,0:T(8,128)(2,1)}, f32[4,1664,128]{2,1,0:T(8,128)}, bf16[4,1664,128]{2,1,0:T(8,128)...) custom-call(s32[6]{0:T(128)} %stack.86.refs_0_, ...), custom_call_target="tpu_custom_call" | custom-call | flops 6979321856 | bytes 110100480 | tf_op jit(solution)/shard_map/hidden_grad_terms/pallas_call | solution.py:41
  33.8 1.5 collective-permute-done.refs_6_
  35.3 3.2 %collective-permute-done.1.refs_5_ = bf16[256,2048]{1,0:T(8,128)(2,1)} collective-permute-done((bf16[256,2048]{1,0:T(8,128)(2,1)}, bf16[256,2048]{1,0:T(8,128)(2,1)}, u32[]{:S(2)}, u32[]{:S(2)}) %collective-permute-start.1) | collective-permute-done | bytes 1048608 | tf_op jit(solution)/shard_map/ppermute | solution.py:282
  38.5 1.9 collective-permute-start.2
  40.4 5.9 %collective-permute-start.3 = (bf16[256,2048]{1,0:T(8,128)(2,1)}, bf16[256,2048]{1,0:T(8,128)(2,1)}, u32[]{:S(2)}, u32[]{:S(2)}) collective-permute-start(bf16[256,2048]{1,0:T(8,128)(2,1)} %collective-permute-done.1.refs_5_), channel_id=1, source_target_pairs={{1,0},{2,1},{5,4},{6,5},{9,8},{10,9},{13,12},{14,13},{17,16},{18,1... | collective-permute-start | bytes 3145736 | tf_op jit(solution)/shard_map/ppermute | solution.py:282
  46.3 18.5 %hidden_grad_terms.6 = (f32[4,1664,128]{2,1,0:T(8,128)}, bf16[4,1664,128]{2,1,0:T(8,128)(2,1)}, f32[4,1664,128]{2,1,0:T(8,128)}, bf16[4,1664,128]{2,1,0:T(8,128)...) custom-call(s32[6]{0:T(128)} %stack.91.refs_0_, ...), custom_call_target="tpu_custom_call", output_to_operand_aliasing={{0}: (7, {}), {1}: (8, {}), {2}: (9, {}), {3}: (10, {}), {4... | custom-call | flops 6979321856 | bytes 111149056 | tf_op jit(solution)/shard_map/hidden_grad_terms/pallas_call | solution.py:41
  64.8 4.9 %pad_maximum_fusion = bf16[13312,128]{1,0:T(8,128)(2,1)} fusion(bf16[6656,128]{1,0:T(8,128)(2,1)} %collective-permute-done.5.refs_18_.refs_4_, bf16[6656,128]{1,0:T(8,128)(2,1)} %collective-permute-done.4.refs_16_.refs_2_), kind=kLoop, calls=%fused_computation | loop fusion | flops 6815744 | bytes 6815744 | tf_op jit(solution)/shard_map/concatenate | solution.py:335
  69.8 1.6 collective-permute-start.8
  71.4 2.3 %collective-permute-start.7 = (bf16[256,2048]{1,0:T(8,128)(2,1)}, bf16[256,2048]{1,0:T(8,128)(2,1)}, u32[]{:S(2)}, u32[]{:S(2)}) collective-permute-start(bf16[256,2048]{1,0:T(8,128)(2,1)} %collective-permute-done.2.refs_7_), channel_id=1, source_target_pairs={{2,3},{6,7},{10,11},{14,15},{18,19},{22,23},{26,27},{30,31}} | collective-permute-start | bytes 3145736 | tf_op jit(solution)/shard_map/ppermute | solution.py:281
  73.7 2.1 %slice.66 = bf16[3328,128]{1,0:T(8,128)(2,1)} slice(bf16[6656,128]{1,0:T(8,128)(2,1)} %collective-permute-done.4.refs_16_.refs_2_), slice={[0:3328], [0:128]} | slice | bytes 1703936 | tf_op jit(solution)/shard_map/slice | solution.py:344
  75.8 2.1 %slice.67 = bf16[3328,128]{1,0:T(8,128)(2,1)} slice(bf16[6656,128]{1,0:T(8,128)(2,1)} %collective-permute-done.5.refs_18_.refs_4_), slice={[3328:6656], [0:128]} | slice | bytes 1703936 | tf_op jit(solution)/shard_map/slice | solution.py:344
  77.9 0.5 collective-permute-start.11
  78.4 0.5 collective-permute-start.10
  79.0 0.6 stack.82.refs_0_
  79.6 0.7 stack.96.refs_0_
  80.3 18.5 %hidden_grad_terms.7 = (f32[4,1664,128]{2,1,0:T(8,128)}, bf16[4,1664,128]{2,1,0:T(8,128)(2,1)}, f32[4,1664,128]{2,1,0:T(8,128)}, bf16[4,1664,128]{2,1,0:T(8,128)...) custom-call(s32[6]{0:T(128)} %stack.96.refs_0_, ...), custom_call_target="tpu_custom_call", output_to_operand_aliasing={{0}: (8, {}), {1}: (9, {}), {2}: (10, {}), {3}: (11, {}), {... | custom-call | flops 6979321856 | bytes 112197632 | tf_op jit(solution)/shard_map/hidden_grad_terms/pallas_call | solution.py:41
  98.8 0.7 collective-permute-done.11.refs_21_.refs_7_.refs_6_
  100.4 11.2 %hidden_grad_terms.8 = (f32[4,1664,128]{2,1,0:T(8,128)}, bf16[4,1664,128]{2,1,0:T(8,128)(2,1)}, f32[4,1664,128]{2,1,0:T(8,128)}, bf16[4,1664,128]{2,1,0:T(8,128)(2,1)}, bf16[1024,2048]{1,0:T(8,128)(2,1)}) custom-call(s32[6]{0:T(128)} %stack.82.refs_0_, ...), custom_call_target="tpu_custom_call", output_to_operand_aliasing={{0}: (9, {}), {1}: (10, {}), {2}: (11, {}), {3}: (12, {}), ... | custom-call | flops 3489660928 | bytes 113246208 | tf_op jit(solution)/shard_map/hidden_grad_terms/pallas_call | solution.py:41
  112.1 11.2 %hidden_grad_terms.9 = (f32[4,1664,128]{2,1,0:T(8,128)}, bf16[4,1664,128]{2,1,0:T(8,128)(2,1)}, f32[4,1664,128]{2,1,0:T(8,128)}, bf16[4,1664,128]{2,1,0:T(8,128)(2,1)}) custom-call(s32[6]{0:T(128)} %stack.82.refs_0_, bf16[6656,2048]{1,0:T(8,128)(2,1)} %refs_4_.9, ...), custom_call_target="tpu_custom_call", output_to_operand_aliasing={{0}: (9, {}), {1}: (10, {}), {2}: (11, {}), {3}: (12, {})} | custom-call | flops 3489660928 | bytes 113246208 | tf_op jit(solution)/shard_map/hidden_grad_terms/pallas_call | solution.py:41
  123.9 2.9 %add_convert_fusion.3 = bf16[2,1664,128]{2,1,0:T(8,128)(2,1)} fusion(f32[4,1664,128]{2,1,0:T(8,128)} %get-tuple-element.156.refs_13_.refs_2_, bf16[4,1664,128]{2,1,0:T(8,128)(2,1)} %collective-permute-done.17.refs_3_), kind=kLoop, calls=%fused_computation.4 | loop fusion | flops 1277952 | bytes 3407872 | tf_op jit(solution)/shard_map/convert_element_type | solution.py:378
  126.9 1.4 collective-permute-start.21
  128.3 2.5 %add_convert_fusion.2 = bf16[2,1664,128]{2,1,0:T(8,128)(2,1)} fusion(f32[4,1664,128]{2,1,0:T(8,128)S(1)} %copy-done, bf16[4,1664,128]{2,1,0:T(8,128)(2,1)} %collective-permute-done.16.refs_3_), kind=kLoop, calls=%fused_computation.3 | loop fusion | flops 1277952 | bytes 3407872 | tf_op jit(solution)/shard_map/convert_element_type | solution.py:378
  130.8 0.9 collective-permute-start.20
  131.7 1.1 add_convert_fusion.1
  132.8 0.6 collective-permute-start.19
  133.4 1.2 add_convert_fusion.refs_11_
  134.8 1.3 collective-permute-start.18
  136.1 29.4 %weight_grad.2.refs_9_ = bf16[6656,2048]{1,0:T(8,128)(2,1)} custom-call(bf16[6656,128]{1,0:T(8,128)(2,1)} %hidden.1.refs_6_.refs_14_.refs_0_, bf16[6656,128]{1,0:T(8,128)(2,1)} %collective-permute-done.6.refs_16_.refs_15_.refs_1_, bf16[6656,128]{1,0:T(8,128)(2,1)} %collective-permute-done.4.refs_16_.refs_2_, ...), custom_call_target="tpu_custom_call" | custom-call | flops 20937965568 | bytes 21233664 | tf_op jit(solution)/shard_map/weight_grad/pallas_call | solution.py:41
  165.4 2.3 %add_convert_fusion.7 = bf16[1,1664,128]{2,1,0:T(8,128)(2,1)} fusion(f32[4,1664,128]{2,1,0:T(8,128)} %get-tuple-element.156.refs_13_.refs_2_, bf16[2,1664,128]{2,1,0:T(8,128)(2,1)} %collective-permute-done.21.refs_4_, bf16[4,1664,128]{2,1,0:T(8,128)(2,1)} %collective-permute-done.17.refs_3_), kind=kLoop, calls=%fused_computation.8 | loop fusion | flops 1064960 | bytes 2129920 | tf_op jit(solution)/shard_map/convert_element_type | solution.py:378
  167.8 0.8 collective-permute-start.25
  168.5 2.3 %add_convert_fusion.6 = bf16[1,1664,128]{2,1,0:T(8,128)(2,1)} fusion(f32[4,1664,128]{2,1,0:T(8,128)} %get-tuple-element.159.refs_2_, bf16[2,1664,128]{2,1,0:T(8,128)(2,1)} %collective-permute-done.20.refs_4_, bf16[4,1664,128]{2,1,0:T(8,128)(2,1)} %collective-permute-done.16.refs_3_), kind=kLoop, calls=%fused_computation.7 | loop fusion | flops 1064960 | bytes 2129920 | tf_op jit(solution)/shard_map/convert_element_type | solution.py:378
  170.8 1.5 collective-permute-start.24
  172.3 2.3 %add_convert_fusion.5 = bf16[1,1664,128]{2,1,0:T(8,128)(2,1)} fusion(f32[4,1664,128]{2,1,0:T(8,128)} %get-tuple-element.162.refs_2_, bf16[2,1664,128]{2,1,0:T(8,128)(2,1)} %collective-permute-done.19.refs_4_, bf16[4,1664,128]{2,1,0:T(8,128)(2,1)} %copy-done.5), kind=kLoop, calls=%fused_computation.6 | loop fusion | flops 1064960 | bytes 2129920 | tf_op jit(solution)/shard_map/convert_element_type | solution.py:378
  174.7 1.2 collective-permute-start.23
  175.9 2.5 %add_convert_fusion.4.refs_10_ = bf16[1,1664,128]{2,1,0:T(8,128)(2,1)} fusion(f32[4,1664,128]{2,1,0:T(8,128)} %get-tuple-element.165.refs_2_, bf16[2,1664,128]{2,1,0:T(8,128)(2,1)S(1)} %collective-permute-done.18.refs_4_, bf16[4,1664,128]{2,1,0:T(8,128)(2,1)} %copy-done.4), kind=kLoop, calls=%fused_computation.5 | loop fusion | flops 1064960 | bytes 2129920 | tf_op jit(solution)/shard_map/convert_element_type | solution.py:378
  178.3 0.6 collective-permute-start.22
  178.9 12.7 %weight_grad.3.refs_6_ = bf16[6656,2048]{1,0:T(8,128)(2,1)} custom-call(bf16[6656,128]{1,0:T(8,128)(2,1)} %hidden.1.refs_6_.refs_14_.refs_0_, bf16[6656,128]{1,0:T(8,128)(2,1)} %collective-permute-done.6.refs_16_.refs_15_.refs_1_, bf16[6656,128]{1,0:T(8,128)(2,1)} %collective-permute-done.4.refs_16_.refs_2_, ...), custom_call_target="tpu_custom_call", output_to_operand_aliasing={{}: (9, {})} | custom-call | flops 6979321856 | bytes 19529728 | tf_op jit(solution)/shard_map/weight_grad/pallas_call | solution.py:41
  191.7 3.2 %finish.4 = (bf16[128,6656]{1,0:T(8,128)(2,1)}, bf16[128,6656]{1,0:T(8,128)(2,1)}) custom-call(bf16[128,6656]{1,0:T(8,128)(2,1)} %refs_0_.9, bf16[128,6656]{1,0:T(8,128)(2,1)} %refs_1_.19, f32[4,1664,128]{2,1,0:T(8,128)} %get-tuple-element.156.refs_13_.refs_2_, bf16[4,1664,128]{2,1,0:T(8,128)(2,1)} %collective-permute-done.17.refs_3_, ...), custom_call_target="tpu_custom_call" | custom-call | bytes 9797632 | tf_op jit(solution)/shard_map/finish/pallas_call | solution.py:41
  194.9 3.2 %finish.5 = (bf16[128,6656]{1,0:T(8,128)(2,1)}, bf16[128,6656]{1,0:T(8,128)(2,1)}) custom-call(bf16[128,6656]{1,0:T(8,128)(2,1)} %refs_0_.9, bf16[128,6656]{1,0:T(8,128)(2,1)} %refs_1_.19, f32[4,1664,128]{2,1,0:T(8,128)} %get-tuple-element.159.refs_2_, ...), custom_call_target="tpu_custom_call", output_to_operand_aliasing={{0}: (6, {}), {1}: (7, {})} | custom-call | bytes 9797632 | tf_op jit(solution)/shard_map/finish/pallas_call | solution.py:41
  198.1 3.2 %finish.6 = (bf16[128,6656]{1,0:T(8,128)(2,1)}, bf16[128,6656]{1,0:T(8,128)(2,1)}) custom-call(bf16[128,6656]{1,0:T(8,128)(2,1)} %refs_0_.9, bf16[128,6656]{1,0:T(8,128)(2,1)} %refs_1_.19, f32[4,1664,128]{2,1,0:T(8,128)} %get-tuple-element.162.refs_2_, bf16[4,1664,128]{2,1,0:T(8,128)(2,1)} %copy-done.5, ...), custom_call_target="tpu_custom_call", output_to_operand_aliasing={{0}: (6, {}), {1}: (7, {})} | custom-call | bytes 9797632 | tf_op jit(solution)/shard_map/finish/pallas_call | solution.py:41
  201.3 3.2 %finish.7 = (bf16[128,6656]{1,0:T(8,128)(2,1)}, bf16[128,6656]{1,0:T(8,128)(2,1)}) custom-call(bf16[128,6656]{1,0:T(8,128)(2,1)} %refs_0_.9, bf16[128,6656]{1,0:T(8,128)(2,1)} %refs_1_.19, f32[4,1664,128]{2,1,0:T(8,128)} %get-tuple-element.165.refs_2_, bf16[4,1664,128]{2,1,0:T(8,128)(2,1)} %copy-done.4, ...), custom_call_target="tpu_custom_call", output_to_operand_aliasing={{0}: (6, {}), {1}: (7, {})} | custom-call | bytes 9797632 | tf_op jit(solution)/shard_map/finish/pallas_call | solution.py:41
  (45 shorter events, 2.4 us)
Async XLA Ops:
  5.0 41.3 %collective-permute-start.6 = (bf16[6656,128]{1,0:T(8,128)(2,1)}, bf16[6656,128]{1,0:T(8,128)(2,1)}, u32[]{:S(2)}, u32[]{:S(2)}) collective-permute-start(bf16[6656,128]{1,0:T(8,128)(2,1)} %hidden.1.refs_6_.refs_14_.refs_0_), channel_id=1, source_target_pairs={{0,4},{4,0},{8,12},{12,8},{16,20},{20,16},{24,28},{28,24},{1,5},{5... | collective-permute-start | bytes 5111816 | tf_op jit(solution)/shard_map/ppermute | solution.py:268
  5.1 59.8 %collective-permute-start.5 = (bf16[6656,128]{1,0:T(8,128)(2,1)}, bf16[6656,128]{1,0:T(8,128)(2,1)}, u32[]{:S(2)}, u32[]{:S(2)}) collective-permute-start(bf16[6656,128]{1,0:T(8,128)(2,1)} %hidden.1.refs_6_.refs_14_.refs_0_), channel_id=1, source_target_pairs={{0,16},{4,20},{8,24},{12,28},{16,0},{20,4},{24,8},{28,12},{1,17},{... | collective-permute-start | bytes 5111816 | tf_op jit(solution)/shard_map/ppermute | solution.py:268
  6.6 58.3 %collective-permute-start.4 = (bf16[6656,128]{1,0:T(8,128)(2,1)}, bf16[6656,128]{1,0:T(8,128)(2,1)}, u32[]{:S(2)}, u32[]{:S(2)}) collective-permute-start(bf16[6656,128]{1,0:T(8,128)(2,1)} %hidden.1.refs_6_.refs_14_.refs_0_), channel_id=1, source_target_pairs={{0,8},{4,12},{8,0},{12,4},{16,24},{20,28},{24,16},{28,20},{1,9},{5... | collective-permute-start | bytes 5111816 | tf_op jit(solution)/shard_map/ppermute | solution.py:268
  8.1 27.2 %collective-permute-start = (bf16[256,2048]{1,0:T(8,128)(2,1)}, bf16[256,2048]{1,0:T(8,128)(2,1)}, u32[]{:S(2)}, u32[]{:S(2)}) collective-permute-start(bf16[256,2048]{1,0:T(8,128)(2,1)} %refs_5_.1), channel_id=1, source_target_pairs={{0,1},{1,2},{2,3},{4,5},{5,6},{6,7},{8,9},{9,10},{10,11},{12,13},{... | collective-permute-start | bytes 3145736 | tf_op jit(solution)/shard_map/ppermute | solution.py:281
  11.5 26.9 %collective-permute-start.1 = (bf16[256,2048]{1,0:T(8,128)(2,1)}, bf16[256,2048]{1,0:T(8,128)(2,1)}, u32[]{:S(2)}, u32[]{:S(2)}) collective-permute-start(bf16[256,2048]{1,0:T(8,128)(2,1)} %refs_5_.1), channel_id=1, source_target_pairs={{1,0},{2,1},{3,2},{5,4},{6,5},{7,6},{9,8},{10,9},{11,10},{13,12},{... | collective-permute-start | bytes 3145736 | tf_op jit(solution)/shard_map/ppermute | solution.py:282
  38.5 31.2 %collective-permute-start.2 = (bf16[256,2048]{1,0:T(8,128)(2,1)}, bf16[256,2048]{1,0:T(8,128)(2,1)}, u32[]{:S(2)}, u32[]{:S(2)}) collective-permute-start(bf16[256,2048]{1,0:T(8,128)(2,1)} %collective-permute-done.refs_6_), channel_id=1, source_target_pairs={{1,2},{2,3},{5,6},{6,7},{9,10},{10,11},{13,14},{14,15},{17,18},{18... | collective-permute-start | bytes 3145736 | tf_op jit(solution)/shard_map/ppermute | solution.py:281
  40.4 29.3 %collective-permute-start.3 = (bf16[256,2048]{1,0:T(8,128)(2,1)}, bf16[256,2048]{1,0:T(8,128)(2,1)}, u32[]{:S(2)}, u32[]{:S(2)}) collective-permute-start(bf16[256,2048]{1,0:T(8,128)(2,1)} %collective-permute-done.1.refs_5_), channel_id=1, source_target_pairs={{1,0},{2,1},{5,4},{6,5},{9,8},{10,9},{13,12},{14,13},{17,16},{18,1... | collective-permute-start | bytes 3145736 | tf_op jit(solution)/shard_map/ppermute | solution.py:282
  69.7 30.1 %collective-permute-start.9 = (bf16[13312,128]{1,0:T(8,128)(2,1)}, bf16[13312,128]{1,0:T(8,128)(2,1)}, u32[]{:S(2)}, u32[]{:S(2)}) collective-permute-start(bf16[13312,128]{1,0:T(8,128)(2,1)} %pad_maximum_fusion), channel_id=1, source_target_pairs={{0,4},{4,0},{8,12},{12,8},{16,20},{20,16},{24,28},{28,24},{1,5},{5... | collective-permute-start | bytes 10223624 | tf_op jit(solution)/shard_map/ppermute | solution.py:268
  69.8 29.0 %collective-permute-start.8 = (bf16[256,2048]{1,0:T(8,128)(2,1)}, bf16[256,2048]{1,0:T(8,128)(2,1)}, u32[]{:S(2)}, u32[]{:S(2)}) collective-permute-start(bf16[256,2048]{1,0:T(8,128)(2,1)} %collective-permute-done.3.refs_6_.refs_5_), channel_id=1, source_target_pairs={{1,0},{5,4},{9,8},{13,12},{17,16},{21,20},{25,24},{29,28}} | collective-permute-start | bytes 3145736 | tf_op jit(solution)/shard_map/ppermute | solution.py:282
  71.4 27.3 %collective-permute-start.7 = (bf16[256,2048]{1,0:T(8,128)(2,1)}, bf16[256,2048]{1,0:T(8,128)(2,1)}, u32[]{:S(2)}, u32[]{:S(2)}) collective-permute-start(bf16[256,2048]{1,0:T(8,128)(2,1)} %collective-permute-done.2.refs_7_), channel_id=1, source_target_pairs={{2,3},{6,7},{10,11},{14,15},{18,19},{22,23},{26,27},{30,31}} | collective-permute-start | bytes 3145736 | tf_op jit(solution)/shard_map/ppermute | solution.py:281
  77.9 21.5 %collective-permute-start.11 = (bf16[3328,128]{1,0:T(8,128)(2,1)}, bf16[3328,128]{1,0:T(8,128)(2,1)S(1)}, u32[]{:S(2)}, u32[]{:S(2)}) collective-permute-start(bf16[3328,128]{1,0:T(8,128)(2,1)} %slice.67), channel_id=1, source_target_pairs={{0,8},{4,12},{8,0},{12,4},{16,24},{20,28},{24,16},{28,20},{1,9},{5... | collective-permute-start | bytes 2555912 | tf_op jit(solution)/shard_map/ppermute | solution.py:268
  78.4 21.4 %collective-permute-start.10 = (bf16[3328,128]{1,0:T(8,128)(2,1)}, bf16[3328,128]{1,0:T(8,128)(2,1)}, u32[]{:S(2)}, u32[]{:S(2)}) collective-permute-start(bf16[3328,128]{1,0:T(8,128)(2,1)} %slice.66), channel_id=1, source_target_pairs={{0,16},{4,20},{8,24},{12,28},{16,0},{20,4},{24,8},{28,12},{1,17},{... | collective-permute-start | bytes 2555912 | tf_op jit(solution)/shard_map/ppermute | solution.py:268
  99.4 0.9 copy-start.3
  99.8 12.3 %collective-permute-start.12 = (bf16[3328,128]{1,0:T(8,128)(2,1)}, bf16[3328,128]{1,0:T(8,128)(2,1)}, u32[]{:S(2)}, u32[]{:S(2)}) collective-permute-start(bf16[3328,128]{1,0:T(8,128)(2,1)} %collective-permute-done.10.refs_20_.refs_6_), channel_id=1, source_target_pairs={{0,4},{4,0},{8,12},{12,8},{16,20},{20,16},{24,28},{28,24},{1,5},{5... | collective-permute-start | bytes 2555912 | tf_op jit(solution)/shard_map/ppermute | solution.py:268
  99.8 12.3 %collective-permute-start.13 = (bf16[3328,128]{1,0:T(8,128)(2,1)S(1)}, bf16[3328,128]{1,0:T(8,128)(2,1)}, u32[]{:S(2)}, u32[]{:S(2)}) collective-permute-start(bf16[3328,128]{1,0:T(8,128)(2,1)S(1)} %collective-permute-done.11.refs_21_.refs_7_.refs_6_), channel_id=1, source_target_pairs={{0,4},{4,0},{8,12},{12,8},{16,20},{20,16},{24,28},{28,24},{1,5},{5... | collective-permute-start | bytes 2555912 | tf_op jit(solution)/shard_map/ppermute | solution.py:268
  111.5 12.4 %collective-permute-start.17 = (bf16[4,1664,128]{2,1,0:T(8,128)(2,1)}, bf16[4,1664,128]{2,1,0:T(8,128)(2,1)}, u32[]{:S(2)}, u32[]{:S(2)}) collective-permute-start(bf16[4,1664,128]{2,1,0:T(8,128)(2,1)} %get-tuple-element.146), channel_id=1, source_target_pairs={{0,4},{4,0},{8,12},{12,8},{16,20},{20,16},{24,28},{28,24},{1,5},{5... | collective-permute-start | bytes 5111816 | tf_op jit(solution)/shard_map/ppermute | solution.py:268
  111.6 16.7 %collective-permute-start.16 = (bf16[4,1664,128]{2,1,0:T(8,128)(2,1)}, bf16[4,1664,128]{2,1,0:T(8,128)(2,1)}, u32[]{:S(2)}, u32[]{:S(2)}) collective-permute-start(bf16[4,1664,128]{2,1,0:T(8,128)(2,1)} %get-tuple-element.145), channel_id=1, source_target_pairs={{0,4},{4,0},{8,12},{12,8},{16,20},{20,16},{24,28},{28,24},{1,5},{5... | collective-permute-start | bytes 5111816 | tf_op jit(solution)/shard_map/ppermute | solution.py:268
  123.3 8.4 %collective-permute-start.15 = (bf16[4,1664,128]{2,1,0:T(8,128)(2,1)}, bf16[4,1664,128]{2,1,0:T(8,128)(2,1)S(1)}, u32[]{:S(2)}, u32[]{:S(2)}) collective-permute-start(bf16[4,1664,128]{2,1,0:T(8,128)(2,1)} %get-tuple-element.143), channel_id=1, source_target_pairs={{0,4},{4,0},{8,12},{12,8},{16,20},{20,16},{24,28},{28,24},{1,5},{5... | collective-permute-start | bytes 5111816 | tf_op jit(solution)/shard_map/ppermute | solution.py:268
  123.5 9.9 %collective-permute-start.14 = (bf16[4,1664,128]{2,1,0:T(8,128)(2,1)}, bf16[4,1664,128]{2,1,0:T(8,128)(2,1)S(1)}, u32[]{:S(2)}, u32[]{:S(2)}) collective-permute-start(bf16[4,1664,128]{2,1,0:T(8,128)(2,1)} %get-tuple-element.141), channel_id=1, source_target_pairs={{0,4},{4,0},{8,12},{12,8},{16,20},{20,16},{24,28},{28,24},{1,5},{5... | collective-permute-start | bytes 5111816 | tf_op jit(solution)/shard_map/ppermute | solution.py:268
  123.9 4.4 %copy-start = (f32[4,1664,128]{2,1,0:T(8,128)S(1)}, f32[4,1664,128]{2,1,0:T(8,128)}, u32[]{:S(2)}) copy-start(f32[4,1664,128]{2,1,0:T(8,128)} %get-tuple-element.159.refs_2_) | copy-start | bytes 10223620
  126.9 38.6 %collective-permute-start.21 = (bf16[2,1664,128]{2,1,0:T(8,128)(2,1)}, bf16[2,1664,128]{2,1,0:T(8,128)(2,1)}, u32[]{:S(2)}, u32[]{:S(2)}) collective-permute-start(bf16[2,1664,128]{2,1,0:T(8,128)(2,1)} %add_convert_fusion.3), channel_id=1, source_target_pairs={{0,8},{4,12},{8,0},{12,4},{16,24},{20,28},{24,16},{28,20},{1,9},{5... | collective-permute-start | bytes 2555912 | tf_op jit(solution)/shard_map/ppermute | solution.py:268
  128.3 3.4 %copy-start.1 = (f32[4,1664,128]{2,1,0:T(8,128)S(1)}, f32[4,1664,128]{2,1,0:T(8,128)}, u32[]{:S(2)}) copy-start(f32[4,1664,128]{2,1,0:T(8,128)} %get-tuple-element.162.refs_2_) | copy-start | bytes 10223620
  130.8 2.6 %copy-start.2 = (f32[4,1664,128]{2,1,0:T(8,128)S(1)}, f32[4,1664,128]{2,1,0:T(8,128)}, u32[]{:S(2)}) copy-start(f32[4,1664,128]{2,1,0:T(8,128)} %get-tuple-element.165.refs_2_) | copy-start | bytes 10223620
  130.8 37.8 %collective-permute-start.20 = (bf16[2,1664,128]{2,1,0:T(8,128)(2,1)}, bf16[2,1664,128]{2,1,0:T(8,128)(2,1)}, u32[]{:S(2)}, u32[]{:S(2)}) collective-permute-start(bf16[2,1664,128]{2,1,0:T(8,128)(2,1)} %add_convert_fusion.2), channel_id=1, source_target_pairs={{0,16},{4,20},{8,24},{12,28},{16,0},{20,4},{24,8},{28,12},{1,17},{... | collective-permute-start | bytes 2555912 | tf_op jit(solution)/shard_map/ppermute | solution.py:268
  131.7 1.6 copy-start.5
  132.8 39.5 %collective-permute-start.19 = (bf16[2,1664,128]{2,1,0:T(8,128)(2,1)}, bf16[2,1664,128]{2,1,0:T(8,128)(2,1)}, u32[]{:S(2)}, u32[]{:S(2)}) collective-permute-start(bf16[2,1664,128]{2,1,0:T(8,128)(2,1)} %add_convert_fusion.1), channel_id=1, source_target_pairs={{0,8},{4,12},{8,0},{12,4},{16,24},{20,28},{24,16},{28,20},{1,9},{5... | collective-permute-start | bytes 2555912 | tf_op jit(solution)/shard_map/ppermute | solution.py:268
  133.4 1.5 copy-start.4
  134.8 41.1 %collective-permute-start.18 = (bf16[2,1664,128]{2,1,0:T(8,128)(2,1)}, bf16[2,1664,128]{2,1,0:T(8,128)(2,1)S(1)}, u32[]{:S(2)}, u32[]{:S(2)}) collective-permute-start(bf16[2,1664,128]{2,1,0:T(8,128)(2,1)} %add_convert_fusion.refs_11_), channel_id=1, source_target_pairs={{0,16},{4,20},{8,24},{12,28},{16,0},{20,4},{24,8},{28,12},{1,17},{... | collective-permute-start | bytes 2555912 | tf_op jit(solution)/shard_map/ppermute | solution.py:268
  167.8 23.9 %collective-permute-start.25 = (bf16[1,1664,128]{2,1,0:T(8,128)(2,1)}, bf16[1,1664,128]{2,1,0:T(8,128)(2,1)}, u32[]{:S(2)}, u32[]{:S(2)}) collective-permute-start(bf16[1,1664,128]{2,1,0:T(8,128)(2,1)} %add_convert_fusion.7), channel_id=1, source_target_pairs={{0,16},{4,20},{8,24},{12,28},{16,0},{20,4},{24,8},{28,12},{1,17},{... | collective-permute-start | bytes 1277960 | tf_op jit(solution)/shard_map/ppermute | solution.py:268
  170.8 24.0 %collective-permute-start.24 = (bf16[1,1664,128]{2,1,0:T(8,128)(2,1)}, bf16[1,1664,128]{2,1,0:T(8,128)(2,1)}, u32[]{:S(2)}, u32[]{:S(2)}) collective-permute-start(bf16[1,1664,128]{2,1,0:T(8,128)(2,1)} %add_convert_fusion.6), channel_id=1, source_target_pairs={{0,8},{4,12},{8,0},{12,4},{16,24},{20,28},{24,16},{28,20},{1,9},{5... | collective-permute-start | bytes 1277960 | tf_op jit(solution)/shard_map/ppermute | solution.py:268
  174.7 23.4 %collective-permute-start.23 = (bf16[1,1664,128]{2,1,0:T(8,128)(2,1)}, bf16[1,1664,128]{2,1,0:T(8,128)(2,1)}, u32[]{:S(2)}, u32[]{:S(2)}) collective-permute-start(bf16[1,1664,128]{2,1,0:T(8,128)(2,1)} %add_convert_fusion.5), channel_id=1, source_target_pairs={{0,16},{4,20},{8,24},{12,28},{16,0},{20,4},{24,8},{28,12},{1,17},{... | collective-permute-start | bytes 1277960 | tf_op jit(solution)/shard_map/ppermute | solution.py:268
  175.9 15.8 %copy-start.6 = (bf16[2,1664,128]{2,1,0:T(8,128)(2,1)}, bf16[2,1664,128]{2,1,0:T(8,128)(2,1)S(1)}, u32[]{:S(2)}) copy-start(bf16[2,1664,128]{2,1,0:T(8,128)(2,1)S(1)} %collective-permute-done.18.refs_4_) | copy-start | bytes 2555908
  178.3 23.0 %collective-permute-start.22 = (bf16[1,1664,128]{2,1,0:T(8,128)(2,1)}, bf16[1,1664,128]{2,1,0:T(8,128)(2,1)}, u32[]{:S(2)}, u32[]{:S(2)}) collective-permute-start(bf16[1,1664,128]{2,1,0:T(8,128)(2,1)} %add_convert_fusion.4.refs_10_), channel_id=1, source_target_pairs={{0,8},{4,12},{8,0},{12,4},{16,24},{20,28},{24,16},{28,20},{1,9},{5... | collective-permute-start | bytes 1277960 | tf_op jit(solution)/shard_map/ppermute | solution.py:268

commit v9 on v8

--- a/solution.py
+++ b/solution.py
@@ -210,10 +210,10 @@
     tokens, depth = dy.shape
     middle = total // 2
     if start < middle < start + rows:
-        tall = divisor(math.gcd(rows, middle - start), 416, 16)
+        tall = divisor(math.gcd(rows, middle - start), 832, 16)
         switch = (middle - start) // tall
     else:
-        tall = divisor(rows, 416, 16)
+        tall = divisor(rows, 832, 16)
         switch = 0
         pieces = [p if len(p) == 1 else [p[start >= middle]] for p in pieces]
 

time: 206 us -> 205 us (level)
  no operation moved by 1% of the time
where the time goes in v9:
time: 205 us; the launch traced here: 204 us
  Pallas kernels  137 us (67%)
  starting transfers between devices  31.6 us (15%)
  other arithmetic  22 us (11%)
  local copies, waits for them, and re-layouts  7.05 us (3%)
  waiting for transfers between devices  5.77 us (3%)
    pallas_call x12, Pallas kernels, run(): pl.pallas_call(body, grid_spec=pltpu.PrefetchScalarGridSpec(num_scalar_pr...  137 us
    convert_element_type x8, other arithmetic, step(): send = sum((t[rows:2 * rows].astype(F32) for t in sums[n])).astype(BF16)  17.1 us
    ppermute x20, starting transfers between devices, swap(): return jax.tree.map(lambda x: lax.ppermute(x, 'row', pairs), x)  14 us
    ppermute x3, starting transfers between devices, forward(): lax.ppermute(down[-1], 'col', [(i, i - 1) for i in range(1, col_count - s...  9.89 us
    ppermute x3, starting transfers between devices, forward(): lax.ppermute(up[-1], 'col', [(i, i + 1) for i in range(s - 1, col_count -...  7.64 us
    concatenate x1, other arithmetic, program(): both = [jnp.concatenate(held[a] + held[b])]  4.87 us
    slice x2, local copies, waits for them, and re-layouts, program(): held[a | b] = [swap(held[a][0][:half], b), swap(held[b][0][half:], a)]  4.22 us
  transfers between devices with their start and end apart: 26, of which 4 were waited for; matrix products, arithmetic and copies ran while one was open for 14% of the time, Pallas kernels for 63%

profile of v9, /device:TPU:16, one launch (start us, length us, event | category | flops | bytes accessed | tf_op | source)
XLA Modules:
  0.0 204.0 jit_solution(15141823715770120157)
XLA Ops:
  0.6 4.4 %hidden.1.refs_6_.refs_14_.refs_0_ = bf16[6656,128]{1,0:T(8,128)(2,1)} custom-call(bf16[128,6656]{1,0:T(8,128)(2,1)} %refs_0_.9, bf16[128,6656]{1,0:T(8,128)(2,1)} %refs_1_.19), custom_call_target="tpu_custom_call" | custom-call | bytes 3407872 | tf_op jit(solution)/shard_map/hidden/pallas_call | solution.py:41
  5.1 1.5 collective-permute-start.5
  6.6 1.5 collective-permute-start.4
  8.1 3.5 %collective-permute-start = (bf16[256,2048]{1,0:T(8,128)(2,1)}, bf16[256,2048]{1,0:T(8,128)(2,1)}, u32[]{:S(2)}, u32[]{:S(2)}) collective-permute-start(bf16[256,2048]{1,0:T(8,128)(2,1)} %refs_5_.1), channel_id=1, source_target_pairs={{0,1},{1,2},{2,3},{4,5},{5,6},{6,7},{8,9},{9,10},{10,11},{12,13},{... | collective-permute-start | bytes 3145736 | tf_op jit(solution)/shard_map/ppermute | solution.py:281
  11.5 2.4 %collective-permute-start.1 = (bf16[256,2048]{1,0:T(8,128)(2,1)}, bf16[256,2048]{1,0:T(8,128)(2,1)}, u32[]{:S(2)}, u32[]{:S(2)}) collective-permute-start(bf16[256,2048]{1,0:T(8,128)(2,1)} %refs_5_.1), channel_id=1, source_target_pairs={{1,0},{2,1},{3,2},{5,4},{6,5},{7,6},{9,8},{10,9},{11,10},{13,12},{... | collective-permute-start | bytes 3145736 | tf_op jit(solution)/shard_map/ppermute | solution.py:282
  14.0 0.7 stack.91.refs_0_
  14.7 0.6 stack.86.refs_0_
  15.3 18.5 %hidden_grad_terms.5 = (f32[4,1664,128]{2,1,0:T(8,128)}, bf16[4,1664,128]{2,1,0:T(8,128)(2,1)}, f32[4,1664,128]{2,1,0:T(8,128)}, bf16[4,1664,128]{2,1,0:T(8,128)...) custom-call(s32[6]{0:T(128)} %stack.86.refs_0_, ...), custom_call_target="tpu_custom_call" | custom-call | flops 6979321856 | bytes 110100480 | tf_op jit(solution)/shard_map/hidden_grad_terms/pallas_call | solution.py:41
  33.8 1.5 collective-permute-done.refs_6_
  35.3 3.2 %collective-permute-done.1.refs_5_ = bf16[256,2048]{1,0:T(8,128)(2,1)} collective-permute-done((bf16[256,2048]{1,0:T(8,128)(2,1)}, bf16[256,2048]{1,0:T(8,128)(2,1)}, u32[]{:S(2)}, u32[]{:S(2)}) %collective-permute-start.1) | collective-permute-done | bytes 1048608 | tf_op jit(solution)/shard_map/ppermute | solution.py:282
  38.5 1.9 collective-permute-start.2
  40.4 5.9 %collective-permute-start.3 = (bf16[256,2048]{1,0:T(8,128)(2,1)}, bf16[256,2048]{1,0:T(8,128)(2,1)}, u32[]{:S(2)}, u32[]{:S(2)}) collective-permute-start(bf16[256,2048]{1,0:T(8,128)(2,1)} %collective-permute-done.1.refs_5_), channel_id=1, source_target_pairs={{1,0},{2,1},{5,4},{6,5},{9,8},{10,9},{13,12},{14,13},{17,16},{18,1... | collective-permute-start | bytes 3145736 | tf_op jit(solution)/shard_map/ppermute | solution.py:282
  46.3 18.5 %hidden_grad_terms.6 = (f32[4,1664,128]{2,1,0:T(8,128)}, bf16[4,1664,128]{2,1,0:T(8,128)(2,1)}, f32[4,1664,128]{2,1,0:T(8,128)}, bf16[4,1664,128]{2,1,0:T(8,128)...) custom-call(s32[6]{0:T(128)} %stack.91.refs_0_, ...), custom_call_target="tpu_custom_call", output_to_operand_aliasing={{0}: (7, {}), {1}: (8, {}), {2}: (9, {}), {3}: (10, {}), {4... | custom-call | flops 6979321856 | bytes 111149056 | tf_op jit(solution)/shard_map/hidden_grad_terms/pallas_call | solution.py:41
  64.8 4.9 %pad_maximum_fusion = bf16[13312,128]{1,0:T(8,128)(2,1)} fusion(bf16[6656,128]{1,0:T(8,128)(2,1)} %collective-permute-done.5.refs_18_.refs_4_, bf16[6656,128]{1,0:T(8,128)(2,1)} %collective-permute-done.4.refs_16_.refs_2_), kind=kLoop, calls=%fused_computation | loop fusion | flops 6815744 | bytes 6815744 | tf_op jit(solution)/shard_map/concatenate | solution.py:335
  69.8 1.6 collective-permute-start.8
  71.4 2.3 %collective-permute-start.7 = (bf16[256,2048]{1,0:T(8,128)(2,1)}, bf16[256,2048]{1,0:T(8,128)(2,1)}, u32[]{:S(2)}, u32[]{:S(2)}) collective-permute-start(bf16[256,2048]{1,0:T(8,128)(2,1)} %collective-permute-done.2.refs_7_), channel_id=1, source_target_pairs={{2,3},{6,7},{10,11},{14,15},{18,19},{22,23},{26,27},{30,31}} | collective-permute-start | bytes 3145736 | tf_op jit(solution)/shard_map/ppermute | solution.py:281
  73.7 2.1 %slice.66 = bf16[3328,128]{1,0:T(8,128)(2,1)} slice(bf16[6656,128]{1,0:T(8,128)(2,1)} %collective-permute-done.4.refs_16_.refs_2_), slice={[0:3328], [0:128]} | slice | bytes 1703936 | tf_op jit(solution)/shard_map/slice | solution.py:344
  75.8 2.1 %slice.67 = bf16[3328,128]{1,0:T(8,128)(2,1)} slice(bf16[6656,128]{1,0:T(8,128)(2,1)} %collective-permute-done.5.refs_18_.refs_4_), slice={[3328:6656], [0:128]} | slice | bytes 1703936 | tf_op jit(solution)/shard_map/slice | solution.py:344
  77.9 0.5 collective-permute-start.11
  78.4 0.5 collective-permute-start.10
  79.0 0.6 stack.82.refs_0_
  79.6 0.7 stack.96.refs_0_
  80.3 18.5 %hidden_grad_terms.7 = (f32[4,1664,128]{2,1,0:T(8,128)}, bf16[4,1664,128]{2,1,0:T(8,128)(2,1)}, f32[4,1664,128]{2,1,0:T(8,128)}, bf16[4,1664,128]{2,1,0:T(8,128)...) custom-call(s32[6]{0:T(128)} %stack.96.refs_0_, ...), custom_call_target="tpu_custom_call", output_to_operand_aliasing={{0}: (8, {}), {1}: (9, {}), {2}: (10, {}), {3}: (11, {}), {... | custom-call | flops 6979321856 | bytes 112197632 | tf_op jit(solution)/shard_map/hidden_grad_terms/pallas_call | solution.py:41
  98.8 0.7 collective-permute-done.11.refs_21_.refs_7_.refs_6_
  100.4 11.2 %hidden_grad_terms.8 = (f32[4,1664,128]{2,1,0:T(8,128)}, bf16[4,1664,128]{2,1,0:T(8,128)(2,1)}, f32[4,1664,128]{2,1,0:T(8,128)}, bf16[4,1664,128]{2,1,0:T(8,128)(2,1)}, bf16[1024,2048]{1,0:T(8,128)(2,1)}) custom-call(s32[6]{0:T(128)} %stack.82.refs_0_, ...), custom_call_target="tpu_custom_call", output_to_operand_aliasing={{0}: (9, {}), {1}: (10, {}), {2}: (11, {}), {3}: (12, {}), ... | custom-call | flops 3489660928 | bytes 113246208 | tf_op jit(solution)/shard_map/hidden_grad_terms/pallas_call | solution.py:41
  112.1 11.2 %hidden_grad_terms.9 = (f32[4,1664,128]{2,1,0:T(8,128)}, bf16[4,1664,128]{2,1,0:T(8,128)(2,1)}, f32[4,1664,128]{2,1,0:T(8,128)}, bf16[4,1664,128]{2,1,0:T(8,128)(2,1)}) custom-call(s32[6]{0:T(128)} %stack.82.refs_0_, bf16[6656,2048]{1,0:T(8,128)(2,1)} %refs_4_.9, ...), custom_call_target="tpu_custom_call", output_to_operand_aliasing={{0}: (9, {}), {1}: (10, {}), {2}: (11, {}), {3}: (12, {})} | custom-call | flops 3489660928 | bytes 113246208 | tf_op jit(solution)/shard_map/hidden_grad_terms/pallas_call | solution.py:41
  123.9 2.9 %add_convert_fusion.3 = bf16[2,1664,128]{2,1,0:T(8,128)(2,1)} fusion(f32[4,1664,128]{2,1,0:T(8,128)} %get-tuple-element.156.refs_13_.refs_2_, bf16[4,1664,128]{2,1,0:T(8,128)(2,1)} %collective-permute-done.17.refs_3_), kind=kLoop, calls=%fused_computation.4 | loop fusion | flops 1277952 | bytes 3407872 | tf_op jit(solution)/shard_map/convert_element_type | solution.py:378
  126.9 1.4 collective-permute-start.21
  128.3 2.5 %add_convert_fusion.2 = bf16[2,1664,128]{2,1,0:T(8,128)(2,1)} fusion(f32[4,1664,128]{2,1,0:T(8,128)S(1)} %copy-done, bf16[4,1664,128]{2,1,0:T(8,128)(2,1)} %collective-permute-done.16.refs_3_), kind=kLoop, calls=%fused_computation.3 | loop fusion | flops 1277952 | bytes 3407872 | tf_op jit(solution)/shard_map/convert_element_type | solution.py:378
  130.8 0.9 collective-permute-start.20
  131.7 1.1 add_convert_fusion.1
  132.8 0.6 collective-permute-start.19
  133.4 1.2 add_convert_fusion.refs_11_
  134.8 1.3 collective-permute-start.18
  136.1 28.5 %weight_grad.2.refs_9_ = bf16[6656,2048]{1,0:T(8,128)(2,1)} custom-call(bf16[6656,128]{1,0:T(8,128)(2,1)} %hidden.1.refs_6_.refs_14_.refs_0_, bf16[6656,128]{1,0:T(8,128)(2,1)} %collective-permute-done.6.refs_16_.refs_15_.refs_1_, bf16[6656,128]{1,0:T(8,128)(2,1)} %collective-permute-done.4.refs_16_.refs_2_, ...), custom_call_target="tpu_custom_call" | custom-call | flops 20937965568 | bytes 21233664 | tf_op jit(solution)/shard_map/weight_grad/pallas_call | solution.py:41
  164.6 2.3 %add_convert_fusion.7 = bf16[1,1664,128]{2,1,0:T(8,128)(2,1)} fusion(f32[4,1664,128]{2,1,0:T(8,128)} %get-tuple-element.156.refs_13_.refs_2_, bf16[2,1664,128]{2,1,0:T(8,128)(2,1)} %collective-permute-done.21.refs_4_, bf16[4,1664,128]{2,1,0:T(8,128)(2,1)} %collective-permute-done.17.refs_3_), kind=kLoop, calls=%fused_computation.8 | loop fusion | flops 1064960 | bytes 2129920 | tf_op jit(solution)/shard_map/convert_element_type | solution.py:378
  166.9 0.8 collective-permute-start.25
  167.7 2.3 %add_convert_fusion.6 = bf16[1,1664,128]{2,1,0:T(8,128)(2,1)} fusion(f32[4,1664,128]{2,1,0:T(8,128)} %get-tuple-element.159.refs_2_, bf16[2,1664,128]{2,1,0:T(8,128)(2,1)} %collective-permute-done.20.refs_4_, bf16[4,1664,128]{2,1,0:T(8,128)(2,1)} %collective-permute-done.16.refs_3_), kind=kLoop, calls=%fused_computation.7 | loop fusion | flops 1064960 | bytes 2129920 | tf_op jit(solution)/shard_map/convert_element_type | solution.py:378
  170.0 1.5 collective-permute-start.24
  171.4 2.3 %add_convert_fusion.5 = bf16[1,1664,128]{2,1,0:T(8,128)(2,1)} fusion(f32[4,1664,128]{2,1,0:T(8,128)} %get-tuple-element.162.refs_2_, bf16[2,1664,128]{2,1,0:T(8,128)(2,1)} %collective-permute-done.19.refs_4_, bf16[4,1664,128]{2,1,0:T(8,128)(2,1)} %copy-done.5), kind=kLoop, calls=%fused_computation.6 | loop fusion | flops 1064960 | bytes 2129920 | tf_op jit(solution)/shard_map/convert_element_type | solution.py:378
  173.8 1.2 collective-permute-start.23
  175.0 2.5 %add_convert_fusion.4.refs_10_ = bf16[1,1664,128]{2,1,0:T(8,128)(2,1)} fusion(f32[4,1664,128]{2,1,0:T(8,128)} %get-tuple-element.165.refs_2_, bf16[2,1664,128]{2,1,0:T(8,128)(2,1)S(1)} %collective-permute-done.18.refs_4_, bf16[4,1664,128]{2,1,0:T(8,128)(2,1)} %copy-done.4), kind=kLoop, calls=%fused_computation.5 | loop fusion | flops 1064960 | bytes 2129920 | tf_op jit(solution)/shard_map/convert_element_type | solution.py:378
  177.5 0.6 collective-permute-start.22
  178.0 13.1 %weight_grad.3.refs_6_ = bf16[6656,2048]{1,0:T(8,128)(2,1)} custom-call(bf16[6656,128]{1,0:T(8,128)(2,1)} %hidden.1.refs_6_.refs_14_.refs_0_, bf16[6656,128]{1,0:T(8,128)(2,1)} %collective-permute-done.6.refs_16_.refs_15_.refs_1_, bf16[6656,128]{1,0:T(8,128)(2,1)} %collective-permute-done.4.refs_16_.refs_2_, ...), custom_call_target="tpu_custom_call", output_to_operand_aliasing={{}: (9, {})} | custom-call | flops 6979321856 | bytes 19529728 | tf_op jit(solution)/shard_map/weight_grad/pallas_call | solution.py:41
  191.1 3.2 %finish.4 = (bf16[128,6656]{1,0:T(8,128)(2,1)}, bf16[128,6656]{1,0:T(8,128)(2,1)}) custom-call(bf16[128,6656]{1,0:T(8,128)(2,1)} %refs_0_.9, bf16[128,6656]{1,0:T(8,128)(2,1)} %refs_1_.19, f32[4,1664,128]{2,1,0:T(8,128)} %get-tuple-element.156.refs_13_.refs_2_, bf16[4,1664,128]{2,1,0:T(8,128)(2,1)} %collective-permute-done.17.refs_3_, ...), custom_call_target="tpu_custom_call" | custom-call | bytes 9797632 | tf_op jit(solution)/shard_map/finish/pallas_call | solution.py:41
  194.3 3.2 %finish.5 = (bf16[128,6656]{1,0:T(8,128)(2,1)}, bf16[128,6656]{1,0:T(8,128)(2,1)}) custom-call(bf16[128,6656]{1,0:T(8,128)(2,1)} %refs_0_.9, bf16[128,6656]{1,0:T(8,128)(2,1)} %refs_1_.19, f32[4,1664,128]{2,1,0:T(8,128)} %get-tuple-element.159.refs_2_, ...), custom_call_target="tpu_custom_call", output_to_operand_aliasing={{0}: (6, {}), {1}: (7, {})} | custom-call | bytes 9797632 | tf_op jit(solution)/shard_map/finish/pallas_call | solution.py:41
  197.6 3.2 %finish.6 = (bf16[128,6656]{1,0:T(8,128)(2,1)}, bf16[128,6656]{1,0:T(8,128)(2,1)}) custom-call(bf16[128,6656]{1,0:T(8,128)(2,1)} %refs_0_.9, bf16[128,6656]{1,0:T(8,128)(2,1)} %refs_1_.19, f32[4,1664,128]{2,1,0:T(8,128)} %get-tuple-element.162.refs_2_, bf16[4,1664,128]{2,1,0:T(8,128)(2,1)} %copy-done.5, ...), custom_call_target="tpu_custom_call", output_to_operand_aliasing={{0}: (6, {}), {1}: (7, {})} | custom-call | bytes 9797632 | tf_op jit(solution)/shard_map/finish/pallas_call | solution.py:41
  200.8 3.2 %finish.7 = (bf16[128,6656]{1,0:T(8,128)(2,1)}, bf16[128,6656]{1,0:T(8,128)(2,1)}) custom-call(bf16[128,6656]{1,0:T(8,128)(2,1)} %refs_0_.9, bf16[128,6656]{1,0:T(8,128)(2,1)} %refs_1_.19, f32[4,1664,128]{2,1,0:T(8,128)} %get-tuple-element.165.refs_2_, bf16[4,1664,128]{2,1,0:T(8,128)(2,1)} %copy-done.4, ...), custom_call_target="tpu_custom_call", output_to_operand_aliasing={{0}: (6, {}), {1}: (7, {})} | custom-call | bytes 9797632 | tf_op jit(solution)/shard_map/finish/pallas_call | solution.py:41
  (45 shorter events, 2.4 us)
Async XLA Ops:
  5.0 41.3 %collective-permute-start.6 = (bf16[6656,128]{1,0:T(8,128)(2,1)}, bf16[6656,128]{1,0:T(8,128)(2,1)}, u32[]{:S(2)}, u32[]{:S(2)}) collective-permute-start(bf16[6656,128]{1,0:T(8,128)(2,1)} %hidden.1.refs_6_.refs_14_.refs_0_), channel_id=1, source_target_pairs={{0,4},{4,0},{8,12},{12,8},{16,20},{20,16},{24,28},{28,24},{1,5},{5... | collective-permute-start | bytes 5111816 | tf_op jit(solution)/shard_map/ppermute | solution.py:268
  5.1 59.8 %collective-permute-start.5 = (bf16[6656,128]{1,0:T(8,128)(2,1)}, bf16[6656,128]{1,0:T(8,128)(2,1)}, u32[]{:S(2)}, u32[]{:S(2)}) collective-permute-start(bf16[6656,128]{1,0:T(8,128)(2,1)} %hidden.1.refs_6_.refs_14_.refs_0_), channel_id=1, source_target_pairs={{0,16},{4,20},{8,24},{12,28},{16,0},{20,4},{24,8},{28,12},{1,17},{... | collective-permute-start | bytes 5111816 | tf_op jit(solution)/shard_map/ppermute | solution.py:268
  6.6 58.3 %collective-permute-start.4 = (bf16[6656,128]{1,0:T(8,128)(2,1)}, bf16[6656,128]{1,0:T(8,128)(2,1)}, u32[]{:S(2)}, u32[]{:S(2)}) collective-permute-start(bf16[6656,128]{1,0:T(8,128)(2,1)} %hidden.1.refs_6_.refs_14_.refs_0_), channel_id=1, source_target_pairs={{0,8},{4,12},{8,0},{12,4},{16,24},{20,28},{24,16},{28,20},{1,9},{5... | collective-permute-start | bytes 5111816 | tf_op jit(solution)/shard_map/ppermute | solution.py:268
  8.1 27.2 %collective-permute-start = (bf16[256,2048]{1,0:T(8,128)(2,1)}, bf16[256,2048]{1,0:T(8,128)(2,1)}, u32[]{:S(2)}, u32[]{:S(2)}) collective-permute-start(bf16[256,2048]{1,0:T(8,128)(2,1)} %refs_5_.1), channel_id=1, source_target_pairs={{0,1},{1,2},{2,3},{4,5},{5,6},{6,7},{8,9},{9,10},{10,11},{12,13},{... | collective-permute-start | bytes 3145736 | tf_op jit(solution)/shard_map/ppermute | solution.py:281
  11.5 26.9 %collective-permute-start.1 = (bf16[256,2048]{1,0:T(8,128)(2,1)}, bf16[256,2048]{1,0:T(8,128)(2,1)}, u32[]{:S(2)}, u32[]{:S(2)}) collective-permute-start(bf16[256,2048]{1,0:T(8,128)(2,1)} %refs_5_.1), channel_id=1, source_target_pairs={{1,0},{2,1},{3,2},{5,4},{6,5},{7,6},{9,8},{10,9},{11,10},{13,12},{... | collective-permute-start | bytes 3145736 | tf_op jit(solution)/shard_map/ppermute | solution.py:282
  38.5 31.2 %collective-permute-start.2 = (bf16[256,2048]{1,0:T(8,128)(2,1)}, bf16[256,2048]{1,0:T(8,128)(2,1)}, u32[]{:S(2)}, u32[]{:S(2)}) collective-permute-start(bf16[256,2048]{1,0:T(8,128)(2,1)} %collective-permute-done.refs_6_), channel_id=1, source_target_pairs={{1,2},{2,3},{5,6},{6,7},{9,10},{10,11},{13,14},{14,15},{17,18},{18... | collective-permute-start | bytes 3145736 | tf_op jit(solution)/shard_map/ppermute | solution.py:281
  40.4 29.3 %collective-permute-start.3 = (bf16[256,2048]{1,0:T(8,128)(2,1)}, bf16[256,2048]{1,0:T(8,128)(2,1)}, u32[]{:S(2)}, u32[]{:S(2)}) collective-permute-start(bf16[256,2048]{1,0:T(8,128)(2,1)} %collective-permute-done.1.refs_5_), channel_id=1, source_target_pairs={{1,0},{2,1},{5,4},{6,5},{9,8},{10,9},{13,12},{14,13},{17,16},{18,1... | collective-permute-start | bytes 3145736 | tf_op jit(solution)/shard_map/ppermute | solution.py:282
  69.7 30.1 %collective-permute-start.9 = (bf16[13312,128]{1,0:T(8,128)(2,1)}, bf16[13312,128]{1,0:T(8,128)(2,1)}, u32[]{:S(2)}, u32[]{:S(2)}) collective-permute-start(bf16[13312,128]{1,0:T(8,128)(2,1)} %pad_maximum_fusion), channel_id=1, source_target_pairs={{0,4},{4,0},{8,12},{12,8},{16,20},{20,16},{24,28},{28,24},{1,5},{5... | collective-permute-start | bytes 10223624 | tf_op jit(solution)/shard_map/ppermute | solution.py:268
  69.8 29.0 %collective-permute-start.8 = (bf16[256,2048]{1,0:T(8,128)(2,1)}, bf16[256,2048]{1,0:T(8,128)(2,1)}, u32[]{:S(2)}, u32[]{:S(2)}) collective-permute-start(bf16[256,2048]{1,0:T(8,128)(2,1)} %collective-permute-done.3.refs_6_.refs_5_), channel_id=1, source_target_pairs={{1,0},{5,4},{9,8},{13,12},{17,16},{21,20},{25,24},{29,28}} | collective-permute-start | bytes 3145736 | tf_op jit(solution)/shard_map/ppermute | solution.py:282
  71.4 27.3 %collective-permute-start.7 = (bf16[256,2048]{1,0:T(8,128)(2,1)}, bf16[256,2048]{1,0:T(8,128)(2,1)}, u32[]{:S(2)}, u32[]{:S(2)}) collective-permute-start(bf16[256,2048]{1,0:T(8,128)(2,1)} %collective-permute-done.2.refs_7_), channel_id=1, source_target_pairs={{2,3},{6,7},{10,11},{14,15},{18,19},{22,23},{26,27},{30,31}} | collective-permute-start | bytes 3145736 | tf_op jit(solution)/shard_map/ppermute | solution.py:281
  77.9 21.5 %collective-permute-start.11 = (bf16[3328,128]{1,0:T(8,128)(2,1)}, bf16[3328,128]{1,0:T(8,128)(2,1)S(1)}, u32[]{:S(2)}, u32[]{:S(2)}) collective-permute-start(bf16[3328,128]{1,0:T(8,128)(2,1)} %slice.67), channel_id=1, source_target_pairs={{0,8},{4,12},{8,0},{12,4},{16,24},{20,28},{24,16},{28,20},{1,9},{5... | collective-permute-start | bytes 2555912 | tf_op jit(solution)/shard_map/ppermute | solution.py:268
  78.4 21.4 %collective-permute-start.10 = (bf16[3328,128]{1,0:T(8,128)(2,1)}, bf16[3328,128]{1,0:T(8,128)(2,1)}, u32[]{:S(2)}, u32[]{:S(2)}) collective-permute-start(bf16[3328,128]{1,0:T(8,128)(2,1)} %slice.66), channel_id=1, source_target_pairs={{0,16},{4,20},{8,24},{12,28},{16,0},{20,4},{24,8},{28,12},{1,17},{... | collective-permute-start | bytes 2555912 | tf_op jit(solution)/shard_map/ppermute | solution.py:268
  99.4 0.9 copy-start.3
  99.8 12.3 %collective-permute-start.12 = (bf16[3328,128]{1,0:T(8,128)(2,1)}, bf16[3328,128]{1,0:T(8,128)(2,1)}, u32[]{:S(2)}, u32[]{:S(2)}) collective-permute-start(bf16[3328,128]{1,0:T(8,128)(2,1)} %collective-permute-done.10.refs_20_.refs_6_), channel_id=1, source_target_pairs={{0,4},{4,0},{8,12},{12,8},{16,20},{20,16},{24,28},{28,24},{1,5},{5... | collective-permute-start | bytes 2555912 | tf_op jit(solution)/shard_map/ppermute | solution.py:268
  99.8 12.3 %collective-permute-start.13 = (bf16[3328,128]{1,0:T(8,128)(2,1)S(1)}, bf16[3328,128]{1,0:T(8,128)(2,1)}, u32[]{:S(2)}, u32[]{:S(2)}) collective-permute-start(bf16[3328,128]{1,0:T(8,128)(2,1)S(1)} %collective-permute-done.11.refs_21_.refs_7_.refs_6_), channel_id=1, source_target_pairs={{0,4},{4,0},{8,12},{12,8},{16,20},{20,16},{24,28},{28,24},{1,5},{5... | collective-permute-start | bytes 2555912 | tf_op jit(solution)/shard_map/ppermute | solution.py:268
  111.5 12.4 %collective-permute-start.17 = (bf16[4,1664,128]{2,1,0:T(8,128)(2,1)}, bf16[4,1664,128]{2,1,0:T(8,128)(2,1)}, u32[]{:S(2)}, u32[]{:S(2)}) collective-permute-start(bf16[4,1664,128]{2,1,0:T(8,128)(2,1)} %get-tuple-element.146), channel_id=1, source_target_pairs={{0,4},{4,0},{8,12},{12,8},{16,20},{20,16},{24,28},{28,24},{1,5},{5... | collective-permute-start | bytes 5111816 | tf_op jit(solution)/shard_map/ppermute | solution.py:268
  111.6 16.7 %collective-permute-start.16 = (bf16[4,1664,128]{2,1,0:T(8,128)(2,1)}, bf16[4,1664,128]{2,1,0:T(8,128)(2,1)}, u32[]{:S(2)}, u32[]{:S(2)}) collective-permute-start(bf16[4,1664,128]{2,1,0:T(8,128)(2,1)} %get-tuple-element.145), channel_id=1, source_target_pairs={{0,4},{4,0},{8,12},{12,8},{16,20},{20,16},{24,28},{28,24},{1,5},{5... | collective-permute-start | bytes 5111816 | tf_op jit(solution)/shard_map/ppermute | solution.py:268
  123.3 8.4 %collective-permute-start.15 = (bf16[4,1664,128]{2,1,0:T(8,128)(2,1)}, bf16[4,1664,128]{2,1,0:T(8,128)(2,1)S(1)}, u32[]{:S(2)}, u32[]{:S(2)}) collective-permute-start(bf16[4,1664,128]{2,1,0:T(8,128)(2,1)} %get-tuple-element.143), channel_id=1, source_target_pairs={{0,4},{4,0},{8,12},{12,8},{16,20},{20,16},{24,28},{28,24},{1,5},{5... | collective-permute-start | bytes 5111816 | tf_op jit(solution)/shard_map/ppermute | solution.py:268
  123.5 9.9 %collective-permute-start.14 = (bf16[4,1664,128]{2,1,0:T(8,128)(2,1)}, bf16[4,1664,128]{2,1,0:T(8,128)(2,1)S(1)}, u32[]{:S(2)}, u32[]{:S(2)}) collective-permute-start(bf16[4,1664,128]{2,1,0:T(8,128)(2,1)} %get-tuple-element.141), channel_id=1, source_target_pairs={{0,4},{4,0},{8,12},{12,8},{16,20},{20,16},{24,28},{28,24},{1,5},{5... | collective-permute-start | bytes 5111816 | tf_op jit(solution)/shard_map/ppermute | solution.py:268
  123.9 4.4 %copy-start = (f32[4,1664,128]{2,1,0:T(8,128)S(1)}, f32[4,1664,128]{2,1,0:T(8,128)}, u32[]{:S(2)}) copy-start(f32[4,1664,128]{2,1,0:T(8,128)} %get-tuple-element.159.refs_2_) | copy-start | bytes 10223620
  126.9 37.7 %collective-permute-start.21 = (bf16[2,1664,128]{2,1,0:T(8,128)(2,1)}, bf16[2,1664,128]{2,1,0:T(8,128)(2,1)}, u32[]{:S(2)}, u32[]{:S(2)}) collective-permute-start(bf16[2,1664,128]{2,1,0:T(8,128)(2,1)} %add_convert_fusion.3), channel_id=1, source_target_pairs={{0,8},{4,12},{8,0},{12,4},{16,24},{20,28},{24,16},{28,20},{1,9},{5... | collective-permute-start | bytes 2555912 | tf_op jit(solution)/shard_map/ppermute | solution.py:268
  128.3 3.4 %copy-start.1 = (f32[4,1664,128]{2,1,0:T(8,128)S(1)}, f32[4,1664,128]{2,1,0:T(8,128)}, u32[]{:S(2)}) copy-start(f32[4,1664,128]{2,1,0:T(8,128)} %get-tuple-element.162.refs_2_) | copy-start | bytes 10223620
  130.8 2.6 %copy-start.2 = (f32[4,1664,128]{2,1,0:T(8,128)S(1)}, f32[4,1664,128]{2,1,0:T(8,128)}, u32[]{:S(2)}) copy-start(f32[4,1664,128]{2,1,0:T(8,128)} %get-tuple-element.165.refs_2_) | copy-start | bytes 10223620
  130.8 36.9 %collective-permute-start.20 = (bf16[2,1664,128]{2,1,0:T(8,128)(2,1)}, bf16[2,1664,128]{2,1,0:T(8,128)(2,1)}, u32[]{:S(2)}, u32[]{:S(2)}) collective-permute-start(bf16[2,1664,128]{2,1,0:T(8,128)(2,1)} %add_convert_fusion.2), channel_id=1, source_target_pairs={{0,16},{4,20},{8,24},{12,28},{16,0},{20,4},{24,8},{28,12},{1,17},{... | collective-permute-start | bytes 2555912 | tf_op jit(solution)/shard_map/ppermute | solution.py:268
  131.7 1.6 copy-start.5
  132.8 38.6 %collective-permute-start.19 = (bf16[2,1664,128]{2,1,0:T(8,128)(2,1)}, bf16[2,1664,128]{2,1,0:T(8,128)(2,1)}, u32[]{:S(2)}, u32[]{:S(2)}) collective-permute-start(bf16[2,1664,128]{2,1,0:T(8,128)(2,1)} %add_convert_fusion.1), channel_id=1, source_target_pairs={{0,8},{4,12},{8,0},{12,4},{16,24},{20,28},{24,16},{28,20},{1,9},{5... | collective-permute-start | bytes 2555912 | tf_op jit(solution)/shard_map/ppermute | solution.py:268
  133.4 1.5 copy-start.4
  134.8 40.2 %collective-permute-start.18 = (bf16[2,1664,128]{2,1,0:T(8,128)(2,1)}, bf16[2,1664,128]{2,1,0:T(8,128)(2,1)S(1)}, u32[]{:S(2)}, u32[]{:S(2)}) collective-permute-start(bf16[2,1664,128]{2,1,0:T(8,128)(2,1)} %add_convert_fusion.refs_11_), channel_id=1, source_target_pairs={{0,16},{4,20},{8,24},{12,28},{16,0},{20,4},{24,8},{28,12},{1,17},{... | collective-permute-start | bytes 2555912 | tf_op jit(solution)/shard_map/ppermute | solution.py:268
  166.9 24.2 %collective-permute-start.25 = (bf16[1,1664,128]{2,1,0:T(8,128)(2,1)}, bf16[1,1664,128]{2,1,0:T(8,128)(2,1)}, u32[]{:S(2)}, u32[]{:S(2)}) collective-permute-start(bf16[1,1664,128]{2,1,0:T(8,128)(2,1)} %add_convert_fusion.7), channel_id=1, source_target_pairs={{0,16},{4,20},{8,24},{12,28},{16,0},{20,4},{24,8},{28,12},{1,17},{... | collective-permute-start | bytes 1277960 | tf_op jit(solution)/shard_map/ppermute | solution.py:268
  170.0 24.4 %collective-permute-start.24 = (bf16[1,1664,128]{2,1,0:T(8,128)(2,1)}, bf16[1,1664,128]{2,1,0:T(8,128)(2,1)}, u32[]{:S(2)}, u32[]{:S(2)}) collective-permute-start(bf16[1,1664,128]{2,1,0:T(8,128)(2,1)} %add_convert_fusion.6), channel_id=1, source_target_pairs={{0,8},{4,12},{8,0},{12,4},{16,24},{20,28},{24,16},{28,20},{1,9},{5... | collective-permute-start | bytes 1277960 | tf_op jit(solution)/shard_map/ppermute | solution.py:268
  173.8 23.8 %collective-permute-start.23 = (bf16[1,1664,128]{2,1,0:T(8,128)(2,1)}, bf16[1,1664,128]{2,1,0:T(8,128)(2,1)}, u32[]{:S(2)}, u32[]{:S(2)}) collective-permute-start(bf16[1,1664,128]{2,1,0:T(8,128)(2,1)} %add_convert_fusion.5), channel_id=1, source_target_pairs={{0,16},{4,20},{8,24},{12,28},{16,0},{20,4},{24,8},{28,12},{1,17},{... | collective-permute-start | bytes 1277960 | tf_op jit(solution)/shard_map/ppermute | solution.py:268
  175.0 16.1 %copy-start.6 = (bf16[2,1664,128]{2,1,0:T(8,128)(2,1)}, bf16[2,1664,128]{2,1,0:T(8,128)(2,1)S(1)}, u32[]{:S(2)}) copy-start(bf16[2,1664,128]{2,1,0:T(8,128)(2,1)S(1)} %collective-permute-done.18.refs_4_) | copy-start | bytes 2555908
  177.5 23.3 %collective-permute-start.22 = (bf16[1,1664,128]{2,1,0:T(8,128)(2,1)}, bf16[1,1664,128]{2,1,0:T(8,128)(2,1)}, u32[]{:S(2)}, u32[]{:S(2)}) collective-permute-start(bf16[1,1664,128]{2,1,0:T(8,128)(2,1)} %add_convert_fusion.4.refs_10_), channel_id=1, source_target_pairs={{0,8},{4,12},{8,0},{12,4},{16,24},{20,28},{24,16},{28,20},{1,9},{5... | collective-permute-start | bytes 1277960 | tf_op jit(solution)/shard_map/ppermute | solution.py:268
